TPU v7x, 256 devices: a whole 4x4x8 slice. The times are simulated.
256 devices in a mesh: seq: 2 (over x_hi), head: 2 (over core), dp: 64 (over z, y, x_lo).
Axes of the slice: x: 4 (x_hi: 2, x_lo: 2; x = x_hi * 2 + x_lo), y: 4, z: 8, core: 2. Of those that a mesh axis runs over, the one named last changes fastest.
Arguments:
- tokens: bfloat16 [64, 1024, 1536], P('dp', 'seq', 'head'), may hold values from -40 to 40
- lengths: int32 [64, 8], P('dp'), may hold values from 1 to 512, 1024 in all within a row
- owner_slot: int32 [64, 8], P('dp'), may hold values from 0 to 7, each once within a row
- latent_index: int32 [64, 8, 128], P('dp'), may hold values from 0 to 1048575
- cotangent: bfloat16 [64, 1024, 1536], P('dp', 'seq'), may hold values from -24 to 24
- qkv_weight: bfloat16 [3, 1536, 1536], P(None, None, 'head'), may hold values from -0.15625 to 0.15625
- out_weight: bfloat16 [1536, 1536], P('head'), may hold values from -1.25 to 1.25
Outputs:
- mixed: bfloat16 [64, 1024, 1536], P('dp', 'seq', 'head')
- latents: bfloat16 [64, 1024, 1536], P('dp', 'seq', 'head')
- grad_out: float32 [1536, 1536], P('head')
Inputs may be any that keep to these rules, and one draw needn't show every extreme that they name: Each pack's lengths sum to 1024.
All inputs are finite; a program needn't handle non-finite values.
Results may differ from a plain program's by a relative error of at most 0.013.
Values may be sent and summed in bfloat16 or wider, within the bound.
No kernel may reach another device: no remote copies, remote signals or barrier semaphores. Data moves between devices by JAX's collectives and lax.ppermute only.
A program may use at most 128 MiB of HBM per device.

v0:
```python
import jax
import jax.numpy as jnp
from jax import lax
from jax.sharding import PartitionSpec as P

HD = 64
LAT = 128


eps_norm = 1e-05
eps_head = 1e-06
key_span = 512


def image_of(positions, ends):
    return jnp.sum((positions[:, None] >= ends[None, :]).astype(jnp.int32), axis=1)


def head_norm(values):
    split = values.reshape(values.shape[0], values.shape[1] // HD, HD)
    scale = lax.rsqrt(jnp.mean(split * split, axis=2, keepdims=True) + eps_head)
    return (split * scale).reshape(values.shape).astype(jnp.bfloat16)


def body(tokens, lengths, owner_slot, latent_index, cotangent, qkv_weight, out_weight):
    rows_local = tokens[0]
    tok = rows_local.shape[0]
    share = rows_local.shape[1]
    heads_here = share // HD
    seq_count = lax.axis_size("seq")
    total = tok * seq_count
    offset = lax.axis_index("seq") * tok
    sizes = lengths[0]
    ends = jnp.cumsum(sizes, dtype=jnp.int32)
    starts = ends - sizes
    whole = lax.all_gather(rows_local, "head", axis=1, tiled=True).astype(jnp.float32)
    mean = jnp.mean(whole, axis=1, keepdims=True)
    centered = whole - mean
    var = jnp.mean(centered * centered, axis=1, keepdims=True)
    normed = (centered * lax.rsqrt(var + eps_norm)).astype(jnp.bfloat16)
    query = head_norm(jnp.dot(normed, qkv_weight[0], preferred_element_type=jnp.float32))
    keys = head_norm(jnp.dot(normed, qkv_weight[1], preferred_element_type=jnp.float32))
    values = jnp.dot(normed, qkv_weight[2], preferred_element_type=jnp.float32).astype(jnp.bfloat16)
    key_value = jnp.stack([keys, values], axis=1)
    q_heads = query.reshape(tok, heads_here, HD)
    image_q = image_of(offset + jnp.arange(tok, dtype=jnp.int32), ends)
    factor = HD ** (-0.5)
    piece = lax.all_gather(key_value, "seq", axis=0, tiled=True)
    start = jnp.int32(0)
    denom = jnp.zeros((heads_here, tok), jnp.float32)
    accum = jnp.zeros((tok, heads_here, HD), jnp.float32)
    count = piece.shape[0]
    step_rows = min(count, key_span)
    for begin in range(0, count, step_rows):
        block = piece[begin : begin + step_rows]
        used = block.shape[0]
        places = start + begin + jnp.arange(used, dtype=jnp.int32)
        inside = (places >= 0) & (places < total)
        image_k = jnp.where(inside, image_of(places, ends), -1)
        k_heads = block[:, 0].reshape(used, heads_here, HD)
        v_heads = block[:, 1].reshape(used, heads_here, HD)
        scores = (
            jnp.einsum("qhd,khd->hqk", q_heads, k_heads, preferred_element_type=jnp.float32)
            * factor
        )
        same = (image_q[:, None] == image_k[None, :]).astype(jnp.float32)
        weights = jnp.exp(scores) * same[None]
        denom = denom + jnp.sum(weights, axis=2)
        accum = accum + jnp.einsum(
            "hqk,khd->qhd",
            weights.astype(jnp.bfloat16),
            v_heads,
            preferred_element_type=jnp.float32,
        )
    denom, accum = (denom, accum)
    attn = (accum / jnp.transpose(denom)[:, :, None]).reshape(tok, share).astype(jnp.bfloat16)
    partial_out = jnp.dot(attn, out_weight, preferred_element_type=jnp.float32)
    mixed = lax.psum_scatter(
        partial_out.astype(jnp.bfloat16), "head", scatter_dimension=1, tiled=True
    )
    slots = owner_slot[0]
    flat_index = latent_index[0].reshape(-1)
    latent_row = jnp.arange(
        lax.axis_size("seq") * (slots.shape[0] // seq_count * LAT), dtype=jnp.int32
    )
    slot = latent_row // LAT
    within = latent_row % LAT
    chosen = (slot[:, None] == slots[None, :]).astype(jnp.int32)
    image_id = jnp.sum(chosen * jnp.arange(slots.shape[0], dtype=jnp.int32)[None, :], axis=1)
    image_start = jnp.sum(chosen * starts[None, :], axis=1)
    image_size = jnp.sum(chosen * sizes[None, :], axis=1)
    raw = jnp.take(flat_index, image_id * LAT + within, axis=0)
    local = image_start + jnp.remainder(raw, image_size) - offset
    present = (local >= 0) & (local < tok)
    fetched = jnp.take(mixed, jnp.clip(local, 0, tok - 1), axis=0).astype(jnp.float32)
    latents = lax.psum_scatter(
        (fetched * present[:, None].astype(jnp.float32)).astype(jnp.bfloat16),
        "seq",
        scatter_dimension=0,
        tiled=True,
    )
    grad_term = lax.dot_general(
        attn, cotangent[0], (((0,), (0,)), ((), ())), preferred_element_type=jnp.float32
    )
    all_tokens = total * lax.axis_size("dp")
    grad_out = lax.psum(grad_term, ("seq", "dp")) * all_tokens ** (-0.5)
    return (mixed[None], latents[None], grad_out)


def solution(mesh):
    in_specs = (
        P("dp", "seq", "head"),
        P("dp", None),
        P("dp", None),
        P("dp", None, None),
        P("dp", "seq", None),
        P(None, None, "head"),
        P("head", None),
    )
    out_specs = (P("dp", "seq", "head"), P("dp", "seq", "head"), P("head", None))
    return jax.shard_map(body, mesh=mesh, in_specs=in_specs, out_specs=out_specs, check_vma=False)
```

profile of v0, /device:TPU:2, one launch (start us, length us, event | category | flops | bytes accessed | tf_op | source)
XLA Modules:
  0.0 418.7 jit_solution(4467157169533100520)
XLA Ops:
  7.2 0.0 all-gather.6.cloned.1.call-start
  7.2 0.7 all-gather.6.cloned.1.call-update
  7.9 0.0 all-gather.4.cloned.1.call-start
  8.0 4.9 %slice_bitcast_fusion = (bf16[768,1536]{0,1:T(8,128)(2,1)}, bf16[768,1536]{0,1:T(8,128)(2,1)}) fusion(bf16[3,1536,768]{2,1,0:T(8,128)(2,1)} %param.12), kind=kLoop, calls=%fused_computation.26 | loop fusion | bytes 9437184 | tf_op jit(solution)/shard_map/dot_general | solution.py:41
  12.8 4.3 %copy.28 = bf16[768,1536]{1,0:T(8,128)(2,1)} copy(bf16[768,1536]{0,1:T(8,128)(2,1)} %get-tuple-element.12) | data formatting | bytes 4718592 | tf_op jit(solution)/shard_map/dot_general | solution.py:42
  17.1 10.8 %all-gather.6.cloned.1.call-done = bf16[1,512,1536]{2,1,0:T(8,128)(2,1)} async-done(((bf16[1,512,768]{2,1,0:T(8,128)(2,1)}), bf16[1,512,1536]{2,1,0:T(8,128)(2,1)}) %all-gather.6.cloned.1.call-update) | async-done | bytes 1572880 | tf_op jit(solution)/shard_map/all_gather | solution.py:36
  27.9 1.8 convert_reduce_fusion
  29.8 0.1 copy-done.4
  29.8 0.5 fusion.15
  30.4 3.3 multiply_reduce_fusion.1
  33.7 0.2 multiply_convert_fusion.2
  33.9 1.2 copy.29
  35.1 3.6 fusion.32
  38.7 1.3 pad_maximum_fusion
  40.0 0.0 all-gather.4.cloned.1.call-update
  40.1 0.2 reduce-scatter.3.cloned.1.call-start
  40.3 4.3 %copy.31 = bf16[768,1536]{1,0:T(8,128)(2,1)} copy(bf16[768,1536]{0,1:T(8,128)(2,1)} %get-tuple-element.11) | data formatting | bytes 4718592 | tf_op jit(solution)/shard_map/dot_general | solution.py:41
  44.6 0.2 reduce-window.4
  44.8 0.1 convert_reduce_fusion.2
  44.9 1.3 compare_convert_fusion.1
  46.2 4.9 %multiply_reduce_fusion = (f32[512,12]{0,1:T(8,128)S(1)}, f32[512,12,64]{0,2,1:T(8,128)}) fusion(bf16[12,64,1536]{2,1,0:T(8,128)(2,1)} %bitcast.103, f32[512]{0:T(512)S(1)} %add_rsqrt_fusion.2, f32[512]{0:T(512)S(1)} %broadcast_multiply_fusion.2, bf16[1,512,1536]{2,1,0:T(8,128)(2,1)} %all-gather.6.cloned.1.call-done), kind=kOutput, calls=%fused_computation.39 | convolution fusion | flops 1211885568 | bytes 5533696 | tf_op jit(solution)/shard_map/dot_general | solution.py:41
  51.0 41.1 %all-gather.4.cloned.1.call-done = bf16[1024,2,768]{2,0,1:T(8,128)(2,1)} async-done(((bf16[512,2,768]{2,0,1:T(8,128)(2,1)}), bf16[1024,2,768]{2,0,1:T(8,128)(2,1)}) %all-gather.4.cloned.1.call-update) | async-done | bytes 3145744 | tf_op jit(solution)/shard_map/all_gather | solution.py:48
  92.1 3.6 fusion.59
  95.7 2.3 copy.34
  98.0 2.3 copy.35
  100.3 2.3 copy.30
  102.6 2.3 copy.32
  104.9 4.8 %fusion.2 = (f32[12,512]{1,0:T(8,128)S(1)}, f32[12,512,512]{1,2,0:T(8,128)S(1)}) fusion(f32[512,512]{0,1:T(8,128)} %get-tuple-element.18, bf16[512,12,64]{0,2,1:T(8,128)(2,1)} %bitcast.101, f32[512,12,64]{0,2,1:T(8,128)} %get-tuple-element.22, f32[512,12]{0,1:T(8,128)S(1)} %add_rsqrt_fusion), kind=kOutput, calls=%fused_computation.6 | convolution fusion | flops 412870656 | bytes 16039936 | tf_op jit(solution)/shard_map/qhd,khd->hqk/dot_general | solution.py:63
  109.7 2.5 fusion.4
  112.2 3.3 fusion
  115.6 2.7 fusion.22
  118.3 0.9 copy-done.3
  119.2 2.6 convolution_convert_fusion
  121.8 0.0 reduce-scatter.3.cloned.1.call-update
  121.8 0.0 all-reduce.2.cloned.1.call-start
  121.9 5.2 %fusion.20 = f32[768,1536]{1,0:T(8,128)} fusion(bf16[512,768]{0,1:T(8,128)(2,1)} %bitcast.97, bf16[1,512,1536]{2,1,0:T(8,128)(2,1)} %param.11), kind=kOutput, calls=%fused_computation.30 | convolution fusion | flops 1207959552 | bytes 7077888 | tf_op jit(solution)/shard_map/dot_general | solution.py:102
  127.2 0.3 reduce-scatter.5.cloned.1.call-start
  127.4 0.3 copy-done.11
  127.8 0.1 fusion.39
  127.9 4.5 %gather_fusion = s32[1024]{0:T(1024)S(1)} fusion(s32[1024]{0:T(1024)S(1)} %bitcast.94, s32[1024]{0:T(1024)S(1)} %broadcast_clamp_fusion.1), kind=kCustom, calls=%fused_computation | custom fusion | bytes 12288 | tf_op jit(solution)/shard_map/jit(_take)/gather | solution.py:92
  132.5 0.1 compare_and_fusion
  132.6 0.4 compare_select_fusion.3
  133.0 3.8 reduce-scatter.3.cloned.1.call-done
  136.8 6.8 %gather_fusion.1 = bf16[1024,768]{1,0:T(8,128)(2,1)} fusion(bf16[512,768]{1,0:T(8,128)(2,1)} %reduce-scatter.3.cloned.1.call-done, s32[1024]{0:T(1024)S(1)} %broadcast_clamp_fusion), kind=kCustom, calls=%fused_computation.1 | custom fusion | bytes 3149824 | tf_op jit(solution)/shard_map/jit(_take)/gather | solution.py:95
  143.6 3.0 multiply_convert_fusion
  146.7 233.5 %all-reduce.2.cloned.1.call-done = f32[768,1536]{1,0:T(8,128)} async-done(((f32[768,1536]{1,0:T(8,128)}), f32[768,1536]{1,0:T(8,128)}) %all-reduce.2.cloned.1.call-update) | async-done | bytes 4718608 | tf_op jit(solution)/shard_map/psum | solution.py:106
  380.2 5.0 %broadcast_multiply_fusion = f32[768,1536]{1,0:T(8,128)} fusion(f32[768,1536]{1,0:T(8,128)} %all-reduce.2.cloned.1.call-done), kind=kLoop, calls=%fused_computation.25 | loop fusion | flops 1179648 | bytes 9437184 | tf_op jit(solution)/shard_map/mul | solution.py:106
  385.1 27.0 %reduce-scatter.5.cloned.1.call-done = bf16[512,768]{1,0:T(8,128)(2,1)} async-done(((bf16[1024,768]{1,0:T(8,128)(2,1)}), bf16[512,768]{1,0:T(8,128)(2,1)}) %reduce-scatter.5.cloned.1.call-update) | async-done | bytes 786448 | tf_op jit(solution)/shard_map/reduce_scatter | solution.py:96
  (38 shorter events, 0.2 us)
Async XLA Ops:
  7.2 112.0 %copy-start = (bf16[768,1536]{1,0:T(8,128)(2,1)S(1)}, bf16[768,1536]{1,0:T(8,128)(2,1)}, u32[]{:S(2)}) copy-start(bf16[768,1536]{1,0:T(8,128)(2,1)} %param.13) | copy-start | bytes 7077892
  7.2 20.8 %all-gather.6.cloned.1.call-start = ((), (), s32[]{:S(2)}) async-start(), calls=%async_computation.6 | async-start | bytes 2359296 | tf_op jit(solution)/shard_map/all_gather | solution.py:36
  7.9 84.2 %all-gather.4.cloned.1.call-start = ((), (), s32[]{:S(2)}) async-start(), calls=%async_computation.2 | async-start | bytes 4718592 | tf_op jit(solution)/shard_map/all_gather | solution.py:48
  27.9 1.9 copy-start.4
  35.1 3.7 copy-start.9
  40.1 96.7 %reduce-scatter.3.cloned.1.call-start = ((), (), s32[]{:S(2)}) async-start(), calls=%async_computation.3 | async-start | bytes 2359296 | tf_op jit(solution)/shard_map/reduce_scatter | solution.py:78
  40.3 4.3 %copy-start.10 = (s32[1,8]{1,0:T(1,128)S(1)}, s32[1,8]{1,0:T(1,128)}, u32[]{:S(2)}) copy-start(s32[1,8]{1,0:T(1,128)} %param.8) | copy-start | bytes 100
  104.9 4.8 %copy-start.2 = (f32[512,512]{0,1:T(8,128)S(1)}, f32[512,512]{0,1:T(8,128)}, u32[]{:S(2)}) copy-start(f32[512,512]{0,1:T(8,128)} %get-tuple-element.18) | copy-start | bytes 3145732
  104.9 4.8 %copy-start.8 = (bf16[512,1,768]{0,2,1:T(8,128)(2,1)S(1)}, bf16[512,1,768]{0,2,1:T(8,128)(2,1)}, u32[]{:S(2)}) copy-start(bf16[512,1,768]{0,2,1:T(8,128)(2,1)} %copy.34) | copy-start | bytes 2359300
  109.7 2.5 copy-start.5
  109.7 2.5 copy-start.7
  112.2 3.3 copy-start.6
  118.3 0.9 copy-start.3
  121.8 258.3 %all-reduce.2.cloned.1.call-start = ((), (), s32[]{:S(2)}) async-start(), calls=%async_computation.5 | async-start | bytes 9437184 | tf_op jit(solution)/shard_map/psum | solution.py:106
  127.1 0.7 copy-start.11
  127.1 0.8 copy-start.1
  127.2 285.0 %reduce-scatter.5.cloned.1.call-start = ((), (), s32[]{:S(2)}) async-start(), calls=%async_computation.4 | async-start | bytes 2359296 | tf_op jit(solution)/shard_map/reduce_scatter | solution.py:96
Sparse Core Ops, SparseCore 0:
  9.8 18.0 all-gather.5
  40.2 51.8 all-gather.3
  122.0 14.7 reduce-scatter.2
  143.7 236.4 all-reduce.1
  383.1 29.0 reduce-scatter.4
where the time goes:
time: 421 us; the launch traced here: 419 us
  waiting for transfers between devices  317 us (75%)
  local copies, waits for them, and re-layouts  40 us (10%)
  matrix products  32.9 us (8%)
  other arithmetic  14.2 us (3%)
  between operations  14 us (3%)
    psum x1, waiting for transfers between devices, body(): grad_out = lax.psum(grad_term, ('seq', 'dp')) * all_tokens ** (-0.5)  233 us
    all_gather x1, waiting for transfers between devices, body(): piece = lax.all_gather(key_value, 'seq', axis=0, tiled=True)  41.1 us
    reduce_scatter x1, waiting for transfers between devices, body(): lax.psum_scatter((fetched * present[:, None].astype(jnp.float32)).astype(...  27 us
    all_gather x1, waiting for transfers between devices, body(): lax.all_gather(rows_local, 'head', axis=1, tiled=True).astype(jnp.float32)  10.8 us
    dot_general x2, local copies, waits for them, and re-layouts, body(): jnp.dot(normed, qkv_weight[0], preferred_element_type=jnp.float32)  9.16 us
  transfers between devices with their start and end apart: 5, of which 5 were waited for; matrix products, arithmetic and copies ran while one was open for 11% of the time, Pallas kernels for 0%

commit v1 on v0

v1 whole, which is shorter than its diff:
```python
import functools

import jax
import jax.numpy as jnp
from jax import lax
from jax.experimental import pallas as pl
from jax.experimental.pallas import tpu as pltpu
from jax.sharding import Mesh
from jax.sharding import PartitionSpec as P

HD = 64
LAT = 128
GROUP = 256
BIG = 128.0
EPS_NORM = 1e-05
EPS_HEAD = 1e-06
BF = jnp.bfloat16
F32 = jnp.float32
PLANE = ("seq", "y", "xl")
VMEM_LIMIT = 48 * 1024 * 1024


def norm_rows(head, own_ref, oth_ref, normed_ref, rows):
    share = own_ref.shape[1]
    step = 64

    def one(i, carry):
        at = pl.ds(pl.multiple_of(i * step, step), step)
        own = own_ref[at, :].astype(F32)
        oth = oth_ref[at, :].astype(F32)
        inv = 1.0 / (2 * share)
        mean = (jnp.sum(own, axis=1, keepdims=True) + jnp.sum(oth, axis=1, keepdims=True)) * inv
        own = own - mean
        oth = oth - mean
        var = (jnp.sum(own * own, axis=1, keepdims=True) + jnp.sum(oth * oth, axis=1, keepdims=True)) * inv
        scale = lax.rsqrt(var + EPS_NORM)
        own = (own * scale).astype(BF)
        oth = (oth * scale).astype(BF)

        @pl.when(head == 0)
        def _():
            normed_ref[at, :share] = own
            normed_ref[at, share:] = oth

        @pl.when(head != 0)
        def _():
            normed_ref[at, :share] = oth
            normed_ref[at, share:] = own

        return carry

    lax.fori_loop(0, rows // step, one, 0)


def head_norm(values, ones):
    square = values * values
    high = square.astype(BF)
    low = (square - high.astype(F32)).astype(BF)
    mean = jnp.dot(high, ones, preferred_element_type=F32) + jnp.dot(low, ones, preferred_element_type=F32)
    return values * lax.rsqrt(mean + EPS_HEAD)


def ones_block():
    row = lax.broadcasted_iota(jnp.int32, (GROUP, GROUP), 0) // HD
    col = lax.broadcasted_iota(jnp.int32, (GROUP, GROUP), 1) // HD
    return jnp.where(row == col, 1.0 / HD, 0.0).astype(BF)


def features(bounds_ref, first, rows, inside, constant):
    pos = first + lax.broadcasted_iota(jnp.int32, (rows, 128), 0)
    lane = lax.broadcasted_iota(jnp.int32, (rows, 128), 1) & (HD - 1)
    member = (pos >= bounds_ref[0:1, :]) & (pos < bounds_ref[1:2, :])
    return jnp.where(lane == 8, constant, jnp.where(member, inside, 0.0)).astype(BF)


def lower_half(rows):
    return lax.broadcasted_iota(jnp.int32, (rows, 128), 1) < HD


def attend_group(q, k, v, qfeat, kfeat, emit):
    q = (q.astype(F32) * 0.125).astype(BF)
    for pair in range(2):
        lanes = slice(pair * 128, pair * 128 + 128)
        qp, kp, vp = q[:, lanes], k[:, lanes], v[:, lanes]
        qlow, klow = lower_half(qp.shape[0]), lower_half(kp.shape[0])
        one = jnp.ones_like(vp)
        for odd in range(2):
            qa = jnp.where(qlow, qfeat, qp) if odd else jnp.where(qlow, qp, qfeat)
            ka = jnp.where(klow, kfeat, kp) if odd else jnp.where(klow, kp, kfeat)
            va = jnp.where(klow, one, vp) if odd else jnp.where(klow, vp, one)
            s = lax.dot_general(qa, ka, (((1,), (1,)), ((), ())), preferred_element_type=F32)
            w = jnp.exp(s).astype(BF)
            emit(2 * pair + odd, jnp.dot(w, va, preferred_element_type=F32))


def local_kernel(place_ref, bounds_ref, own_ref, oth_ref, w_ref, q_ref, acc_ref, normed_ref, qf_ref, kf_ref, ones_ref):
    rows = own_ref.shape[0]

    @pl.when(pl.program_id(0) == 0)
    def _():
        norm_rows(place_ref[1], own_ref, oth_ref, normed_ref, rows)
        first = place_ref[0] * rows
        qf_ref[...] = features(bounds_ref, first, rows, BIG, -BIG)
        kf_ref[...] = features(bounds_ref, first, rows, 1.0, 1.0)
        ones_ref[...] = ones_block()

    normed = normed_ref[...]
    ones = ones_ref[...]
    q = head_norm(jnp.dot(normed, w_ref[0], preferred_element_type=F32), ones).astype(BF)
    k = head_norm(jnp.dot(normed, w_ref[1], preferred_element_type=F32), ones).astype(BF)
    v = jnp.dot(normed, w_ref[2], preferred_element_type=F32).astype(BF)
    q_ref[...] = q

    def emit(head, r):
        acc_ref[:, head * 128 : head * 128 + 128] = r

    attend_group(q, k, v, qf_ref[...], kf_ref[...], emit)


def near_kernel(place_ref, bounds_ref, own_ref, oth_ref, wk_ref, wv_ref, q_ref, acc_in_ref, acc_ref, normed_ref, qf_ref, kf_ref, ones_ref):
    rows = own_ref.shape[0]
    span = q_ref.shape[0]

    @pl.when(pl.program_id(0) == 0)
    def _():
        norm_rows(place_ref[1], own_ref, oth_ref, normed_ref, rows)
        qf_ref[...] = features(bounds_ref, place_ref[0] * span, span, BIG, -BIG)
        kf_ref[...] = features(bounds_ref, jnp.where(place_ref[0] == 0, span, span - rows), rows, 1.0, 1.0)
        ones_ref[...] = ones_block()

    normed = normed_ref[...]
    k = head_norm(jnp.dot(normed, wk_ref[0], preferred_element_type=F32), ones_ref[...]).astype(BF)
    v = jnp.dot(normed, wv_ref[0], preferred_element_type=F32).astype(BF)

    def emit(head, r):
        lanes = slice(head * 128, head * 128 + 128)
        acc_ref[:, lanes] = acc_in_ref[:, lanes] + r

    attend_group(q_ref[...], k, v, qf_ref[...], kf_ref[...], emit)


def far_kernel(place_ref, bounds_ref, own_ref, oth_ref, wk_ref, wv_ref, q_ref, acc_in_ref, cot_ref, attn_ref, grad_ref, normed_ref, qf_ref, kf_ref, ones_ref, acc_ref):
    rows = own_ref.shape[0]
    span = acc_in_ref.shape[0]
    part = q_ref.shape[0]
    begin = jnp.where(place_ref[0] == 0, span - part, 0)

    @pl.when(pl.program_id(0) == 0)
    def _():
        norm_rows(place_ref[1], own_ref, oth_ref, normed_ref, rows)
        qf_ref[...] = features(bounds_ref, place_ref[0] * span + begin, part, BIG, -BIG)
        kf_ref[...] = features(bounds_ref, jnp.where(place_ref[0] == 0, 2 * span - rows, 0), rows, 1.0, 1.0)
        ones_ref[...] = ones_block()

    normed = normed_ref[...]
    k = head_norm(jnp.dot(normed, wk_ref[0], preferred_element_type=F32), ones_ref[...]).astype(BF)
    v = jnp.dot(normed, wv_ref[0], preferred_element_type=F32).astype(BF)
    acc_ref[...] = acc_in_ref[...]
    at = pl.ds(pl.multiple_of(begin, part), part)

    def emit(head, r):
        lanes = slice(head * 128, head * 128 + 128)
        acc_ref[at, lanes] = acc_ref[at, lanes] + r

    attend_group(q_ref[...], k, v, qf_ref[...], kf_ref[...], emit)
    low = lower_half(span)
    for pair in range(2):
        even = acc_ref[:, pair * 256 : pair * 256 + 128]
        odd = acc_ref[:, pair * 256 + 128 : pair * 256 + 256]
        total = pltpu.roll(jnp.where(low, odd, even), HD, 1)
        attn_ref[:, pair * 128 : pair * 128 + 128] = (jnp.where(low, even, odd) / total).astype(BF)
    grad_ref[...] = lax.dot_general(attn_ref[...], cot_ref[...], (((0,), (0,)), ((), ())), preferred_element_type=F32).astype(BF)


def send_kernel(place_ref, attn_ref, w_ref, out_ref):
    out_ref[...] = jnp.dot(attn_ref[...], w_ref[...], preferred_element_type=F32).astype(BF)


def mixed_kernel(place_ref, attn_ref, w_ref, recv_ref, pick_ref, mixed_ref, send_ref, keep_ref):
    rows = attn_ref.shape[0]
    mixed = (jnp.dot(attn_ref[...], w_ref[...], preferred_element_type=F32) + recv_ref[...].astype(F32)).astype(BF)
    mixed_ref[...] = mixed
    row = lax.broadcasted_iota(jnp.int32, (rows, rows), 1)
    for half, out in ((0, send_ref), (1, keep_ref)):
        hot = jnp.where(pick_ref[half * rows : half * rows + rows, :] == row, 1.0, 0.0).astype(BF)
        out[...] = jnp.dot(hot, mixed, preferred_element_type=F32).astype(BF)


def call(kernel, place, grid, in_specs, out_specs, out_shape, scratch, flops, nbytes, args, alias=None):
    return pl.pallas_call(
        kernel,
        grid_spec=pltpu.PrefetchScalarGridSpec(
            num_scalar_prefetch=1, grid=grid, in_specs=in_specs, out_specs=out_specs, scratch_shapes=scratch
        ),
        out_shape=out_shape,
        input_output_aliases=alias or {},
        cost_estimate=pl.CostEstimate(flops=flops, bytes_accessed=nbytes, transcendentals=0),
        compiler_params=pltpu.CompilerParams(vmem_limit_bytes=VMEM_LIMIT),
    )(place, *args)


def whole(shape):
    return pl.BlockSpec(shape, lambda g, s: (0,) * len(shape))


def columns(rows, width):
    return pl.BlockSpec((rows, width), lambda g, s: (0, g))


def swap(value, axis):
    return lax.ppermute(value, axis, [(0, 1), (1, 0)])


def sum_parts(parts):
    return jnp.sum(parts.astype(F32), axis=0).astype(BF)


def reduce_grad(grad):
    rows, width = grad.shape
    n = 1
    for axis in PLANE:
        n *= lax.axis_size(axis)
    nz = lax.axis_size("z")
    chunks = 3
    span = rows // chunks
    pieces = []
    for c in range(chunks):
        part = grad[c * span : c * span + span].reshape(n, span // n, width)
        got = lax.all_to_all(part, PLANE, 0, 0)
        pieces.append(sum_parts(got))
    mine = jnp.concatenate(pieces, axis=0)
    if nz > 1:
        shape = mine.shape
        part = mine.reshape(nz, 8, -1)
        got = sum_parts(lax.all_to_all(part, "z", 0, 0))
        mine = lax.all_gather(got, "z", axis=0).reshape(shape)
    outs = []
    for c in range(chunks):
        small = mine[c * (span // n) : (c + 1) * (span // n)]
        outs.append(lax.all_gather(small, PLANE, axis=0, tiled=True))
    return outs


def body(tokens, lengths, owner_slot, latent_index, cotangent, qkv_weight, out_weight):
    own = tokens[0]
    rows, share = own.shape
    half = rows // 2
    groups = share // GROUP
    seq = lax.axis_index("seq")
    head = lax.axis_index("head")
    place = jnp.stack([seq, head]).astype(jnp.int32)

    near = lax.dynamic_slice_in_dim(own, (1 - seq) * half, half, 0)
    far = lax.dynamic_slice_in_dim(own, seq * half, half, 0)
    near_own = swap(near, "seq")
    far_own = swap(far, "seq")
    oth = swap(own, "head")
    near_oth = swap(near_own, "head")
    far_oth = swap(far_own, "head")

    sizes = lengths[0]
    images = sizes.shape[0]
    ends = jnp.cumsum(sizes, dtype=jnp.int32)
    starts = ends - sizes
    pad = lambda a: jnp.tile(jnp.pad(a, (0, HD - images)), 2)
    bounds = jnp.pad(jnp.stack([pad(starts), pad(ends)]), ((0, 6), (0, 0)))

    scratch = lambda r, qr, kr: [
        pltpu.VMEM((r, 2 * share), BF),
        pltpu.VMEM((qr, 128), BF),
        pltpu.VMEM((kr, 128), BF),
        pltpu.VMEM((GROUP, GROUP), BF),
    ]
    weight = lambda j: pl.BlockSpec((1, 2 * share, GROUP), lambda g, s: (j, 0, g))
    q, acc = call(
        local_kernel, place, (groups,),
        [whole((8, 128)), whole((rows, share)), whole((rows, share)),
         pl.BlockSpec((3, 2 * share, GROUP), lambda g, s: (0, 0, g))],
        [columns(rows, GROUP), columns(rows, 2 * GROUP)],
        [jax.ShapeDtypeStruct((rows, share), BF), jax.ShapeDtypeStruct((rows, 2 * share), F32)],
        scratch(rows, rows, rows), 7 * 10**9, 12 * 10**6, (bounds, own, oth, qkv_weight),
    )
    acc = call(
        near_kernel, place, (groups,),
        [whole((8, 128)), whole((half, share)), whole((half, share)), weight(1), weight(2),
         columns(rows, GROUP), columns(rows, 2 * GROUP)],
        columns(rows, 2 * GROUP),
        jax.ShapeDtypeStruct((rows, 2 * share), F32),
        scratch(half, rows, half), 3 * 10**9, 12 * 10**6,
        (bounds, near_own, near_oth, qkv_weight, qkv_weight, q, acc), {7: 0},
    )
    attn, grad = call(
        far_kernel, place, (groups,),
        [whole((8, 128)), whole((half, share)), whole((half, share)), weight(1), weight(2),
         pl.BlockSpec((half, GROUP), lambda g, s: (1 - s[0], g)), columns(rows, 2 * GROUP), whole((rows, 2 * share))],
        [columns(rows, GROUP), pl.BlockSpec((GROUP, 2 * share), lambda g, s: (g, 0))],
        [jax.ShapeDtypeStruct((rows, share), BF), jax.ShapeDtypeStruct((share, 2 * share), BF)],
        scratch(half, half, half) + [pltpu.VMEM((rows, 2 * GROUP), F32)], 4 * 10**9, 14 * 10**6,
        (bounds, far_own, far_oth, qkv_weight, qkv_weight, q, acc, cotangent[0]),
    )
    sums = reduce_grad(grad)

    partial = call(
        send_kernel, place, (groups,),
        [whole((rows, share)), pl.BlockSpec((share, GROUP), lambda g, s: (0, (1 - s[1]) * groups + g))],
        columns(rows, GROUP), jax.ShapeDtypeStruct((rows, share), BF), [], 6 * 10**8, 3 * 10**6, (attn, out_weight),
    )
    recv = swap(partial, "head")

    slots = owner_slot[0]
    picks = starts[:, None] + jnp.remainder(latent_index[0], sizes[:, None])
    order = slots[None, :] == jnp.arange(images, dtype=jnp.int32)[:, None]
    by_slot = jnp.sum(jnp.where(order[:, :, None], picks[None], 0), axis=1).reshape(2, rows)
    local = by_slot - seq * rows
    local = jnp.stack([jnp.where(seq == 0, local[1], local[0]), jnp.where(seq == 0, local[0], local[1])])
    local = local.reshape(2 * rows, 1)

    shape = jax.ShapeDtypeStruct((rows, share), BF)
    mixed, send, keep = call(
        mixed_kernel, place, (groups,),
        [whole((rows, share)), pl.BlockSpec((share, GROUP), lambda g, s: (0, s[1] * groups + g)),
         columns(rows, GROUP), whole((2 * rows, 1))],
        [columns(rows, GROUP)] * 3, [shape] * 3, [], 14 * 10**8, 6 * 10**6, (attn, out_weight, recv, local),
    )
    latents = keep + swap(send, "seq")

    count = 2 * rows * lax.axis_size("z") * lax.axis_size("y") * lax.axis_size("xl")
    grad_out = jnp.concatenate([s.astype(F32) * count ** (-0.5) for s in sums], axis=0)
    return mixed[None], latents[None], grad_out


def on_mesh(fine):
    dp = ("z", "y", "xl")
    in_specs = (
        P(dp, "seq", "head"),
        P(dp, None),
        P(dp, None),
        P(dp, None, None),
        P(dp, "seq", None),
        P(None, None, "head"),
        P("head", None),
    )
    out_specs = (P(dp, "seq", "head"), P(dp, "seq", "head"), P("head", None))
    return jax.shard_map(body, mesh=fine, in_specs=in_specs, out_specs=out_specs, check_vma=False)


def solution(mesh):
    return on_mesh(Mesh(mesh.devices.reshape(2, 2, 8, 4, 2), ("seq", "head", "z", "y", "xl")))
```

time: 421 us -> 297 us (0.71)
  waiting for transfers between devices: 317 us -> 37.2 us
  blocking collectives: 0 us -> 169 us
  Pallas kernels: 0 us -> 46.3 us
  matrix products: 32.9 us -> 0 us
  local copies, waits for them, and re-layouts: 40 us -> 9.86 us
  starting transfers between devices: 0.6 us -> 24.8 us
  between operations: 14 us -> 0.84 us
  other arithmetic: 14.2 us -> 8.35 us
    psum x1 -> x0, waiting for transfers between devices: 233 us -> none  [body(): grad_out = lax.psum(grad_term, ('seq', 'dp')) * all_tokens ** (-0.5)]
    all_gather x0 -> x4, blocking collectives: none -> 148 us  [the longest x3 122 us: reduce_grad(): outs.append(lax.all_gather(small, PLANE, axis=0, tiled=True))]
    all_gather x2 -> x0, waiting for transfers between devices: 51.9 us -> none  [the longest x1 41.1 us: body(): piece = lax.all_gather(key_value, 'seq', axis=0, tiled=True)]
    pallas_call x0 -> x5, Pallas kernels: none -> 46.3 us  [call(): pl.pallas_call(kernel, grid_spec=pltpu.PrefetchScalarGridSpec(num_scalar_...]
    dot_general x9 -> x0, matrix products: 32.9 us -> none  [the longest x2 8.08 us: body(): jnp.einsum('qhd,khd->hqk', q_heads, k_heads, preferred_element_type=jnp.f...]
    reduce_scatter x2 -> x0, waiting for transfers between devices: 30.8 us -> none  [the longest x1 27 us: body(): lax.psum_scatter((fetched * present[:, None].astype(jnp.float32)).astype(...]
    all_to_all x0 -> x1, blocking collectives: none -> 21.1 us  [reduce_grad(): got = lax.all_to_all(part, PLANE, 0, 0)]
    all_to_all x0 -> x3, waiting for transfers between devices: none -> 19.8 us  [the longest x2 19.8 us: reduce_grad(): got = lax.all_to_all(part, PLANE, 0, 0)]
  transfers between devices with their start and end apart: 5 -> 10, of which waited for: 5 -> 4; matrix products, arithmetic and copies ran while one was open for 11% -> 4% of each run, Pallas kernels for 0% -> 12%
where the time goes in v1:
time: 297 us; the launch traced here: 296 us
  blocking collectives  169 us (57%)
  Pallas kernels  46.3 us (16%)
  waiting for transfers between devices  37.2 us (13%)
  starting transfers between devices  24.8 us (8%)
  local copies, waits for them, and re-layouts  9.86 us (3%)
  other arithmetic  8.35 us (3%)
    all_gather x3, blocking collectives, reduce_grad(): outs.append(lax.all_gather(small, PLANE, axis=0, tiled=True))  122 us
    pallas_call x5, Pallas kernels, call(): pl.pallas_call(kernel, grid_spec=pltpu.PrefetchScalarGridSpec(num_scalar_...  46.3 us
    all_gather x1, blocking collectives, reduce_grad(): mine = lax.all_gather(got, 'z', axis=0).reshape(shape)  26.1 us
    all_to_all x1, blocking collectives, reduce_grad(): got = lax.all_to_all(part, PLANE, 0, 0)  21.1 us
    all_to_all x2, waiting for transfers between devices, reduce_grad(): got = lax.all_to_all(part, PLANE, 0, 0)  19.8 us
    ppermute x7, waiting for transfers between devices, swap(): return lax.ppermute(value, axis, [(0, 1), (1, 0)])  17.4 us
    all_to_all x2, starting transfers between devices, reduce_grad(): got = lax.all_to_all(part, PLANE, 0, 0)  11.1 us
    all_to_all x1, starting transfers between devices, reduce_grad(): got = sum_parts(lax.all_to_all(part, 'z', 0, 0))  8.47 us
  transfers between devices with their start and end apart: 10, of which 4 were waited for; matrix products, arithmetic and copies ran while one was open for 4% of the time, Pallas kernels for 12%

profile of v1, /device:TPU:2, one launch (start us, length us, event | category | flops | bytes accessed | tf_op | source)
XLA Modules:
  0.0 296.2 jit_solution(12153148838209396108)
XLA Ops:
  0.6 0.1 collective-permute-start.2
  0.8 1.2 dynamic-slice_bitcast_fusion
  1.9 2.2 collective-permute-start.3
  4.1 1.4 collective-permute-start
  5.6 0.2 reduce-window.7
  5.8 0.1 stack_tile.6
  5.8 0.1 stack_tile.7
  6.0 0.1 pad_add_fusion.1.place_ref
  6.0 9.4 %collective-permute-done.3.own_ref = bf16[256,768]{1,0:T(8,128)(2,1)S(1)} collective-permute-done((bf16[256,768]{1,0:T(8,128)(2,1)S(1)}, bf16[256,768]{1,0:T(8,128)(2,1)S(1)}, u32[]{:S(2)}, u32[]{:S(2)}) %collective-permute-start.3) | collective-permute-done | bytes 393248 | tf_op jit(solution)/shard_map/ppermute | solution.py:211
  15.4 0.0 collective-permute-start.4
  15.4 8.0 %collective-permute-done.own_ref = bf16[256,768]{1,0:T(8,128)(2,1)S(1)} collective-permute-done((bf16[256,768]{1,0:T(8,128)(2,1)S(1)}, bf16[256,768]{1,0:T(8,128)(2,1)S(1)}, u32[]{:S(2)}, u32[]{:S(2)}) %collective-permute-start) | collective-permute-done | bytes 393248 | tf_op jit(solution)/shard_map/ppermute | solution.py:211
  23.5 0.0 collective-permute-start.1
  23.5 17.5 %shard_map.94 = (bf16[512,768]{1,0:T(8,128)(2,1)S(1)}, f32[512,1536]{1,0:T(8,128)S(1)}) custom-call(s32[2]{0:T(128)S(1)} %pad_add_fusion.1.place_ref, s32[8,128]{1,0:T(8,128)S(1)} %pad.13.bounds_ref, bf16[512,768]{1,0:T(8,128)(2,1)S(1)} %bitcast.34, bf16[512,768]{1,0:T(8,128)(2,1)S(1)} %collective-permute-done.2.oth_ref, bf16[3,1536,768]{2,1,0:T(8,128)(2,1)} %wv_ref.3), custom_call_target="tpu_custom_call" | custom-call | flops 7000000000 | bytes 12000000 | tf_op jit(solution)/shard_map/pallas_call | solution.py:190
  41.0 0.0 copy-start.2
  41.0 8.7 %shard_map.95.acc_in_ref = f32[512,1536]{1,0:T(8,128)S(1)} custom-call(s32[2]{0:T(128)S(1)} %pad_add_fusion.1.place_ref, s32[8,128]{1,0:T(8,128)S(1)} %pad.13.bounds_ref, bf16[256,768]{1,0:T(8,128)(2,1)S(1)} %collective-permute-done.3.own_ref, bf16[256,768]{1,0:T(8,128)(2,1)S(1)} %collective-permute-done.4.oth_ref, ...), custom_call_target="tpu_custom_call", output_to_operand_aliasing={{}: (7, {})} | custom-call | flops 3000000000 | bytes 12000000 | tf_op jit(solution)/shard_map/pallas_call | solution.py:190
  49.7 0.0 copy-start
  49.7 1.7 copy-done
  51.3 12.0 %shard_map.96 = (bf16[512,768]{1,0:T(8,128)(2,1)S(1)}, bf16[768,1536]{1,0:T(8,128)(2,1)}) custom-call(s32[2]{0:T(128)S(1)} %pad_add_fusion.1.place_ref, s32[8,128]{1,0:T(8,128)S(1)} %pad.13.bounds_ref, bf16[256,768]{1,0:T(8,128)(2,1)S(1)} %collective-permute-done.own_ref, bf16[256,768]{1,0:T(8,128)(2,1)S(1)} %collective-permute-done.1.oth_ref, ...), custom_call_target="tpu_custom_call" | custom-call | flops 4000000000 | bytes 14000000 | tf_op jit(solution)/shard_map/pallas_call | solution.py:190
  63.3 2.9 fusion.2
  66.2 21.1 %all_to_all.20 = bf16[16,16,1536]{2,1,0:T(8,128)(2,1)} all-to-all(bf16[16,16,1536]{2,1,0:T(8,128)(2,1)S(1)} %bitcast.38), channel_id=1, replica_groups=mesh['seq'=2,'head'=2,'z'=8,'y'=4,'xl'=2] {'seq','y','xl'}, dimensions={0} | all-to-all | bytes 1572864 | tf_op jit(solution)/shard_map/all_to_all | solution.py:229
  87.3 5.6 %all-to-all-start.1 = ((bf16[16,16,1536]{2,1,0:T(8,128)(2,1)}), bf16[16,16,1536]{2,1,0:T(8,128)(2,1)}, u32[]{:S(2)}, u32[]{:S(2)}) async-start(bf16[16,16,1536]{2,1,0:T(8,128)(2,1)} %bitcast.37), calls=%async_computation.1 | async-start | bytes 1572864 | tf_op jit(solution)/shard_map/all_to_all | solution.py:229
  93.0 12.7 %all-to-all-done.1 = bf16[16,16,1536]{2,1,0:T(8,128)(2,1)} async-done(((bf16[16,16,1536]{2,1,0:T(8,128)(2,1)}), bf16[16,16,1536]{2,1,0:T(8,128)(2,1)}, u32[]{:S(2)}, u32[]{:S(2)}) %all-to-all-start.1) | async-done | bytes 786464 | tf_op jit(solution)/shard_map/all_to_all | solution.py:229
  105.7 5.5 %all-to-all-start.2 = ((bf16[16,16,1536]{2,1,0:T(8,128)(2,1)}), bf16[16,16,1536]{2,1,0:T(8,128)(2,1)}, u32[]{:S(2)}, u32[]{:S(2)}) async-start(bf16[16,16,1536]{2,1,0:T(8,128)(2,1)} %bitcast.36), calls=%async_computation.2 | async-start | bytes 1572864 | tf_op jit(solution)/shard_map/all_to_all | solution.py:229
  111.2 0.2 fusion.1
  111.3 0.1 select_reduce_fusion
  111.4 2.8 shard_map.97
  114.2 0.0 collective-permute-start.5
  114.3 1.2 reduce_sum.58
  115.5 1.2 reduce_sum.59
  116.7 7.1 %all-to-all-done.2 = bf16[16,16,1536]{2,1,0:T(8,128)(2,1)} async-done(((bf16[16,16,1536]{2,1,0:T(8,128)(2,1)}), bf16[16,16,1536]{2,1,0:T(8,128)(2,1)}, u32[]{:S(2)}, u32[]{:S(2)}) %all-to-all-start.2) | async-done | bytes 786464 | tf_op jit(solution)/shard_map/all_to_all | solution.py:229
  123.9 1.2 reduce_sum.60
  125.1 0.8 reshape.137
  125.9 8.5 %all-to-all-start.3 = ((bf16[8,8,1152]{2,1,0:T(8,128)(2,1)}), bf16[8,8,1152]{2,1,0:T(8,128)(2,1)S(1)}, u32[]{:S(2)}, u32[]{:S(2)}) async-start(bf16[8,8,1152]{2,1,0:T(8,128)(2,1)} %reshape.137), calls=%async_computation.3 | async-start | bytes 294912 | tf_op jit(solution)/shard_map/all_to_all | solution.py:235
  134.4 1.0 copy.14
  135.5 1.0 copy-done.6
  136.5 5.4 %shard_map.98 = (bf16[512,768]{1,0:T(8,128)(2,1)}, bf16[512,768]{1,0:T(8,128)(2,1)}, bf16[512,768]{1,0:T(8,128)(2,1)S(1)}) custom-call(s32[2]{0:T(128)S(1)} %pad_add_fusion.1.place_ref, bf16[512,768]{1,0:T(8,128)(2,1)S(1)} %get-tuple-element.12.attn_ref, bf16[768,1536]{1,0:T(8,128)(2,1)S(1)} %copy-done.1, bf16[512,768]{1,0:T(8,128)(2,1)} %collective-permute-done.5.recv_ref, ...), custom_call_target="tpu_custom_call" | custom-call | flops 1400000000 | bytes 6000000 | tf_op jit(solution)/shard_map/pallas_call | solution.py:190
  141.9 0.9 copy-done.4
  142.8 1.5 collective-permute-start.6
  144.3 26.1 %all-gather = bf16[64,1152]{1,0:T(8,128)(2,1)S(1)} all-gather(bf16[8,1152]{1,0:T(8,128)(2,1)S(1)} %reduce_sum.61), channel_id=2, replica_groups=mesh['seq'=2,'head'=2,'z'=8,'y'=4,'xl'=2] {'z'}, dimensions={0}, use_global_device_ids=true | all-gather | bytes 165888 | tf_op jit(solution)/shard_map/all_gather | solution.py:236
  170.4 0.1 reshape.138
  170.6 40.4 %all_gather.19 = bf16[256,1536]{1,0:T(8,128)(2,1)S(1)} all-gather(bf16[16,1536]{1,0:T(8,128)(2,1)S(1)} %get-tuple-element.23), channel_id=1, replica_groups=mesh['seq'=2,'head'=2,'z'=8,'y'=4,'xl'=2] {'seq','y','xl'}, dimensions={0}, use_global_device_ids=true | all-gather | bytes 835584 | tf_op jit(solution)/shard_map/all_gather | solution.py:240
  211.0 0.2 convert_multiply_fusion
  211.2 42.8 %all_gather.18 = bf16[256,1536]{1,0:T(8,128)(2,1)S(1)} all-gather(bf16[16,1536]{1,0:T(8,128)(2,1)S(1)} %get-tuple-element.24), channel_id=1, replica_groups=mesh['seq'=2,'head'=2,'z'=8,'y'=4,'xl'=2] {'seq','y','xl'}, dimensions={0}, use_global_device_ids=true | all-gather | bytes 835584 | tf_op jit(solution)/shard_map/all_gather | solution.py:240
  254.0 0.2 convert_multiply_fusion.1
  254.1 38.4 %all_gather.17 = bf16[256,1536]{1,0:T(8,128)(2,1)S(1)} all-gather(bf16[16,1536]{1,0:T(8,128)(2,1)S(1)} %get-tuple-element.22), channel_id=1, replica_groups=mesh['seq'=2,'head'=2,'z'=8,'y'=4,'xl'=2] {'seq','y','xl'}, dimensions={0}, use_global_device_ids=true | all-gather | bytes 835584 | tf_op jit(solution)/shard_map/all_gather | solution.py:240
  292.5 0.2 convert_multiply_fusion.2
  292.7 2.5 pad_maximum_fusion
  295.2 1.0 add_bitcast_fusion
  (37 shorter events, 0.2 us)
Async XLA Ops:
  0.6 22.8 %copy-start.3 = (bf16[1,512,768]{2,1,0:T(8,128)(2,1)S(1)}, bf16[1,512,768]{2,1,0:T(8,128)(2,1)}, u32[]{:S(2)}) copy-start(bf16[1,512,768]{2,1,0:T(8,128)(2,1)} %param.7) | copy-start | bytes 2359300
  0.6 4.9 %copy-start.8 = (s32[1,8]{1,0:T(1,128)S(1)}, s32[1,8]{1,0:T(1,128)}, u32[]{:S(2)}) copy-start(s32[1,8]{1,0:T(1,128)} %param.8) | copy-start | bytes 100
  0.6 22.8 %collective-permute-start.2 = (bf16[512,768]{1,0:T(8,128)(2,1)}, bf16[512,768]{1,0:T(8,128)(2,1)S(1)}, u32[]{:S(2)}, u32[]{:S(2)}) collective-permute-start(bf16[512,768]{1,0:T(8,128)(2,1)} %bitcast.33), channel_id=1, source_target_pairs={{0,64},{64,0},{1,65},{65,1},{2,66},{66,2},{3,67},{67,3},{4,68},{68... | collective-permute-start | bytes 2359304 | tf_op jit(solution)/shard_map/ppermute | solution.py:211
  1.9 13.5 %collective-permute-start.3 = (bf16[256,768]{1,0:T(8,128)(2,1)S(1)}, bf16[256,768]{1,0:T(8,128)(2,1)S(1)}, u32[]{:S(2)}, u32[]{:S(2)}) collective-permute-start(bf16[256,768]{1,0:T(8,128)(2,1)S(1)} %get-tuple-element.20), channel_id=1, source_target_pairs={{0,128},{128,0},{1,129},{129,1},{2,130},{130,2},{3,131},{131,3},{4... | collective-permute-start | bytes 1179656 | tf_op jit(solution)/shard_map/ppermute | solution.py:211
  4.1 19.3 %collective-permute-start = (bf16[256,768]{1,0:T(8,128)(2,1)S(1)}, bf16[256,768]{1,0:T(8,128)(2,1)S(1)}, u32[]{:S(2)}, u32[]{:S(2)}) collective-permute-start(bf16[256,768]{1,0:T(8,128)(2,1)S(1)} %get-tuple-element.21), channel_id=1, source_target_pairs={{0,128},{128,0},{1,129},{129,1},{2,130},{130,2},{3,131},{131,3},{4... | collective-permute-start | bytes 1179656 | tf_op jit(solution)/shard_map/ppermute | solution.py:211
  15.4 25.5 %collective-permute-start.4 = (bf16[256,768]{1,0:T(8,128)(2,1)S(1)}, bf16[256,768]{1,0:T(8,128)(2,1)S(1)}, u32[]{:S(2)}, u32[]{:S(2)}) collective-permute-start(bf16[256,768]{1,0:T(8,128)(2,1)S(1)} %collective-permute-done.3.own_ref), channel_id=1, source_target_pairs={{0,64},{64,0},{1,65},{65,1},{2,66},{66,2},{3,67},{67,3},{4,68},{68... | collective-permute-start | bytes 1179656 | tf_op jit(solution)/shard_map/ppermute | solution.py:211
  23.5 27.9 %collective-permute-start.1 = (bf16[256,768]{1,0:T(8,128)(2,1)S(1)}, bf16[256,768]{1,0:T(8,128)(2,1)S(1)}, u32[]{:S(2)}, u32[]{:S(2)}) collective-permute-start(bf16[256,768]{1,0:T(8,128)(2,1)S(1)} %collective-permute-done.own_ref), channel_id=1, source_target_pairs={{0,64},{64,0},{1,65},{65,1},{2,66},{66,2},{3,67},{67,3},{4,68},{68... | collective-permute-start | bytes 1179656 | tf_op jit(solution)/shard_map/ppermute | solution.py:211
  41.0 10.4 %copy-start.2 = (bf16[1,512,1536]{2,1,0:T(8,128)(2,1)S(1)}, bf16[1,512,1536]{2,1,0:T(8,128)(2,1)}, u32[]{:S(2)}) copy-start(bf16[1,512,1536]{2,1,0:T(8,128)(2,1)} %param.11) | copy-start | bytes 4718596
  49.7 1.7 copy-start
  66.2 26.7 %copy-start.9 = (s32[1,8]{1,0:T(1,128)S(1)}, s32[1,8]{1,0:T(1,128)}, u32[]{:S(2)}) copy-start(s32[1,8]{1,0:T(1,128)} %param.9) | copy-start | bytes 100
  87.3 23.8 %copy-start.7 = (s32[1,8,128]{2,1,0:T(8,128)S(1)}, s32[1,8,128]{2,1,0:T(8,128)}, u32[]{:S(2)}) copy-start(s32[1,8,128]{2,1,0:T(8,128)} %param.10) | copy-start | bytes 12292
  87.3 24.1 %copy-start.1 = (bf16[768,1536]{1,0:T(8,128)(2,1)S(1)}, bf16[768,1536]{1,0:T(8,128)(2,1)}, u32[]{:S(2)}) copy-start(bf16[768,1536]{1,0:T(8,128)(2,1)} %w_ref.5) | copy-start | bytes 7077892
  87.3 18.3 %all-to-all-start.1 = ((bf16[16,16,1536]{2,1,0:T(8,128)(2,1)}), bf16[16,16,1536]{2,1,0:T(8,128)(2,1)}, u32[]{:S(2)}, u32[]{:S(2)}) async-start(bf16[16,16,1536]{2,1,0:T(8,128)(2,1)} %bitcast.37), calls=%async_computation.1 | async-start | bytes 1572864 | tf_op jit(solution)/shard_map/all_to_all | solution.py:229
  105.7 18.2 %all-to-all-start.2 = ((bf16[16,16,1536]{2,1,0:T(8,128)(2,1)}), bf16[16,16,1536]{2,1,0:T(8,128)(2,1)}, u32[]{:S(2)}, u32[]{:S(2)}) async-start(bf16[16,16,1536]{2,1,0:T(8,128)(2,1)} %bitcast.36), calls=%async_computation.2 | async-start | bytes 1572864 | tf_op jit(solution)/shard_map/all_to_all | solution.py:229
  114.2 21.2 %collective-permute-start.5 = (bf16[512,768]{1,0:T(8,128)(2,1)}, bf16[512,768]{1,0:T(8,128)(2,1)}, u32[]{:S(2)}, u32[]{:S(2)}) collective-permute-start(bf16[512,768]{1,0:T(8,128)(2,1)} %shard_map.97), channel_id=1, source_target_pairs={{0,64},{64,0},{1,65},{65,1},{2,66},{66,2},{3,67},{67,3},{4,68},{68... | collective-permute-start | bytes 2359304 | tf_op jit(solution)/shard_map/ppermute | solution.py:211
  125.9 18.4 %all-to-all-start.3 = ((bf16[8,8,1152]{2,1,0:T(8,128)(2,1)}), bf16[8,8,1152]{2,1,0:T(8,128)(2,1)S(1)}, u32[]{:S(2)}, u32[]{:S(2)}) async-start(bf16[8,8,1152]{2,1,0:T(8,128)(2,1)} %reshape.137), calls=%async_computation.3 | async-start | bytes 294912 | tf_op jit(solution)/shard_map/all_to_all | solution.py:235
  135.5 1.0 copy-start.6
  141.9 0.9 copy-start.4
  142.8 152.5 %collective-permute-start.6 = (bf16[512,768]{1,0:T(8,128)(2,1)}, bf16[512,768]{1,0:T(8,128)(2,1)S(1)}, u32[]{:S(2)}, u32[]{:S(2)}) collective-permute-start(bf16[512,768]{1,0:T(8,128)(2,1)} %get-tuple-element.15), channel_id=1, source_target_pairs={{0,128},{128,0},{1,129},{129,1},{2,130},{130,2},{3,131},{131,3},{4... | collective-permute-start | bytes 2359304 | tf_op jit(solution)/shard_map/ppermute | solution.py:211
  292.7 2.5 copy-start.5

commit v2 on v1

--- a/solution.py
+++ b/solution.py
@@ -16,7 +16,6 @@
 EPS_HEAD = 1e-06
 BF = jnp.bfloat16
 F32 = jnp.float32
-PLANE = ("seq", "y", "xl")
 VMEM_LIMIT = 48 * 1024 * 1024
 
 
@@ -53,10 +52,7 @@
 
 
 def head_norm(values, ones):
-    square = values * values
-    high = square.astype(BF)
-    low = (square - high.astype(F32)).astype(BF)
-    mean = jnp.dot(high, ones, preferred_element_type=F32) + jnp.dot(low, ones, preferred_element_type=F32)
+    mean = jnp.dot((values * values).astype(BF), ones, preferred_element_type=F32)
     return values * lax.rsqrt(mean + EPS_HEAD)
 
 
@@ -117,59 +113,41 @@
     attend_group(q, k, v, qf_ref[...], kf_ref[...], emit)
 
 
-def near_kernel(place_ref, bounds_ref, own_ref, oth_ref, wk_ref, wv_ref, q_ref, acc_in_ref, acc_ref, normed_ref, qf_ref, kf_ref, ones_ref):
+def foreign_kernel(place_ref, bounds_ref, own_ref, oth_ref, wk_ref, wv_ref, q_ref, acc_in_ref, attn_ref, turned_ref, normed_ref, qf_ref, kf_ref, ones_ref, k_ref, v_ref, acc_ref):
     rows = own_ref.shape[0]
-    span = q_ref.shape[0]
+    half = rows // 2
 
     @pl.when(pl.program_id(0) == 0)
     def _():
         norm_rows(place_ref[1], own_ref, oth_ref, normed_ref, rows)
-        qf_ref[...] = features(bounds_ref, place_ref[0] * span, span, BIG, -BIG)
-        kf_ref[...] = features(bounds_ref, jnp.where(place_ref[0] == 0, span, span - rows), rows, 1.0, 1.0)
+        qf_ref[...] = features(bounds_ref, place_ref[0] * rows, rows, BIG, -BIG)
+        kf_ref[...] = features(bounds_ref, (1 - place_ref[0]) * rows, rows, 1.0, 1.0)
         ones_ref[...] = ones_block()
 
     normed = normed_ref[...]
-    k = head_norm(jnp.dot(normed, wk_ref[0], preferred_element_type=F32), ones_ref[...]).astype(BF)
-    v = jnp.dot(normed, wv_ref[0], preferred_element_type=F32).astype(BF)
-
-    def emit(head, r):
+    k_ref[...] = head_norm(jnp.dot(normed, wk_ref[0], preferred_element_type=F32), ones_ref[...]).astype(BF)
+    v_ref[...] = jnp.dot(normed, wv_ref[0], preferred_element_type=F32).astype(BF)
+    near = pl.ds(pl.multiple_of(place_ref[0] * half, half), half)
+    far = pl.ds(pl.multiple_of((1 - place_ref[0]) * half, half), half)
+
+    def emit_near(head, r):
         lanes = slice(head * 128, head * 128 + 128)
         acc_ref[:, lanes] = acc_in_ref[:, lanes] + r
 
-    attend_group(q_ref[...], k, v, qf_ref[...], kf_ref[...], emit)
-
-
-def far_kernel(place_ref, bounds_ref, own_ref, oth_ref, wk_ref, wv_ref, q_ref, acc_in_ref, cot_ref, attn_ref, grad_ref, normed_ref, qf_ref, kf_ref, ones_ref, acc_ref):
-    rows = own_ref.shape[0]
-    span = acc_in_ref.shape[0]
-    part = q_ref.shape[0]
-    begin = jnp.where(place_ref[0] == 0, span - part, 0)
-
-    @pl.when(pl.program_id(0) == 0)
-    def _():
-        norm_rows(place_ref[1], own_ref, oth_ref, normed_ref, rows)
-        qf_ref[...] = features(bounds_ref, place_ref[0] * span + begin, part, BIG, -BIG)
-        kf_ref[...] = features(bounds_ref, jnp.where(place_ref[0] == 0, 2 * span - rows, 0), rows, 1.0, 1.0)
-        ones_ref[...] = ones_block()
-
-    normed = normed_ref[...]
-    k = head_norm(jnp.dot(normed, wk_ref[0], preferred_element_type=F32), ones_ref[...]).astype(BF)
-    v = jnp.dot(normed, wv_ref[0], preferred_element_type=F32).astype(BF)
-    acc_ref[...] = acc_in_ref[...]
-    at = pl.ds(pl.multiple_of(begin, part), part)
-
-    def emit(head, r):
+    attend_group(q_ref[...], k_ref[near, :], v_ref[near, :], qf_ref[...], kf_ref[near, :], emit_near)
+
+    def emit_far(head, r):
         lanes = slice(head * 128, head * 128 + 128)
-        acc_ref[at, lanes] = acc_ref[at, lanes] + r
-
-    attend_group(q_ref[...], k, v, qf_ref[...], kf_ref[...], emit)
-    low = lower_half(span)
+        acc_ref[far, lanes] = acc_ref[far, lanes] + r
+
+    attend_group(q_ref[far, :], k_ref[far, :], v_ref[far, :], qf_ref[far, :], kf_ref[far, :], emit_far)
+    low = lower_half(rows)
     for pair in range(2):
         even = acc_ref[:, pair * 256 : pair * 256 + 128]
         odd = acc_ref[:, pair * 256 + 128 : pair * 256 + 256]
         total = pltpu.roll(jnp.where(low, odd, even), HD, 1)
         attn_ref[:, pair * 128 : pair * 128 + 128] = (jnp.where(low, even, odd) / total).astype(BF)
-    grad_ref[...] = lax.dot_general(attn_ref[...], cot_ref[...], (((0,), (0,)), ((), ())), preferred_element_type=F32).astype(BF)
+    turned_ref[...] = attn_ref[...].T
 
 
 def send_kernel(place_ref, attn_ref, w_ref, out_ref):
@@ -211,52 +189,165 @@
     return lax.ppermute(value, axis, [(0, 1), (1, 0)])
 
 
-def sum_parts(parts):
-    return jnp.sum(parts.astype(F32), axis=0).astype(BF)
-
-
-def reduce_grad(grad):
-    rows, width = grad.shape
-    n = 1
-    for axis in PLANE:
-        n *= lax.axis_size(axis)
-    nz = lax.axis_size("z")
-    chunks = 3
-    span = rows // chunks
-    pieces = []
-    for c in range(chunks):
-        part = grad[c * span : c * span + span].reshape(n, span // n, width)
-        got = lax.all_to_all(part, PLANE, 0, 0)
-        pieces.append(sum_parts(got))
-    mine = jnp.concatenate(pieces, axis=0)
-    if nz > 1:
-        shape = mine.shape
-        part = mine.reshape(nz, 8, -1)
-        got = sum_parts(lax.all_to_all(part, "z", 0, 0))
-        mine = lax.all_gather(got, "z", axis=0).reshape(shape)
-    outs = []
-    for c in range(chunks):
-        small = mine[c * (span // n) : (c + 1) * (span // n)]
-        outs.append(lax.all_gather(small, PLANE, axis=0, tiled=True))
-    return outs
+def grad_kernel(mask_ref, turned_ref, cot_ref, send_ref, keep_ref):
+    mask = mask_ref[0]
+    eight, piece, _ = send_ref.shape
+    top = mask >> 3
+    block = 4 * piece
+    for out, upper in ((send_ref, 1 - top), (keep_ref, top)):
+        for b in range(2):
+            first = pl.multiple_of(upper * eight * piece + b * block, piece)
+            got = jnp.dot(turned_ref[pl.ds(first, block), :], cot_ref[...], preferred_element_type=F32).astype(BF)
+            for i in range(4):
+                out[(b * 4 + i) ^ (mask & 7)] = got[i * piece : i * piece + piece]
+
+
+def place_kernel(mask_ref, lower0_ref, upper0_ref, lower1_ref, upper1_ref, out_ref, *, scale):
+    _, piece, width = lower0_ref.shape
+    for i in range(2):
+        rows = slice(i * piece, i * piece + piece)
+        for c, (lower, upper) in enumerate(((lower0_ref, upper0_ref), (lower1_ref, upper1_ref))):
+            at = (pl.program_id(0) * 2 + i) ^ mask_ref[c]
+            cols = slice(c * width, c * width + width)
+
+            @pl.when(at < 8)
+            def _():
+                out_ref[rows, cols] = lower[at & 7].astype(F32) * scale
+
+            @pl.when(at >= 8)
+            def _():
+                out_ref[rows, cols] = upper[at & 7].astype(F32) * scale
+
+
+AXES = ("seq", "head", "z", "y", "xl")
+ROUTES = (
+    ((("y", 0), ("y", 1), ("z", 0), ("z", 1)), (("z", 0), ("z", 1), ("y", 0), ("y", 1))),
+    ((("z", 1), ("z", 0), ("y", 1), ("y", 0)), (("y", 1), ("y", 0), ("z", 1), ("z", 0))),
+)
+
+
+def across(i, kind, n):
+    if kind == 0:
+        return i ^ 1
+    return (i + 1) % n if i % 2 else (i - 1) % n
+
+
+def bit_of(i, kind):
+    return ((i + 1) >> 1) & 1 if kind == 0 else (i >> 1) & 1
+
+
+def every_device(sizes):
+    for i in range(sizes[0] * sizes[1] * sizes[2] * sizes[3] * sizes[4]):
+        at, rest = {}, i
+        for name, n in reversed(list(zip(AXES, sizes))):
+            at[name] = rest % n
+            rest //= n
+        yield i, at
+
+
+def index_of(at, sizes):
+    i = 0
+    for name, n in zip(AXES, sizes):
+        i = i * n + at[name]
+    return i
+
+
+def pairs(sizes, partner):
+    out = []
+    for i, at in every_device(sizes):
+        out.append((i, index_of(partner(at), sizes)))
+    return out
+
+
+def pair_table(sizes, chunk, stage):
+    n = dict(zip(AXES, sizes))
+
+    def partner(at):
+        axis, kind = ROUTES[chunk][at["head"]][stage]
+        return {**at, axis: across(at[axis], kind, n[axis])}
+
+    return pairs(sizes, partner)
+
+
+def last_tables(sizes):
+    n = dict(zip(AXES, sizes))
+    x = lambda at: at["seq"] * n["xl"] + at["xl"]
+    tables = []
+    for kind in (0, 1):
+        def partner(at, kind=kind):
+            to = across(x(at), kind, n["seq"] * n["xl"])
+            return {**at, "seq": to // n["xl"], "xl": to % n["xl"]}
+
+        tables.append(pairs(sizes, partner))
+    tables.append(pairs(sizes, lambda at: {**at, "z": (at["z"] + n["z"] // 2) % n["z"]}))
+    return tables
+
+
+def mask_of(chunk, head):
+    masks = []
+    for core in (0, 1):
+        mask = jnp.int32(0)
+        for axis, kind in ROUTES[chunk][core]:
+            mask = mask * 2 + bit_of(lax.axis_index(axis).astype(jnp.int32), kind)
+        masks.append(mask)
+    return jnp.where(head == 0, masks[0], masks[1])
+
+
+def add(a, b):
+    return (a.astype(F32) + b.astype(F32)).astype(BF)
+
+
+def reduce_grad(turned, cot, scale, head):
+    share, width = turned.shape[0], cot.shape[1]
+    sizes = tuple(lax.axis_size(a) for a in AXES)
+    masks = [mask_of(c, head) for c in range(2)]
+    piece = share // 16
+    half = jax.ShapeDtypeStruct((8, piece, width // 2), BF)
+    move = lambda value, table: lax.ppermute(value, AXES, table)
+    held = []
+    for c in range(2):
+        held.append(list(call(
+            grad_kernel, masks[c][None], (1,),
+            [whole(turned.shape), pl.BlockSpec((cot.shape[0], width // 2), lambda g, s, c=c: (0, c))],
+            [whole(half.shape)] * 2, [half] * 2, [], 6 * 10**8, 4 * 10**6, (turned, cot),
+        )))
+    for stage in range(4):
+        for c in range(2):
+            send, keep = held[c]
+            got = move(send, pair_table(sizes, c, stage))
+            n = keep.shape[0] // 2
+            if n:
+                held[c] = [add(keep[n:], got[n:]), add(keep[:n], got[:n])]
+            else:
+                held[c] = add(keep, got)
+    both = jnp.concatenate(held, axis=0)
+    for table in last_tables(sizes):
+        both = add(both, move(both, table))
+    lower = [both[0:1], both[1:2]]
+    upper = [None, None]
+    for stage in (3, 2, 1, 0):
+        for c in range(2):
+            if upper[c] is not None:
+                lower[c] = jnp.concatenate([lower[c], upper[c]], axis=0)
+            upper[c] = move(lower[c], pair_table(sizes, c, stage))
+    return call(
+        functools.partial(place_kernel, scale=scale), jnp.stack(masks), (8,),
+        [whole(half.shape)] * 4, pl.BlockSpec((2 * piece, width), lambda g, s: (g, 0)),
+        jax.ShapeDtypeStruct((share, width), F32), [], 10**6, 7 * 10**6,
+        (lower[0], upper[0], lower[1], upper[1]),
+    )
 
 
 def body(tokens, lengths, owner_slot, latent_index, cotangent, qkv_weight, out_weight):
     own = tokens[0]
     rows, share = own.shape
-    half = rows // 2
     groups = share // GROUP
     seq = lax.axis_index("seq")
     head = lax.axis_index("head")
     place = jnp.stack([seq, head]).astype(jnp.int32)
 
-    near = lax.dynamic_slice_in_dim(own, (1 - seq) * half, half, 0)
-    far = lax.dynamic_slice_in_dim(own, seq * half, half, 0)
-    near_own = swap(near, "seq")
-    far_own = swap(far, "seq")
     oth = swap(own, "head")
-    near_oth = swap(near_own, "head")
-    far_oth = swap(far_own, "head")
+    foreign_own = swap(own, "seq")
 
     sizes = lengths[0]
     images = sizes.shape[0]
@@ -280,25 +371,20 @@
         [jax.ShapeDtypeStruct((rows, share), BF), jax.ShapeDtypeStruct((rows, 2 * share), F32)],
         scratch(rows, rows, rows), 7 * 10**9, 12 * 10**6, (bounds, own, oth, qkv_weight),
     )
-    acc = call(
-        near_kernel, place, (groups,),
-        [whole((8, 128)), whole((half, share)), whole((half, share)), weight(1), weight(2),
+    foreign_own, q = lax.optimization_barrier((foreign_own, q))
+    foreign_oth = swap(foreign_own, "head")
+    attn, turned = call(
+        foreign_kernel, place, (groups,),
+        [whole((8, 128)), whole((rows, share)), whole((rows, share)), weight(1), weight(2),
          columns(rows, GROUP), columns(rows, 2 * GROUP)],
-        columns(rows, 2 * GROUP),
-        jax.ShapeDtypeStruct((rows, 2 * share), F32),
-        scratch(half, rows, half), 3 * 10**9, 12 * 10**6,
-        (bounds, near_own, near_oth, qkv_weight, qkv_weight, q, acc), {7: 0},
-    )
-    attn, grad = call(
-        far_kernel, place, (groups,),
-        [whole((8, 128)), whole((half, share)), whole((half, share)), weight(1), weight(2),
-         pl.BlockSpec((half, GROUP), lambda g, s: (1 - s[0], g)), columns(rows, 2 * GROUP), whole((rows, 2 * share))],
-        [columns(rows, GROUP), pl.BlockSpec((GROUP, 2 * share), lambda g, s: (g, 0))],
-        [jax.ShapeDtypeStruct((rows, share), BF), jax.ShapeDtypeStruct((share, 2 * share), BF)],
-        scratch(half, half, half) + [pltpu.VMEM((rows, 2 * GROUP), F32)], 4 * 10**9, 14 * 10**6,
-        (bounds, far_own, far_oth, qkv_weight, qkv_weight, q, acc, cotangent[0]),
-    )
-    sums = reduce_grad(grad)
+        [columns(rows, GROUP), pl.BlockSpec((GROUP, rows), lambda g, s: (g, 0))],
+        [jax.ShapeDtypeStruct((rows, share), BF), jax.ShapeDtypeStruct((share, rows), BF)],
+        scratch(rows, rows, rows)
+        + [pltpu.VMEM((rows, GROUP), BF), pltpu.VMEM((rows, GROUP), BF), pltpu.VMEM((rows, 2 * GROUP), F32)],
+        4 * 10**9, 14 * 10**6, (bounds, foreign_own, foreign_oth, qkv_weight, qkv_weight, q, acc),
+    )
+    count = 2 * rows * lax.axis_size("z") * lax.axis_size("y") * lax.axis_size("xl")
+    grad_out = reduce_grad(turned, cotangent[0], count ** (-0.5), head)
 
     partial = call(
         send_kernel, place, (groups,),
@@ -324,8 +410,6 @@
     )
     latents = keep + swap(send, "seq")
 
-    count = 2 * rows * lax.axis_size("z") * lax.axis_size("y") * lax.axis_size("xl")
-    grad_out = jnp.concatenate([s.astype(F32) * count ** (-0.5) for s in sums], axis=0)
     return mixed[None], latents[None], grad_out
 
 

time: 297 us -> 154 us (0.52)
  blocking collectives: 169 us -> 0 us
  starting transfers between devices: 24.8 us -> 44.8 us
  waiting for transfers between devices: 37.2 us -> 42 us
    all_gather x4 -> x0, blocking collectives: 148 us -> none  [the longest x3 122 us: reduce_grad(): outs.append(lax.all_gather(small, PLANE, axis=0, tiled=True))]
    ppermute x0 -> x19, starting transfers between devices: none -> 39.8 us  [reduce_grad(): move = lambda value, table: lax.ppermute(value, AXES, table)]
    ppermute x0 -> x19, waiting for transfers between devices: none -> 37.7 us  [reduce_grad(): move = lambda value, table: lax.ppermute(value, AXES, table)]
    all_to_all x1 -> x0, blocking collectives: 21.1 us -> none  [reduce_grad(): got = lax.all_to_all(part, PLANE, 0, 0)]
    all_to_all x3 -> x0, waiting for transfers between devices: 19.8 us -> none  [the longest x2 19.8 us: reduce_grad(): got = lax.all_to_all(part, PLANE, 0, 0)]
    all_to_all x3 -> x0, starting transfers between devices: 19.6 us -> none  [the longest x2 11.1 us: reduce_grad(): got = lax.all_to_all(part, PLANE, 0, 0)]
    ppermute x7 -> x5, waiting for transfers between devices: 17.4 us -> 4.33 us  [swap(): return lax.ppermute(value, axis, [(0, 1), (1, 0)])]
    unnamed x22 -> x30, local copies, waits for them, and re-layouts: 4.66 us -> 9.79 us
  transfers between devices with their start and end apart: 10 -> 24, of which waited for: 4 -> 16; matrix products, arithmetic and copies ran while one was open for 4% -> 6% of each run, Pallas kernels for 12% -> 17%
where the time goes in v2:
time: 154 us
  Pallas kernels  45.7 us (30%)
  starting transfers between devices  44.8 us (29%)
  waiting for transfers between devices  42 us (27%)
  other arithmetic  10.5 us (7%)
  local copies, waits for them, and re-layouts  10 us (6%)
    pallas_call x7, Pallas kernels, call(): pl.pallas_call(kernel, grid_spec=pltpu.PrefetchScalarGridSpec(num_scalar_...  45.7 us
    ppermute x19, starting transfers between devices, reduce_grad(): move = lambda value, table: lax.ppermute(value, AXES, table)  39.8 us
    ppermute x19, waiting for transfers between devices, reduce_grad(): move = lambda value, table: lax.ppermute(value, AXES, table)  37.7 us
    unnamed x30, local copies, waits for them, and re-layouts  9.79 us
    ppermute x5, starting transfers between devices, swap(): return lax.ppermute(value, axis, [(0, 1), (1, 0)])  5.06 us
    convert_element_type x11, other arithmetic, add(): return (a.astype(F32) + b.astype(F32)).astype(BF)  4.89 us
    ppermute x5, waiting for transfers between devices, swap(): return lax.ppermute(value, axis, [(0, 1), (1, 0)])  4.33 us
  transfers between devices with their start and end apart: 24, of which 16 were waited for; matrix products, arithmetic and copies ran while one was open for 6% of the time, Pallas kernels for 17%

profile of v2, /device:TPU:2, one launch (start us, length us, event | category | flops | bytes accessed | tf_op | source)
XLA Modules:
  0.0 153.8 jit_solution(10179978358251281419)
XLA Ops:
  0.7 2.2 %collective-permute-start = (bf16[512,768]{1,0:T(8,128)(2,1)}, bf16[512,768]{1,0:T(8,128)(2,1)S(1)}, u32[]{:S(2)}, u32[]{:S(2)}) collective-permute-start(bf16[512,768]{1,0:T(8,128)(2,1)} %bitcast.31), channel_id=1, source_target_pairs={{0,128},{128,0},{1,129},{129,1},{2,130},{130,2},{3,131},{131,3},{4... | collective-permute-start | bytes 2359304 | tf_op jit(solution)/shard_map/ppermute | solution.py:189
  4.7 1.1 copy-done.10
  5.9 16.7 %shard_map.94 = (bf16[512,768]{1,0:T(8,128)(2,1)S(1)}, f32[512,1536]{1,0:T(8,128)S(1)}) custom-call(s32[2]{0:T(128)S(1)} %pad_add_fusion.1.place_ref, s32[8,128]{1,0:T(8,128)S(1)} %pad.13.bounds_ref, bf16[512,768]{1,0:T(8,128)(2,1)S(1)} %bitcast.32, bf16[512,768]{1,0:T(8,128)(2,1)S(1)} %collective-permute-done.1.oth_ref, bf16[3,1536,768]{2,1,0:T(8,128)(2,1)} %wv_ref.1), custom_call_target="tpu_custom_call" | custom-call | flops 7000000000 | bytes 12000000 | tf_op jit(solution)/shard_map/pallas_call | solution.py:168
  22.5 1.7 %copy-done.1 = f32[512,1536]{1,0:T(8,128)} copy-done((f32[512,1536]{1,0:T(8,128)}, f32[512,1536]{1,0:T(8,128)S(1)}, u32[]{:S(2)}) %copy-start.1) | copy-done | bytes 3145752
  25.2 2.2 %collective-permute-done.2.oth_ref = bf16[512,768]{1,0:T(8,128)(2,1)S(1)} collective-permute-done((bf16[512,768]{1,0:T(8,128)(2,1)S(1)}, bf16[512,768]{1,0:T(8,128)(2,1)S(1)}, u32[]{:S(2)}, u32[]{:S(2)}) %collective-permute-start.2) | collective-permute-done | bytes 786464 | tf_op jit(solution)/shard_map/ppermute | solution.py:189
  27.4 0.9 copy-done.5
  28.2 1.1 copy-done.4
  29.4 1.1 copy-done.6
  30.5 14.6 %shard_map.95 = (bf16[512,768]{1,0:T(8,128)(2,1)S(1)}, bf16[768,512]{1,0:T(8,128)(2,1)S(1)}) custom-call(s32[2]{0:T(128)S(1)} %pad_add_fusion.1.place_ref, s32[8,128]{1,0:T(8,128)S(1)} %pad.13.bounds_ref, bf16[512,768]{1,0:T(8,128)(2,1)S(1)} %collective-permute-done.own_ref, bf16[512,768]{1,0:T(8,128)(2,1)S(1)} %copy-done.6, bf16[3,1536,768]{2,1,0:T(8,128)(2,1)} %wv_ref.1, ...), custom_call_target="tpu_custom_call" | custom-call | flops 4000000000 | bytes 14000000 | tf_op jit(solution)/shard_map/pallas_call | solution.py:168
  46.0 1.3 shard_map.98
  47.3 1.6 %collective-permute-start.5 = (bf16[8,48,768]{2,1,0:T(8,128)(2,1)}, bf16[8,48,768]{2,1,0:T(8,128)(2,1)}, u32[]{:S(2)}, u32[]{:S(2)}) collective-permute-start(bf16[8,48,768]{2,1,0:T(8,128)(2,1)} %get-tuple-element.26), channel_id=1, source_target_pairs={{0,2},{1,3},{2,0},{3,1},{4,6},{5,7},{6,4},{7,5},{8,10},{9,11},{10,... | collective-permute-start | bytes 1769480 | tf_op jit(solution)/shard_map/ppermute | solution.py:306
  49.7 5.9 %collective-permute-start.9 = (bf16[8,48,768]{2,1,0:T(8,128)(2,1)S(1)}, bf16[8,48,768]{2,1,0:T(8,128)(2,1)S(1)}, u32[]{:S(2)}, u32[]{:S(2)}) collective-permute-start(bf16[8,48,768]{2,1,0:T(8,128)(2,1)S(1)} %get-tuple-element.28), channel_id=1, source_target_pairs={{0,56},{1,57},{2,58},{3,59},{4,60},{5,61},{6,62},{7,63},{8,16},{9,... | collective-permute-start | bytes 1769480 | tf_op jit(solution)/shard_map/ppermute | solution.py:306
  55.6 1.9 %collective-permute-done.5 = bf16[8,48,768]{2,1,0:T(8,128)(2,1)} collective-permute-done((bf16[8,48,768]{2,1,0:T(8,128)(2,1)}, bf16[8,48,768]{2,1,0:T(8,128)(2,1)}, u32[]{:S(2)}, u32[]{:S(2)}) %collective-permute-start.5) | collective-permute-done | bytes 589856 | tf_op jit(solution)/shard_map/ppermute | solution.py:306
  57.5 1.2 add_convert_fusion.3
  58.8 3.1 %collective-permute-start.6 = (bf16[4,48,768]{2,1,0:T(8,128)(2,1)S(1)}, bf16[4,48,768]{2,1,0:T(8,128)(2,1)S(1)}, u32[]{:S(2)}, u32[]{:S(2)}) collective-permute-start(bf16[4,48,768]{2,1,0:T(8,128)(2,1)S(1)} %get-tuple-element.30), channel_id=1, source_target_pairs={{0,6},{1,7},{2,4},{3,5},{4,2},{5,3},{6,0},{7,1},{8,14},{9,15},{10,... | collective-permute-start | bytes 884744 | tf_op jit(solution)/shard_map/ppermute | solution.py:306
  61.9 1.6 %collective-permute-done.9 = bf16[8,48,768]{2,1,0:T(8,128)(2,1)S(1)} collective-permute-done((bf16[8,48,768]{2,1,0:T(8,128)(2,1)S(1)}, bf16[8,48,768]{2,1,0:T(8,128)(2,1)S(1)}, u32[]{:S(2)}, u32[]{:S(2)}) %collective-permute-start.9) | collective-permute-done | bytes 589856 | tf_op jit(solution)/shard_map/ppermute | solution.py:306
  64.0 2.7 %collective-permute-done.6 = bf16[4,48,768]{2,1,0:T(8,128)(2,1)S(1)} collective-permute-done((bf16[4,48,768]{2,1,0:T(8,128)(2,1)S(1)}, bf16[4,48,768]{2,1,0:T(8,128)(2,1)S(1)}, u32[]{:S(2)}, u32[]{:S(2)}) %collective-permute-start.6) | collective-permute-done | bytes 294944 | tf_op jit(solution)/shard_map/ppermute | solution.py:306
  66.9 2.2 %collective-permute-start.7 = (bf16[2,48,768]{2,1,0:T(8,128)(2,1)S(1)}, bf16[2,48,768]{2,1,0:T(8,128)(2,1)S(1)}, u32[]{:S(2)}, u32[]{:S(2)}) collective-permute-start(bf16[2,48,768]{2,1,0:T(8,128)(2,1)S(1)} %get-tuple-element.34), channel_id=1, source_target_pairs={{0,8},{1,9},{2,10},{3,11},{4,12},{5,13},{6,14},{7,15},{8,0},{9,1},... | collective-permute-start | bytes 442376 | tf_op jit(solution)/shard_map/ppermute | solution.py:306
  69.0 1.4 collective-permute-done.10
  70.5 2.3 %collective-permute-start.11 = (bf16[2,48,768]{2,1,0:T(8,128)(2,1)S(1)}, bf16[2,48,768]{2,1,0:T(8,128)(2,1)S(1)}, u32[]{:S(2)}, u32[]{:S(2)}) collective-permute-start(bf16[2,48,768]{2,1,0:T(8,128)(2,1)S(1)} %get-tuple-element.36), channel_id=1, source_target_pairs={{0,6},{1,7},{2,4},{3,5},{4,2},{5,3},{6,0},{7,1},{8,14},{9,15},{10,... | collective-permute-start | bytes 442376 | tf_op jit(solution)/shard_map/ppermute | solution.py:306
  72.8 5.4 %collective-permute-start.8 = (bf16[1,48,768]{2,1,0:T(8,128)(2,1)S(1)}, bf16[1,48,768]{2,1,0:T(8,128)(2,1)S(1)}, u32[]{:S(2)}, u32[]{:S(2)}) collective-permute-start(bf16[1,48,768]{2,1,0:T(8,128)(2,1)S(1)} %add_convert_fusion.15), channel_id=1, source_target_pairs={{0,56},{1,57},{2,58},{3,59},{4,60},{5,61},{6,62},{7,63},{8,16},{9,... | collective-permute-start | bytes 221192 | tf_op jit(solution)/shard_map/ppermute | solution.py:306
  78.7 1.9 %collective-permute-done.8 = bf16[1,48,768]{2,1,0:T(8,128)(2,1)S(1)} collective-permute-done((bf16[1,48,768]{2,1,0:T(8,128)(2,1)S(1)}, bf16[1,48,768]{2,1,0:T(8,128)(2,1)S(1)}, u32[]{:S(2)}, u32[]{:S(2)}) %collective-permute-start.8) | collective-permute-done | bytes 73760 | tf_op jit(solution)/shard_map/ppermute | solution.py:306
  80.6 2.1 %collective-permute-done.12 = bf16[1,48,768]{2,1,0:T(8,128)(2,1)S(1)} collective-permute-done((bf16[1,48,768]{2,1,0:T(8,128)(2,1)S(1)}, bf16[1,48,768]{2,1,0:T(8,128)(2,1)S(1)}, u32[]{:S(2)}, u32[]{:S(2)}) %collective-permute-start.12) | collective-permute-done | bytes 73760 | tf_op jit(solution)/shard_map/ppermute | solution.py:306
  82.8 1.5 collective-permute-start.13
  84.5 3.5 %collective-permute-done.13 = bf16[2,48,768]{2,1,0:T(8,128)(2,1)S(1)} collective-permute-done((bf16[2,48,768]{2,1,0:T(8,128)(2,1)S(1)}, bf16[2,48,768]{2,1,0:T(8,128)(2,1)S(1)}, u32[]{:S(2)}, u32[]{:S(2)}) %collective-permute-start.13) | collective-permute-done | bytes 147488 | tf_op jit(solution)/shard_map/ppermute | solution.py:306
  88.8 5.4 %collective-permute-done.14 = bf16[2,48,768]{2,1,0:T(8,128)(2,1)} collective-permute-done((bf16[2,48,768]{2,1,0:T(8,128)(2,1)}, bf16[2,48,768]{2,1,0:T(8,128)(2,1)}, u32[]{:S(2)}, u32[]{:S(2)}) %collective-permute-start.14) | collective-permute-done | bytes 147488 | tf_op jit(solution)/shard_map/ppermute | solution.py:306
  94.2 1.6 %add_convert_fusion.5 = bf16[2,48,768]{2,1,0:T(8,128)(2,1)} fusion(bf16[2,48,768]{2,1,0:T(8,128)(2,1)} %collective-permute-done.14, bf16[2,48,768]{2,1,0:T(8,128)(2,1)S(1)} %collective-permute-done.13, bf16[1,48,768]{2,1,0:T(8,128)(2,1)S(1)} %add_convert_fusion.11, bf16[1,48,768]{2,1,0:T(8,128)(2,1)S(1)} %add_convert_fusion.14), kind=kLoop, calls=%fused_computation.10 | loop fusion | flops 663552 | bytes 589824 | tf_op jit(solution)/shard_map/convert_element_type | solution.py:297
  95.8 4.8 %collective-permute-start.15 = (bf16[2,48,768]{2,1,0:T(8,128)(2,1)}, bf16[2,48,768]{2,1,0:T(8,128)(2,1)S(1)}, u32[]{:S(2)}, u32[]{:S(2)}) collective-permute-start(bf16[2,48,768]{2,1,0:T(8,128)(2,1)} %add_convert_fusion.5), channel_id=1, source_target_pairs={{0,32},{1,33},{2,34},{3,35},{4,36},{5,37},{6,38},{7,39},{8,40},{9,... | collective-permute-start | bytes 442376 | tf_op jit(solution)/shard_map/ppermute | solution.py:306
  100.6 2.8 %shard_map.96 = bf16[512,768]{1,0:T(8,128)(2,1)} custom-call(s32[2]{0:T(128)S(1)} %pad_add_fusion.1.place_ref, bf16[512,768]{1,0:T(8,128)(2,1)S(1)} %copy-done.8, bf16[768,1536]{1,0:T(8,128)(2,1)S(1)} %copy-done.2), custom_call_target="tpu_custom_call" | custom-call | flops 600000000 | bytes 3000000 | tf_op jit(solution)/shard_map/pallas_call | solution.py:168
  103.4 1.6 %collective-permute-done.15 = bf16[2,48,768]{2,1,0:T(8,128)(2,1)S(1)} collective-permute-done((bf16[2,48,768]{2,1,0:T(8,128)(2,1)}, bf16[2,48,768]{2,1,0:T(8,128)(2,1)S(1)}, u32[]{:S(2)}, u32[]{:S(2)}) %collective-permute-start.15) | collective-permute-done | bytes 147488 | tf_op jit(solution)/shard_map/ppermute | solution.py:306
  105.0 0.9 add_convert_fusion.4
  106.0 3.7 %collective-permute-start.16 = (bf16[1,48,768]{2,1,0:T(8,128)(2,1)S(1)}, bf16[1,48,768]{2,1,0:T(8,128)(2,1)S(1)}, u32[]{:S(2)}, u32[]{:S(2)}) collective-permute-start(bf16[1,48,768]{2,1,0:T(8,128)(2,1)S(1)} %get-tuple-element.38), channel_id=1, source_target_pairs={{0,56},{1,57},{2,58},{3,59},{4,60},{5,61},{6,62},{7,63},{8,16},{9,... | collective-permute-start | bytes 221192 | tf_op jit(solution)/shard_map/ppermute | solution.py:306
  109.7 2.3 %collective-permute-done.16 = bf16[1,48,768]{2,1,0:T(8,128)(2,1)S(1)} collective-permute-done((bf16[1,48,768]{2,1,0:T(8,128)(2,1)S(1)}, bf16[1,48,768]{2,1,0:T(8,128)(2,1)S(1)}, u32[]{:S(2)}, u32[]{:S(2)}) %collective-permute-start.16) | collective-permute-done | bytes 73760 | tf_op jit(solution)/shard_map/ppermute | solution.py:306
  112.7 1.0 copy.13
  113.8 1.0 collective-permute-done.20
  114.8 2.6 %collective-permute-start.21 = (bf16[2,48,768]{2,1,0:T(8,128)(2,1)S(1)}, bf16[2,48,768]{2,1,0:T(8,128)(2,1)S(1)}, u32[]{:S(2)}, u32[]{:S(2)}) collective-permute-start(bf16[2,48,768]{2,1,0:T(8,128)(2,1)S(1)} %pad_maximum_fusion.6), channel_id=1, source_target_pairs={{0,6},{1,7},{2,4},{3,5},{4,2},{5,3},{6,0},{7,1},{8,14},{9,15},{10,... | collective-permute-start | bytes 442376 | tf_op jit(solution)/shard_map/ppermute | solution.py:306
  118.2 0.9 pad_maximum_fusion.2
  119.1 2.7 %collective-permute-start.18 = (bf16[4,48,768]{2,1,0:T(8,128)(2,1)S(1)}, bf16[4,48,768]{2,1,0:T(8,128)(2,1)S(1)}, u32[]{:S(2)}, u32[]{:S(2)}) collective-permute-start(bf16[4,48,768]{2,1,0:T(8,128)(2,1)S(1)} %pad_maximum_fusion.2), channel_id=1, source_target_pairs={{0,6},{1,7},{2,4},{3,5},{4,2},{5,3},{6,0},{7,1},{8,14},{9,15},{10,... | collective-permute-start | bytes 884744 | tf_op jit(solution)/shard_map/ppermute | solution.py:306
  121.9 1.0 copy-done.9
  122.9 5.1 %shard_map.97 = (bf16[512,768]{1,0:T(8,128)(2,1)}, bf16[512,768]{1,0:T(8,128)(2,1)S(1)}, bf16[512,768]{1,0:T(8,128)(2,1)S(1)}) custom-call(s32[2]{0:T(128)S(1)} %pad_add_fusion.1.place_ref, bf16[512,768]{1,0:T(8,128)(2,1)S(1)} %copy-done.8, bf16[768,1536]{1,0:T(8,128)(2,1)S(1)} %copy-done.2, bf16[512,768]{1,0:T(8,128)(2,1)} %collective-permute-done.3.recv_ref, ...), custom_call_target="tpu_custom_call" | custom-call | flops 1400000000 | bytes 6000000 | tf_op jit(solution)/shard_map/pallas_call | solution.py:168
  128.0 2.6 %collective-permute-start.4 = (bf16[512,768]{1,0:T(8,128)(2,1)S(1)}, bf16[512,768]{1,0:T(8,128)(2,1)S(1)}, u32[]{:S(2)}, u32[]{:S(2)}) collective-permute-start(bf16[512,768]{1,0:T(8,128)(2,1)S(1)} %get-tuple-element.23), channel_id=1, source_target_pairs={{0,128},{128,0},{1,129},{129,1},{2,130},{130,2},{3,131},{131,3},{4... | collective-permute-start | bytes 2359304 | tf_op jit(solution)/shard_map/ppermute | solution.py:189
  130.8 1.0 pad_maximum_fusion.lower0_ref
  131.9 6.3 %collective-permute-done.22 = bf16[4,48,768]{2,1,0:T(8,128)(2,1)S(1)} collective-permute-done((bf16[4,48,768]{2,1,0:T(8,128)(2,1)S(1)}, bf16[4,48,768]{2,1,0:T(8,128)(2,1)S(1)}, u32[]{:S(2)}, u32[]{:S(2)}) %collective-permute-start.22) | collective-permute-done | bytes 294944 | tf_op jit(solution)/shard_map/ppermute | solution.py:306
  138.3 2.9 %collective-permute-start.23 = (bf16[8,48,768]{2,1,0:T(8,128)(2,1)S(1)}, bf16[8,48,768]{2,1,0:T(8,128)(2,1)S(1)}, u32[]{:S(2)}, u32[]{:S(2)}) collective-permute-start(bf16[8,48,768]{2,1,0:T(8,128)(2,1)S(1)} %pad_maximum_fusion.1.lower1_ref), channel_id=1, source_target_pairs={{0,56},{1,57},{2,58},{3,59},{4,60},{5,61},{6,62},{7,63},{8,16},{9,... | collective-permute-start | bytes 1769480 | tf_op jit(solution)/shard_map/ppermute | solution.py:306
  141.2 2.2 %collective-permute-done.4 = bf16[512,768]{1,0:T(8,128)(2,1)S(1)} collective-permute-done((bf16[512,768]{1,0:T(8,128)(2,1)S(1)}, bf16[512,768]{1,0:T(8,128)(2,1)S(1)}, u32[]{:S(2)}, u32[]{:S(2)}) %collective-permute-start.4) | collective-permute-done | bytes 786464 | tf_op jit(solution)/shard_map/ppermute | solution.py:189
  143.4 1.0 add_bitcast_fusion
  144.3 5.1 %collective-permute-done.23.upper1_ref = bf16[8,48,768]{2,1,0:T(8,128)(2,1)S(1)} collective-permute-done((bf16[8,48,768]{2,1,0:T(8,128)(2,1)S(1)}, bf16[8,48,768]{2,1,0:T(8,128)(2,1)S(1)}, u32[]{:S(2)}, u32[]{:S(2)}) %collective-permute-start.23) | collective-permute-done | bytes 589856 | tf_op jit(solution)/shard_map/ppermute | solution.py:306
  149.5 4.4 %shard_map.100 = f32[768,1536]{1,0:T(8,128)} custom-call(s32[2]{0:T(128)S(1)} %pad_add_fusion.2.mask_ref, bf16[8,48,768]{2,1,0:T(8,128)(2,1)S(1)} %pad_maximum_fusion.lower0_ref, bf16[8,48,768]{2,1,0:T(8,128)(2,1)S(1)} %collective-permute-done.19.upper0_ref, bf16[8,48,768]{2,1,0:T(8,128)(2,1)S(1)} %pad_maximum_fusion.1.lower1_ref, ...), custom_call_target="tpu_custom_call" | custom-call | flops 1000000 | bytes 7000000 | tf_op jit(solution)/shard_map/pallas_call | solution.py:168
  (76 shorter events, 8.7 us)
Async XLA Ops:
  0.6 4.1 %collective-permute-start.1 = (bf16[512,768]{1,0:T(8,128)(2,1)}, bf16[512,768]{1,0:T(8,128)(2,1)S(1)}, u32[]{:S(2)}, u32[]{:S(2)}) collective-permute-start(bf16[512,768]{1,0:T(8,128)(2,1)} %bitcast.30), channel_id=1, source_target_pairs={{0,64},{64,0},{1,65},{65,1},{2,66},{66,2},{3,67},{67,3},{4,68},{68... | collective-permute-start | bytes 2359304 | tf_op jit(solution)/shard_map/ppermute | solution.py:189
  0.7 24.3 %collective-permute-start = (bf16[512,768]{1,0:T(8,128)(2,1)}, bf16[512,768]{1,0:T(8,128)(2,1)S(1)}, u32[]{:S(2)}, u32[]{:S(2)}) collective-permute-start(bf16[512,768]{1,0:T(8,128)(2,1)} %bitcast.31), channel_id=1, source_target_pairs={{0,128},{128,0},{1,129},{129,1},{2,130},{130,2},{3,131},{131,3},{4... | collective-permute-start | bytes 2359304 | tf_op jit(solution)/shard_map/ppermute | solution.py:189
  4.7 1.1 copy-start.10
  22.5 1.7 %copy-start.1 = (f32[512,1536]{1,0:T(8,128)}, f32[512,1536]{1,0:T(8,128)S(1)}, u32[]{:S(2)}) copy-start(f32[512,1536]{1,0:T(8,128)S(1)} %get-tuple-element.19.acc_in_ref) | copy-start | bytes 9437188
  24.2 0.9 copy-start.3
  25.1 2.3 %collective-permute-start.2 = (bf16[512,768]{1,0:T(8,128)(2,1)S(1)}, bf16[512,768]{1,0:T(8,128)(2,1)S(1)}, u32[]{:S(2)}, u32[]{:S(2)}) collective-permute-start(bf16[512,768]{1,0:T(8,128)(2,1)S(1)} %collective-permute-done.own_ref), channel_id=1, source_target_pairs={{0,64},{64,0},{1,65},{65,1},{2,66},{66,2},{3,67},{67,3},{4,68},{68... | collective-permute-start | bytes 2359304 | tf_op jit(solution)/shard_map/ppermute | solution.py:189
  27.4 0.9 copy-start.5
  28.2 1.1 copy-start.4
  29.4 1.1 copy-start.6
  30.5 15.5 %copy-start = (bf16[1,512,1536]{2,1,0:T(8,128)(2,1)S(1)}, bf16[1,512,1536]{2,1,0:T(8,128)(2,1)}, u32[]{:S(2)}) copy-start(bf16[1,512,1536]{2,1,0:T(8,128)(2,1)} %param.11) | copy-start | bytes 4718596
  45.1 0.9 copy-start.7
  47.3 16.7 %copy-start.12 = (s32[1,8]{1,0:T(1,128)S(1)}, s32[1,8]{1,0:T(1,128)}, u32[]{:S(2)}) copy-start(s32[1,8]{1,0:T(1,128)} %param.8) | copy-start | bytes 100
  47.3 10.2 %collective-permute-start.5 = (bf16[8,48,768]{2,1,0:T(8,128)(2,1)}, bf16[8,48,768]{2,1,0:T(8,128)(2,1)}, u32[]{:S(2)}, u32[]{:S(2)}) collective-permute-start(bf16[8,48,768]{2,1,0:T(8,128)(2,1)} %get-tuple-element.26), channel_id=1, source_target_pairs={{0,2},{1,3},{2,0},{3,1},{4,6},{5,7},{6,4},{7,5},{8,10},{9,11},{10,... | collective-permute-start | bytes 1769480 | tf_op jit(solution)/shard_map/ppermute | solution.py:306
  49.7 13.8 %collective-permute-start.9 = (bf16[8,48,768]{2,1,0:T(8,128)(2,1)S(1)}, bf16[8,48,768]{2,1,0:T(8,128)(2,1)S(1)}, u32[]{:S(2)}, u32[]{:S(2)}) collective-permute-start(bf16[8,48,768]{2,1,0:T(8,128)(2,1)S(1)} %get-tuple-element.28), channel_id=1, source_target_pairs={{0,56},{1,57},{2,58},{3,59},{4,60},{5,61},{6,62},{7,63},{8,16},{9,... | collective-permute-start | bytes 1769480 | tf_op jit(solution)/shard_map/ppermute | solution.py:306
  57.5 26.8 %copy-start.11 = (s32[1,8,128]{2,1,0:T(8,128)S(1)}, s32[1,8,128]{2,1,0:T(8,128)}, u32[]{:S(2)}) copy-start(s32[1,8,128]{2,1,0:T(8,128)} %param.10) | copy-start | bytes 12292
  57.5 31.2 %copy-start.13 = (s32[1,8]{1,0:T(1,128)S(1)}, s32[1,8]{1,0:T(1,128)}, u32[]{:S(2)}) copy-start(s32[1,8]{1,0:T(1,128)} %param.9) | copy-start | bytes 100
  58.7 41.9 %copy-start.2 = (bf16[768,1536]{1,0:T(8,128)(2,1)S(1)}, bf16[768,1536]{1,0:T(8,128)(2,1)}, u32[]{:S(2)}) copy-start(bf16[768,1536]{1,0:T(8,128)(2,1)} %w_ref.5) | copy-start | bytes 7077892
  58.8 41.9 %copy-start.8 = (bf16[512,768]{1,0:T(8,128)(2,1)S(1)}, bf16[512,768]{1,0:T(8,128)(2,1)}, u32[]{:S(2)}) copy-start(bf16[512,768]{1,0:T(8,128)(2,1)} %copy-done.7) | copy-start | bytes 2359300
  58.8 8.0 %collective-permute-start.6 = (bf16[4,48,768]{2,1,0:T(8,128)(2,1)S(1)}, bf16[4,48,768]{2,1,0:T(8,128)(2,1)S(1)}, u32[]{:S(2)}, u32[]{:S(2)}) collective-permute-start(bf16[4,48,768]{2,1,0:T(8,128)(2,1)S(1)} %get-tuple-element.30), channel_id=1, source_target_pairs={{0,6},{1,7},{2,4},{3,5},{4,2},{5,3},{6,0},{7,1},{8,14},{9,15},{10,... | collective-permute-start | bytes 884744 | tf_op jit(solution)/shard_map/ppermute | solution.py:306
  63.6 6.8 %collective-permute-start.10 = (bf16[4,48,768]{2,1,0:T(8,128)(2,1)S(1)}, bf16[4,48,768]{2,1,0:T(8,128)(2,1)S(1)}, u32[]{:S(2)}, u32[]{:S(2)}) collective-permute-start(bf16[4,48,768]{2,1,0:T(8,128)(2,1)S(1)} %get-tuple-element.32), channel_id=1, source_target_pairs={{0,8},{1,9},{2,10},{3,11},{4,12},{5,13},{6,14},{7,15},{8,0},{9,1},... | collective-permute-start | bytes 884744 | tf_op jit(solution)/shard_map/ppermute | solution.py:306
  66.9 5.9 %collective-permute-start.7 = (bf16[2,48,768]{2,1,0:T(8,128)(2,1)S(1)}, bf16[2,48,768]{2,1,0:T(8,128)(2,1)S(1)}, u32[]{:S(2)}, u32[]{:S(2)}) collective-permute-start(bf16[2,48,768]{2,1,0:T(8,128)(2,1)S(1)} %get-tuple-element.34), channel_id=1, source_target_pairs={{0,8},{1,9},{2,10},{3,11},{4,12},{5,13},{6,14},{7,15},{8,0},{9,1},... | collective-permute-start | bytes 442376 | tf_op jit(solution)/shard_map/ppermute | solution.py:306
  70.5 7.7 %collective-permute-start.11 = (bf16[2,48,768]{2,1,0:T(8,128)(2,1)S(1)}, bf16[2,48,768]{2,1,0:T(8,128)(2,1)S(1)}, u32[]{:S(2)}, u32[]{:S(2)}) collective-permute-start(bf16[2,48,768]{2,1,0:T(8,128)(2,1)S(1)} %get-tuple-element.36), channel_id=1, source_target_pairs={{0,6},{1,7},{2,4},{3,5},{4,2},{5,3},{6,0},{7,1},{8,14},{9,15},{10,... | collective-permute-start | bytes 442376 | tf_op jit(solution)/shard_map/ppermute | solution.py:306
  72.8 7.7 %collective-permute-start.8 = (bf16[1,48,768]{2,1,0:T(8,128)(2,1)S(1)}, bf16[1,48,768]{2,1,0:T(8,128)(2,1)S(1)}, u32[]{:S(2)}, u32[]{:S(2)}) collective-permute-start(bf16[1,48,768]{2,1,0:T(8,128)(2,1)S(1)} %add_convert_fusion.15), channel_id=1, source_target_pairs={{0,56},{1,57},{2,58},{3,59},{4,60},{5,61},{6,62},{7,63},{8,16},{9,... | collective-permute-start | bytes 221192 | tf_op jit(solution)/shard_map/ppermute | solution.py:306
  78.3 4.4 %collective-permute-start.12 = (bf16[1,48,768]{2,1,0:T(8,128)(2,1)S(1)}, bf16[1,48,768]{2,1,0:T(8,128)(2,1)S(1)}, u32[]{:S(2)}, u32[]{:S(2)}) collective-permute-start(bf16[1,48,768]{2,1,0:T(8,128)(2,1)S(1)} %add_convert_fusion.12), channel_id=1, source_target_pairs={{0,2},{1,3},{2,0},{3,1},{4,6},{5,7},{6,4},{7,5},{8,10},{9,11},{10,... | collective-permute-start | bytes 221192 | tf_op jit(solution)/shard_map/ppermute | solution.py:306
  82.8 5.2 %collective-permute-start.13 = (bf16[2,48,768]{2,1,0:T(8,128)(2,1)S(1)}, bf16[2,48,768]{2,1,0:T(8,128)(2,1)S(1)}, u32[]{:S(2)}, u32[]{:S(2)}) collective-permute-start(bf16[2,48,768]{2,1,0:T(8,128)(2,1)S(1)} %pad_maximum_fusion.4), channel_id=1, source_target_pairs={{0,1},{1,0},{2,3},{3,2},{4,5},{5,4},{6,7},{7,6},{8,9},{9,8},{10,11... | collective-permute-start | bytes 442376 | tf_op jit(solution)/shard_map/ppermute | solution.py:306
  88.7 5.5 %collective-permute-start.14 = (bf16[2,48,768]{2,1,0:T(8,128)(2,1)}, bf16[2,48,768]{2,1,0:T(8,128)(2,1)}, u32[]{:S(2)}, u32[]{:S(2)}) collective-permute-start(bf16[2,48,768]{2,1,0:T(8,128)(2,1)} %add_convert_fusion.6), channel_id=1, source_target_pairs={{0,129},{1,128},{2,131},{3,130},{4,133},{5,132},{6,135},{7,134},{8... | collective-permute-start | bytes 442376 | tf_op jit(solution)/shard_map/ppermute | solution.py:306
  95.8 9.3 %collective-permute-start.15 = (bf16[2,48,768]{2,1,0:T(8,128)(2,1)}, bf16[2,48,768]{2,1,0:T(8,128)(2,1)S(1)}, u32[]{:S(2)}, u32[]{:S(2)}) collective-permute-start(bf16[2,48,768]{2,1,0:T(8,128)(2,1)} %add_convert_fusion.5), channel_id=1, source_target_pairs={{0,32},{1,33},{2,34},{3,35},{4,36},{5,37},{6,38},{7,39},{8,40},{9,... | collective-permute-start | bytes 442376 | tf_op jit(solution)/shard_map/ppermute | solution.py:306
  103.4 18.4 %collective-permute-start.3 = (bf16[512,768]{1,0:T(8,128)(2,1)}, bf16[512,768]{1,0:T(8,128)(2,1)}, u32[]{:S(2)}, u32[]{:S(2)}) collective-permute-start(bf16[512,768]{1,0:T(8,128)(2,1)} %shard_map.96), channel_id=1, source_target_pairs={{0,64},{64,0},{1,65},{65,1},{2,66},{66,2},{3,67},{67,3},{4,68},{68... | collective-permute-start | bytes 2359304 | tf_op jit(solution)/shard_map/ppermute | solution.py:189
  106.0 6.0 %collective-permute-start.16 = (bf16[1,48,768]{2,1,0:T(8,128)(2,1)S(1)}, bf16[1,48,768]{2,1,0:T(8,128)(2,1)S(1)}, u32[]{:S(2)}, u32[]{:S(2)}) collective-permute-start(bf16[1,48,768]{2,1,0:T(8,128)(2,1)S(1)} %get-tuple-element.38), channel_id=1, source_target_pairs={{0,56},{1,57},{2,58},{3,59},{4,60},{5,61},{6,62},{7,63},{8,16},{9,... | collective-permute-start | bytes 221192 | tf_op jit(solution)/shard_map/ppermute | solution.py:306
  109.7 5.1 %collective-permute-start.20 = (bf16[1,48,768]{2,1,0:T(8,128)(2,1)S(1)}, bf16[1,48,768]{2,1,0:T(8,128)(2,1)S(1)}, u32[]{:S(2)}, u32[]{:S(2)}) collective-permute-start(bf16[1,48,768]{2,1,0:T(8,128)(2,1)S(1)} %get-tuple-element.37), channel_id=1, source_target_pairs={{0,2},{1,3},{2,0},{3,1},{4,6},{5,7},{6,4},{7,5},{8,10},{9,11},{10,... | collective-permute-start | bytes 221192 | tf_op jit(solution)/shard_map/ppermute | solution.py:306
  112.7 5.5 %collective-permute-start.17 = (bf16[2,48,768]{2,1,0:T(8,128)(2,1)}, bf16[2,48,768]{2,1,0:T(8,128)(2,1)}, u32[]{:S(2)}, u32[]{:S(2)}) collective-permute-start(bf16[2,48,768]{2,1,0:T(8,128)(2,1)} %pad_maximum_fusion.5), channel_id=1, source_target_pairs={{0,8},{1,9},{2,10},{3,11},{4,12},{5,13},{6,14},{7,15},{8,0},{9,1},... | collective-permute-start | bytes 442376 | tf_op jit(solution)/shard_map/ppermute | solution.py:306
  114.8 15.9 %collective-permute-start.21 = (bf16[2,48,768]{2,1,0:T(8,128)(2,1)S(1)}, bf16[2,48,768]{2,1,0:T(8,128)(2,1)S(1)}, u32[]{:S(2)}, u32[]{:S(2)}) collective-permute-start(bf16[2,48,768]{2,1,0:T(8,128)(2,1)S(1)} %pad_maximum_fusion.6), channel_id=1, source_target_pairs={{0,6},{1,7},{2,4},{3,5},{4,2},{5,3},{6,0},{7,1},{8,14},{9,15},{10,... | collective-permute-start | bytes 442376 | tf_op jit(solution)/shard_map/ppermute | solution.py:306
  119.1 11.7 %collective-permute-start.18 = (bf16[4,48,768]{2,1,0:T(8,128)(2,1)S(1)}, bf16[4,48,768]{2,1,0:T(8,128)(2,1)S(1)}, u32[]{:S(2)}, u32[]{:S(2)}) collective-permute-start(bf16[4,48,768]{2,1,0:T(8,128)(2,1)S(1)} %pad_maximum_fusion.2), channel_id=1, source_target_pairs={{0,6},{1,7},{2,4},{3,5},{4,2},{5,3},{6,0},{7,1},{8,14},{9,15},{10,... | collective-permute-start | bytes 884744 | tf_op jit(solution)/shard_map/ppermute | solution.py:306
  121.9 1.0 copy-start.9
  128.0 15.3 %collective-permute-start.4 = (bf16[512,768]{1,0:T(8,128)(2,1)S(1)}, bf16[512,768]{1,0:T(8,128)(2,1)S(1)}, u32[]{:S(2)}, u32[]{:S(2)}) collective-permute-start(bf16[512,768]{1,0:T(8,128)(2,1)S(1)} %get-tuple-element.23), channel_id=1, source_target_pairs={{0,128},{128,0},{1,129},{129,1},{2,130},{130,2},{3,131},{131,3},{4... | collective-permute-start | bytes 2359304 | tf_op jit(solution)/shard_map/ppermute | solution.py:189
  130.7 7.5 %collective-permute-start.22 = (bf16[4,48,768]{2,1,0:T(8,128)(2,1)S(1)}, bf16[4,48,768]{2,1,0:T(8,128)(2,1)S(1)}, u32[]{:S(2)}, u32[]{:S(2)}) collective-permute-start(bf16[4,48,768]{2,1,0:T(8,128)(2,1)S(1)} %pad_maximum_fusion.3), channel_id=1, source_target_pairs={{0,8},{1,9},{2,10},{3,11},{4,12},{5,13},{6,14},{7,15},{8,0},{9,1},... | collective-permute-start | bytes 884744 | tf_op jit(solution)/shard_map/ppermute | solution.py:306
  131.8 12.6 %collective-permute-start.19 = (bf16[8,48,768]{2,1,0:T(8,128)(2,1)S(1)}, bf16[8,48,768]{2,1,0:T(8,128)(2,1)S(1)}, u32[]{:S(2)}, u32[]{:S(2)}) collective-permute-start(bf16[8,48,768]{2,1,0:T(8,128)(2,1)S(1)} %pad_maximum_fusion.lower0_ref), channel_id=1, source_target_pairs={{0,2},{1,3},{2,0},{3,1},{4,6},{5,7},{6,4},{7,5},{8,10},{9,11},{10,... | collective-permute-start | bytes 1769480 | tf_op jit(solution)/shard_map/ppermute | solution.py:306
  138.3 11.2 %collective-permute-start.23 = (bf16[8,48,768]{2,1,0:T(8,128)(2,1)S(1)}, bf16[8,48,768]{2,1,0:T(8,128)(2,1)S(1)}, u32[]{:S(2)}, u32[]{:S(2)}) collective-permute-start(bf16[8,48,768]{2,1,0:T(8,128)(2,1)S(1)} %pad_maximum_fusion.1.lower1_ref), channel_id=1, source_target_pairs={{0,56},{1,57},{2,58},{3,59},{4,60},{5,61},{6,62},{7,63},{8,16},{9,... | collective-permute-start | bytes 1769480 | tf_op jit(solution)/shard_map/ppermute | solution.py:306

commit v3 on v2

--- a/solution.py
+++ b/solution.py
@@ -16,7 +16,8 @@
 EPS_HEAD = 1e-06
 BF = jnp.bfloat16
 F32 = jnp.float32
-VMEM_LIMIT = 48 * 1024 * 1024
+VMEM_LIMIT = 20 * 1024 * 1024
+FULL_VMEM = 60 * 1024 * 1024
 
 
 def norm_rows(head, own_ref, oth_ref, normed_ref, rows):
@@ -164,7 +165,7 @@
         out[...] = jnp.dot(hot, mixed, preferred_element_type=F32).astype(BF)
 
 
-def call(kernel, place, grid, in_specs, out_specs, out_shape, scratch, flops, nbytes, args, alias=None):
+def call(kernel, place, grid, in_specs, out_specs, out_shape, scratch, flops, nbytes, args, alias=None, limit=VMEM_LIMIT):
     return pl.pallas_call(
         kernel,
         grid_spec=pltpu.PrefetchScalarGridSpec(
@@ -173,7 +174,7 @@
         out_shape=out_shape,
         input_output_aliases=alias or {},
         cost_estimate=pl.CostEstimate(flops=flops, bytes_accessed=nbytes, transcendentals=0),
-        compiler_params=pltpu.CompilerParams(vmem_limit_bytes=VMEM_LIMIT),
+        compiler_params=pltpu.CompilerParams(vmem_limit_bytes=limit),
     )(place, *args)
 
 
@@ -189,34 +190,27 @@
     return lax.ppermute(value, axis, [(0, 1), (1, 0)])
 
 
-def grad_kernel(mask_ref, turned_ref, cot_ref, send_ref, keep_ref):
+def grad_kernel(mask_ref, turned_ref, cot_ref, *out_refs):
     mask = mask_ref[0]
-    eight, piece, _ = send_ref.shape
-    top = mask >> 3
-    block = 4 * piece
-    for out, upper in ((send_ref, 1 - top), (keep_ref, top)):
-        for b in range(2):
-            first = pl.multiple_of(upper * eight * piece + b * block, piece)
-            got = jnp.dot(turned_ref[pl.ds(first, block), :], cot_ref[...], preferred_element_type=F32).astype(BF)
-            for i in range(4):
-                out[(b * 4 + i) ^ (mask & 7)] = got[i * piece : i * piece + piece]
-
-
-def place_kernel(mask_ref, lower0_ref, upper0_ref, lower1_ref, upper1_ref, out_ref, *, scale):
-    _, piece, width = lower0_ref.shape
-    for i in range(2):
-        rows = slice(i * piece, i * piece + piece)
-        for c, (lower, upper) in enumerate(((lower0_ref, upper0_ref), (lower1_ref, upper1_ref))):
-            at = (pl.program_id(0) * 2 + i) ^ mask_ref[c]
-            cols = slice(c * width, c * width + width)
-
-            @pl.when(at < 8)
+    _, piece, _ = out_refs[0].shape
+    for out, places in zip(out_refs, (3, 2, 1, 0)):
+        first = pl.multiple_of(((mask >> 2) ^ places) * (4 * piece), 4 * piece)
+        got = jnp.dot(turned_ref[pl.ds(first, 4 * piece), :], cot_ref[...], preferred_element_type=F32).astype(BF)
+        for i in range(4):
+            out[i ^ (mask & 3)] = got[i * piece : i * piece + piece]
+
+
+def place_kernel(mask_ref, *refs, scale, upper):
+    out_ref = refs[-1]
+    _, piece, _ = refs[0].shape
+    for c in range(2):
+        mask = mask_ref[c]
+        for places in range(2):
+
+            @pl.when((pl.program_id(0) == c) & ((pl.program_id(1) ^ ((mask >> 2) & 1)) == places))
             def _():
-                out_ref[rows, cols] = lower[at & 7].astype(F32) * scale
-
-            @pl.when(at >= 8)
-            def _():
-                out_ref[rows, cols] = upper[at & 7].astype(F32) * scale
+                for i in range(4):
+                    out_ref[i * piece : i * piece + piece, :] = refs[2 * c + places][i ^ (mask & 3)].astype(F32) * scale
 
 
 AXES = ("seq", "head", "z", "y", "xl")
@@ -269,18 +263,33 @@
     return pairs(sizes, partner)
 
 
-def last_tables(sizes):
+def quad_tables(sizes, chunk):
     n = dict(zip(AXES, sizes))
-    x = lambda at: at["seq"] * n["xl"] + at["xl"]
-    tables = []
-    for kind in (0, 1):
-        def partner(at, kind=kind):
-            to = across(x(at), kind, n["seq"] * n["xl"])
-            return {**at, "seq": to // n["xl"], "xl": to % n["xl"]}
-
-        tables.append(pairs(sizes, partner))
-    tables.append(pairs(sizes, lambda at: {**at, "z": (at["z"] + n["z"] // 2) % n["z"]}))
-    return tables
+
+    def partner(at, steps):
+        for step in steps:
+            axis, kind = ROUTES[chunk][at["head"]][step]
+            at = {**at, axis: across(at[axis], kind, n[axis])}
+        return at
+
+    return [pairs(sizes, lambda at, steps=steps: partner(at, steps)) for steps in ((3,), (2,), (2, 3))]
+
+
+def x_tables(sizes):
+    n = dict(zip(AXES, sizes))
+
+    def partner(at, kinds):
+        x = at["seq"] * n["xl"] + at["xl"]
+        for kind in kinds:
+            x = across(x, kind, n["seq"] * n["xl"])
+        return {**at, "seq": x // n["xl"], "xl": x % n["xl"]}
+
+    return [pairs(sizes, lambda at, kinds=kinds: partner(at, kinds)) for kinds in ((0,), (1,), (0, 1))]
+
+
+def z_table(sizes):
+    n = sizes[AXES.index("z")]
+    return pairs(sizes, lambda at: {**at, "z": (at["z"] + n // 2) % n})
 
 
 def mask_of(chunk, head):
@@ -293,8 +302,24 @@
     return jnp.where(head == 0, masks[0], masks[1])
 
 
-def add(a, b):
-    return (a.astype(F32) + b.astype(F32)).astype(BF)
+def add(*terms):
+    terms = [t.astype(F32) for t in terms]
+    while len(terms) > 1:
+        terms = [sum(terms[i + 1 : i + 2], terms[i]) for i in range(0, len(terms), 2)]
+    return terms[0].astype(BF)
+
+
+def place_call(masks, upper, scale, parts, shape, before=None):
+    _, piece, width = parts[0].shape
+    spec = pl.BlockSpec((4 * piece, width), lambda c, b, s: (2 * ((s[c] >> 3) ^ upper) + b, c))
+    held = pl.BlockSpec(parts[0].shape, lambda c, b, s: (0, 0, 0))
+    args, specs, alias = list(parts), [held] * 4, None
+    if before is not None:
+        args, specs, alias = args + [before], specs + [pl.BlockSpec(memory_space=pl.ANY)], {5: 0}
+    return call(
+        functools.partial(place_kernel, scale=scale, upper=upper), masks, (2, 2), specs, spec,
+        jax.ShapeDtypeStruct(shape, F32), [], 10**6, 4 * 10**6, args, alias,
+    )
 
 
 def reduce_grad(turned, cot, scale, head):
@@ -302,40 +327,40 @@
     sizes = tuple(lax.axis_size(a) for a in AXES)
     masks = [mask_of(c, head) for c in range(2)]
     piece = share // 16
-    half = jax.ShapeDtypeStruct((8, piece, width // 2), BF)
+    four = jax.ShapeDtypeStruct((4, piece, width // 2), BF)
     move = lambda value, table: lax.ppermute(value, AXES, table)
+    tables = [[pair_table(sizes, c, stage) for stage in range(2)] for c in range(2)]
+    quads = [quad_tables(sizes, c) for c in range(2)]
     held = []
     for c in range(2):
-        held.append(list(call(
+        held.append(call(
             grad_kernel, masks[c][None], (1,),
             [whole(turned.shape), pl.BlockSpec((cot.shape[0], width // 2), lambda g, s, c=c: (0, c))],
-            [whole(half.shape)] * 2, [half] * 2, [], 6 * 10**8, 4 * 10**6, (turned, cot),
-        )))
-    for stage in range(4):
-        for c in range(2):
-            send, keep = held[c]
-            got = move(send, pair_table(sizes, c, stage))
-            n = keep.shape[0] // 2
-            if n:
-                held[c] = [add(keep[n:], got[n:]), add(keep[:n], got[:n])]
-            else:
-                held[c] = add(keep, got)
-    both = jnp.concatenate(held, axis=0)
-    for table in last_tables(sizes):
-        both = add(both, move(both, table))
-    lower = [both[0:1], both[1:2]]
-    upper = [None, None]
-    for stage in (3, 2, 1, 0):
-        for c in range(2):
-            if upper[c] is not None:
-                lower[c] = jnp.concatenate([lower[c], upper[c]], axis=0)
-            upper[c] = move(lower[c], pair_table(sizes, c, stage))
-    return call(
-        functools.partial(place_kernel, scale=scale), jnp.stack(masks), (8,),
-        [whole(half.shape)] * 4, pl.BlockSpec((2 * piece, width), lambda g, s: (g, 0)),
-        jax.ShapeDtypeStruct((share, width), F32), [], 10**6, 7 * 10**6,
-        (lower[0], upper[0], lower[1], upper[1]),
-    )
+            [whole(four.shape)] * 4, [four] * 4, [], 6 * 10**8, 4 * 10**6, (turned, cot),
+        ))
+    own = []
+    for c in range(2):
+        last, third, second, first = held[c]
+        got_last = move(last, tables[c][0])
+        got_third = move(third, tables[c][0])
+        got = move(add(second, got_last), tables[c][1])
+        at = lambda i: (first[i : i + 1], got_third[i : i + 1], got[i : i + 1])
+        away = [move(add(*at(i)), quads[c][i - 1]) for i in (1, 2, 3)]
+        own.append(add(add(*at(0)), *away))
+    both = jnp.concatenate(own, axis=0)
+    near, over, far = [move(both, table) for table in x_tables(sizes)]
+    both = add(both, near, over, far)
+    both = add(both, move(both, z_table(sizes)))
+    lower, upper = [], []
+    for c in range(2):
+        mine = both[c : c + 1]
+        four = jnp.concatenate([mine] + [move(mine, table) for table in quads[c]], axis=0)
+        next_four = move(four, tables[c][1])
+        lower += [four, next_four]
+        upper += [move(four, tables[c][0]), move(next_four, tables[c][0])]
+    masks = jnp.stack(masks)
+    out = place_call(masks, 0, scale, lower, (share, width))
+    return place_call(masks, 1, scale, upper, (share, width), out)
 
 
 def body(tokens, lengths, owner_slot, latent_index, cotangent, qkv_weight, out_weight):
@@ -369,7 +394,7 @@
          pl.BlockSpec((3, 2 * share, GROUP), lambda g, s: (0, 0, g))],
         [columns(rows, GROUP), columns(rows, 2 * GROUP)],
         [jax.ShapeDtypeStruct((rows, share), BF), jax.ShapeDtypeStruct((rows, 2 * share), F32)],
-        scratch(rows, rows, rows), 7 * 10**9, 12 * 10**6, (bounds, own, oth, qkv_weight),
+        scratch(rows, rows, rows), 7 * 10**9, 12 * 10**6, (bounds, own, oth, qkv_weight), limit=FULL_VMEM,
     )
     foreign_own, q = lax.optimization_barrier((foreign_own, q))
     foreign_oth = swap(foreign_own, "head")
@@ -381,7 +406,7 @@
         [jax.ShapeDtypeStruct((rows, share), BF), jax.ShapeDtypeStruct((share, rows), BF)],
         scratch(rows, rows, rows)
         + [pltpu.VMEM((rows, GROUP), BF), pltpu.VMEM((rows, GROUP), BF), pltpu.VMEM((rows, 2 * GROUP), F32)],
-        4 * 10**9, 14 * 10**6, (bounds, foreign_own, foreign_oth, qkv_weight, qkv_weight, q, acc),
+        4 * 10**9, 14 * 10**6, (bounds, foreign_own, foreign_oth, qkv_weight, qkv_weight, q, acc), limit=FULL_VMEM,
     )
     count = 2 * rows * lax.axis_size("z") * lax.axis_size("y") * lax.axis_size("xl")
     grad_out = reduce_grad(turned, cotangent[0], count ** (-0.5), head)

time: 154 us -> 143 us (0.929)
  waiting for transfers between devices: 42 us -> 21.5 us
  Pallas kernels: 45.7 us -> 50.4 us
  starting transfers between devices: 44.8 us -> 48.9 us
    ppermute x19 -> x28, waiting for transfers between devices: 37.7 us -> 19.6 us  [reduce_grad(): move = lambda value, table: lax.ppermute(value, AXES, table)]
    pallas_call x7 -> x8, Pallas kernels: 45.7 us -> 50.4 us  [call(): pl.pallas_call(kernel, grid_spec=pltpu.PrefetchScalarGridSpec(num_scalar_...]
    ppermute x19 -> x28, starting transfers between devices: 39.8 us -> 44.3 us  [reduce_grad(): move = lambda value, table: lax.ppermute(value, AXES, table)]
    convert_element_type x11 -> x8, other arithmetic: 4.89 us -> 8.23 us  [add(): return terms[0].astype(BF)]
    concatenate x7 -> x3, other arithmetic: 2.71 us -> 0.1 us  [the longest x2 0.08 us: reduce_grad(): jnp.concatenate([mine] + [move(mine, table) for table in quads[c]], axis=0)]
    ppermute x5, waiting for transfers between devices: 4.33 us -> 1.95 us  [swap(): return lax.ppermute(value, axis, [(0, 1), (1, 0)])]
    unnamed x30 -> x42, local copies, waits for them, and re-layouts: 9.79 us -> 8.29 us
  transfers between devices with their start and end apart: 24 -> 33, of which waited for: 16 -> 11; matrix products, arithmetic and copies ran while one was open for 6% -> 10% of each run, Pallas kernels for 17% -> 21%
where the time goes in v3:
time: 143 us
  Pallas kernels  50.4 us (35%)
  starting transfers between devices  48.9 us (34%)
  waiting for transfers between devices  21.5 us (15%)
  other arithmetic  11.8 us (8%)
  local copies, waits for them, and re-layouts  9.09 us (6%)
    pallas_call x8, Pallas kernels, call(): pl.pallas_call(kernel, grid_spec=pltpu.PrefetchScalarGridSpec(num_scalar_...  50.4 us
    ppermute x28, starting transfers between devices, reduce_grad(): move = lambda value, table: lax.ppermute(value, AXES, table)  44.3 us
    ppermute x28, waiting for transfers between devices, reduce_grad(): move = lambda value, table: lax.ppermute(value, AXES, table)  19.6 us
    unnamed x42, local copies, waits for them, and re-layouts  8.29 us
    convert_element_type x8, other arithmetic, add(): return terms[0].astype(BF)  8.23 us
    ppermute x5, starting transfers between devices, swap(): return lax.ppermute(value, axis, [(0, 1), (1, 0)])  4.66 us
  transfers between devices with their start and end apart: 33, of which 11 were waited for; matrix products, arithmetic and copies ran while one was open for 10% of the time, Pallas kernels for 21%

profile of v3, /device:TPU:2, one launch (start us, length us, event | category | flops | bytes accessed | tf_op | source)
XLA Modules:
  0.0 142.6 jit_solution(12241227510977470170)
XLA Ops:
  0.7 2.2 %collective-permute-start = (bf16[512,768]{1,0:T(8,128)(2,1)}, bf16[512,768]{1,0:T(8,128)(2,1)S(1)}, u32[]{:S(2)}, u32[]{:S(2)}) collective-permute-start(bf16[512,768]{1,0:T(8,128)(2,1)} %bitcast.36), channel_id=1, source_target_pairs={{0,128},{128,0},{1,129},{129,1},{2,130},{130,2},{3,131},{131,3},{4... | collective-permute-start | bytes 2359304 | tf_op jit(solution)/shard_map/ppermute | solution.py:190
  6.8 18.0 %shard_map.94 = (bf16[512,768]{1,0:T(8,128)(2,1)}, f32[512,1536]{1,0:T(8,128)}) custom-call(s32[2]{0:T(128)} %pad_add_fusion.1.place_ref, s32[8,128]{1,0:T(8,128)} %pad.13.bounds_ref, bf16[512,768]{1,0:T(8,128)(2,1)} %bitcast.37, bf16[512,768]{1,0:T(8,128)(2,1)} %copy-done.18, bf16[3,1536,768]{2,1,0:T(8,128)(2,1)} %wv_ref.1), custom_call_target="tpu_custom_call" | custom-call | flops 7000000000 | bytes 12000000 | tf_op jit(solution)/shard_map/pallas_call | solution.py:169
  25.2 1.9 %collective-permute-done.2.oth_ref = bf16[512,768]{1,0:T(8,128)(2,1)S(1)} collective-permute-done((bf16[512,768]{1,0:T(8,128)(2,1)S(1)}, bf16[512,768]{1,0:T(8,128)(2,1)S(1)}, u32[]{:S(2)}, u32[]{:S(2)}) %collective-permute-start.2) | collective-permute-done | bytes 786464 | tf_op jit(solution)/shard_map/ppermute | solution.py:190
  28.0 17.0 %shard_map.95 = (bf16[512,768]{1,0:T(8,128)(2,1)}, bf16[768,512]{1,0:T(8,128)(2,1)}) custom-call(s32[2]{0:T(128)} %pad_add_fusion.1.place_ref, s32[8,128]{1,0:T(8,128)} %pad.13.bounds_ref, bf16[512,768]{1,0:T(8,128)(2,1)} %copy-done.14, bf16[512,768]{1,0:T(8,128)(2,1)} %copy-done.15, bf16[3,1536,768]{2,1,0:T(8,128)(2,1)} %wv_ref.1, ...), custom_call_target="tpu_custom_call" | custom-call | flops 4000000000 | bytes 14000000 | tf_op jit(solution)/shard_map/pallas_call | solution.py:169
  45.1 1.1 copy-done.1
  46.2 1.2 shard_map.98
  47.4 1.6 %collective-permute-start.6 = (bf16[4,48,768]{2,1,0:T(8,128)(2,1)}, bf16[4,48,768]{2,1,0:T(8,128)(2,1)}, u32[]{:S(2)}, u32[]{:S(2)}) collective-permute-start(bf16[4,48,768]{2,1,0:T(8,128)(2,1)} %get-tuple-element.32), channel_id=1, source_target_pairs={{0,2},{1,3},{2,0},{3,1},{4,6},{5,7},{6,4},{7,5},{8,10},{9,11},{10,... | collective-permute-start | bytes 884744 | tf_op jit(solution)/shard_map/ppermute | solution.py:331
  49.0 1.2 shard_map.99
  52.4 5.9 %collective-permute-start.12 = (bf16[4,48,768]{2,1,0:T(8,128)(2,1)}, bf16[4,48,768]{2,1,0:T(8,128)(2,1)}, u32[]{:S(2)}, u32[]{:S(2)}) collective-permute-start(bf16[4,48,768]{2,1,0:T(8,128)(2,1)} %get-tuple-element.36), channel_id=1, source_target_pairs={{0,56},{1,57},{2,58},{3,59},{4,60},{5,61},{6,62},{7,63},{8,16},{9,... | collective-permute-start | bytes 884744 | tf_op jit(solution)/shard_map/ppermute | solution.py:331
  58.4 1.0 collective-permute-start.5
  59.4 1.8 %add_convert_fusion.1 = bf16[4,48,768]{2,1,0:T(8,128)(2,1)} fusion(bf16[4,48,768]{2,1,0:T(8,128)(2,1)} %collective-permute-done.6, bf16[4,48,768]{2,1,0:T(8,128)(2,1)} %copy-done.10), kind=kLoop, calls=%fused_computation.2 | loop fusion | flops 589824 | bytes 884736 | tf_op jit(solution)/shard_map/convert_element_type | solution.py:309
  61.2 2.6 %collective-permute-start.7 = (bf16[4,48,768]{2,1,0:T(8,128)(2,1)}, bf16[4,48,768]{2,1,0:T(8,128)(2,1)}, u32[]{:S(2)}, u32[]{:S(2)}) collective-permute-start(bf16[4,48,768]{2,1,0:T(8,128)(2,1)} %add_convert_fusion.1), channel_id=1, source_target_pairs={{0,6},{1,7},{2,4},{3,5},{4,2},{5,3},{6,0},{7,1},{8,14},{9,15},{10,... | collective-permute-start | bytes 884744 | tf_op jit(solution)/shard_map/ppermute | solution.py:331
  63.8 1.8 %add_convert_fusion = bf16[4,48,768]{2,1,0:T(8,128)(2,1)} fusion(bf16[4,48,768]{2,1,0:T(8,128)(2,1)} %collective-permute-done.12, bf16[4,48,768]{2,1,0:T(8,128)(2,1)} %copy-done.9), kind=kLoop, calls=%fused_computation.1 | loop fusion | flops 589824 | bytes 884736 | tf_op jit(solution)/shard_map/convert_element_type | solution.py:309
  65.6 1.1 copy-done.3
  66.8 2.8 %shard_map.96 = bf16[512,768]{1,0:T(8,128)(2,1)} custom-call(s32[2]{0:T(128)S(1)} %copy-done.11, bf16[512,768]{1,0:T(8,128)(2,1)S(1)} %copy-done.3, bf16[768,1536]{1,0:T(8,128)(2,1)S(1)} %copy-done.2), custom_call_target="tpu_custom_call" | custom-call | flops 600000000 | bytes 3000000 | tf_op jit(solution)/shard_map/pallas_call | solution.py:169
  69.6 1.3 add_convert_fusion.12
  70.8 2.6 %collective-permute-start.10 = (bf16[1,48,768]{2,1,0:T(8,128)(2,1)S(1)}, bf16[1,48,768]{2,1,0:T(8,128)(2,1)S(1)}, u32[]{:S(2)}, u32[]{:S(2)}) collective-permute-start(bf16[1,48,768]{2,1,0:T(8,128)(2,1)S(1)} %get-tuple-element.38), channel_id=1, source_target_pairs={{0,16},{1,17},{2,18},{3,19},{4,20},{5,21},{6,22},{7,23},{8,56},{9,... | collective-permute-start | bytes 221192 | tf_op jit(solution)/shard_map/ppermute | solution.py:331
  73.5 3.1 %collective-permute-start.8 = (bf16[1,48,768]{2,1,0:T(8,128)(2,1)S(1)}, bf16[1,48,768]{2,1,0:T(8,128)(2,1)S(1)}, u32[]{:S(2)}, u32[]{:S(2)}) collective-permute-start(bf16[1,48,768]{2,1,0:T(8,128)(2,1)S(1)} %get-tuple-element.37), channel_id=1, source_target_pairs={{0,56},{1,57},{2,58},{3,59},{4,60},{5,61},{6,62},{7,63},{8,16},{9,... | collective-permute-start | bytes 221192 | tf_op jit(solution)/shard_map/ppermute | solution.py:331
  76.6 1.2 add_convert_fusion.7
  78.3 2.7 %collective-permute-start.15 = (bf16[1,48,768]{2,1,0:T(8,128)(2,1)S(1)}, bf16[1,48,768]{2,1,0:T(8,128)(2,1)S(1)}, u32[]{:S(2)}, u32[]{:S(2)}) collective-permute-start(bf16[1,48,768]{2,1,0:T(8,128)(2,1)S(1)} %get-tuple-element.42), channel_id=1, source_target_pairs={{0,6},{1,7},{2,4},{3,5},{4,2},{5,3},{6,0},{7,1},{8,14},{9,15},{10,... | collective-permute-start | bytes 221192 | tf_op jit(solution)/shard_map/ppermute | solution.py:331
  80.9 1.0 collective-permute-start.16
  82.0 1.0 add_convert_fusion.9
  83.8 3.0 %collective-permute-done.16 = bf16[1,48,768]{2,1,0:T(8,128)(2,1)S(1)} collective-permute-done((bf16[1,48,768]{2,1,0:T(8,128)(2,1)S(1)}, bf16[1,48,768]{2,1,0:T(8,128)(2,1)S(1)}, u32[]{:S(2)}, u32[]{:S(2)}) %collective-permute-start.16) | collective-permute-done | bytes 73760 | tf_op jit(solution)/shard_map/ppermute | solution.py:331
  86.8 1.0 add_convert_fusion.4
  87.8 1.5 %collective-permute-start.17 = (bf16[2,48,768]{2,1,0:T(8,128)(2,1)S(1)}, bf16[2,48,768]{2,1,0:T(8,128)(2,1)S(1)}, u32[]{:S(2)}, u32[]{:S(2)}) collective-permute-start(bf16[2,48,768]{2,1,0:T(8,128)(2,1)S(1)} %pad_maximum_fusion.2), channel_id=1, source_target_pairs={{0,1},{1,0},{2,3},{3,2},{4,5},{5,4},{6,7},{7,6},{8,9},{9,8},{10,11... | collective-permute-start | bytes 442376 | tf_op jit(solution)/shard_map/ppermute | solution.py:331
  89.9 2.1 %collective-permute-start.19 = (bf16[2,48,768]{2,1,0:T(8,128)(2,1)S(1)}, bf16[2,48,768]{2,1,0:T(8,128)(2,1)S(1)}, u32[]{:S(2)}, u32[]{:S(2)}) collective-permute-start(bf16[2,48,768]{2,1,0:T(8,128)(2,1)S(1)} %pad_maximum_fusion.2), channel_id=1, source_target_pairs={{0,128},{1,129},{2,130},{3,131},{4,132},{5,133},{6,134},{7,135},{8... | collective-permute-start | bytes 442376 | tf_op jit(solution)/shard_map/ppermute | solution.py:331
  92.0 1.9 %collective-permute-done.17 = bf16[2,48,768]{2,1,0:T(8,128)(2,1)S(1)} collective-permute-done((bf16[2,48,768]{2,1,0:T(8,128)(2,1)S(1)}, bf16[2,48,768]{2,1,0:T(8,128)(2,1)S(1)}, u32[]{:S(2)}, u32[]{:S(2)}) %collective-permute-start.17) | collective-permute-done | bytes 147488 | tf_op jit(solution)/shard_map/ppermute | solution.py:331
  93.9 1.0 collective-permute-done.18
  94.9 1.6 %collective-permute-done.19 = bf16[2,48,768]{2,1,0:T(8,128)(2,1)S(1)} collective-permute-done((bf16[2,48,768]{2,1,0:T(8,128)(2,1)S(1)}, bf16[2,48,768]{2,1,0:T(8,128)(2,1)S(1)}, u32[]{:S(2)}, u32[]{:S(2)}) %collective-permute-start.19) | collective-permute-done | bytes 147488 | tf_op jit(solution)/shard_map/ppermute | solution.py:331
  96.6 3.5 %collective-permute-start.20 = (bf16[2,48,768]{2,1,0:T(8,128)(2,1)S(1)}, bf16[2,48,768]{2,1,0:T(8,128)(2,1)S(1)}, u32[]{:S(2)}, u32[]{:S(2)}) collective-permute-start(bf16[2,48,768]{2,1,0:T(8,128)(2,1)S(1)} %add_convert_fusion.3), channel_id=1, source_target_pairs={{0,32},{1,33},{2,34},{3,35},{4,36},{5,37},{6,38},{7,39},{8,40},{9,... | collective-permute-start | bytes 442376 | tf_op jit(solution)/shard_map/ppermute | solution.py:331
  100.2 1.0 copy.14
  101.2 1.0 copy-done.5
  102.2 5.1 %shard_map.97 = (bf16[512,768]{1,0:T(8,128)(2,1)}, bf16[512,768]{1,0:T(8,128)(2,1)S(1)}, bf16[512,768]{1,0:T(8,128)(2,1)S(1)}) custom-call(s32[2]{0:T(128)S(1)} %copy-done.11, bf16[512,768]{1,0:T(8,128)(2,1)S(1)} %copy-done.4, bf16[768,1536]{1,0:T(8,128)(2,1)S(1)} %copy-done.2, bf16[512,768]{1,0:T(8,128)(2,1)} %collective-permute-done.3.recv_ref, ...), custom_call_target="tpu_custom_call" | custom-call | flops 1400000000 | bytes 6000000 | tf_op jit(solution)/shard_map/pallas_call | solution.py:169
  107.4 2.1 %collective-permute-start.4 = (bf16[512,768]{1,0:T(8,128)(2,1)S(1)}, bf16[512,768]{1,0:T(8,128)(2,1)S(1)}, u32[]{:S(2)}, u32[]{:S(2)}) collective-permute-start(bf16[512,768]{1,0:T(8,128)(2,1)S(1)} %get-tuple-element.27), channel_id=1, source_target_pairs={{0,128},{128,0},{1,129},{129,1},{2,130},{130,2},{3,131},{131,3},{4... | collective-permute-start | bytes 2359304 | tf_op jit(solution)/shard_map/ppermute | solution.py:190
  109.7 2.2 %collective-permute-start.28 = (bf16[1,48,768]{2,1,0:T(8,128)(2,1)S(1)}, bf16[1,48,768]{2,1,0:T(8,128)(2,1)S(1)}, u32[]{:S(2)}, u32[]{:S(2)}) collective-permute-start(bf16[1,48,768]{2,1,0:T(8,128)(2,1)S(1)} %get-tuple-element.43), channel_id=1, source_target_pairs={{0,6},{1,7},{2,4},{3,5},{4,2},{5,3},{6,0},{7,1},{8,14},{9,15},{10,... | collective-permute-start | bytes 221192 | tf_op jit(solution)/shard_map/ppermute | solution.py:331
  111.9 1.9 %collective-permute-start.29 = (bf16[1,48,768]{2,1,0:T(8,128)(2,1)S(1)}, bf16[1,48,768]{2,1,0:T(8,128)(2,1)S(1)}, u32[]{:S(2)}, u32[]{:S(2)}) collective-permute-start(bf16[1,48,768]{2,1,0:T(8,128)(2,1)S(1)} %get-tuple-element.43), channel_id=1, source_target_pairs={{0,4},{1,5},{2,6},{3,7},{4,0},{5,1},{6,2},{7,3},{8,12},{9,13},{10,... | collective-permute-start | bytes 221192 | tf_op jit(solution)/shard_map/ppermute | solution.py:331
  113.7 1.2 collective-permute-start.21
  114.9 1.0 collective-permute-start.22
  115.9 1.5 %collective-permute-start.23 = (bf16[1,48,768]{2,1,0:T(8,128)(2,1)S(1)}, bf16[1,48,768]{2,1,0:T(8,128)(2,1)S(1)}, u32[]{:S(2)}, u32[]{:S(2)}) collective-permute-start(bf16[1,48,768]{2,1,0:T(8,128)(2,1)S(1)} %get-tuple-element.44), channel_id=1, source_target_pairs={{0,16},{1,17},{2,18},{3,19},{4,20},{5,21},{6,22},{7,23},{8,56},{9,... | collective-permute-start | bytes 221192 | tf_op jit(solution)/shard_map/ppermute | solution.py:331
  118.0 1.6 %collective-permute-start.31 = (bf16[4,48,768]{2,1,0:T(8,128)(2,1)S(1)}, bf16[4,48,768]{2,1,0:T(8,128)(2,1)S(1)}, u32[]{:S(2)}, u32[]{:S(2)}) collective-permute-start(bf16[4,48,768]{2,1,0:T(8,128)(2,1)S(1)} %pad_maximum_fusion.1.refs_2_), channel_id=1, source_target_pairs={{0,8},{1,9},{2,10},{3,11},{4,12},{5,13},{6,14},{7,15},{8,0},{9,1},... | collective-permute-start | bytes 884744 | tf_op jit(solution)/shard_map/ppermute | solution.py:331
  119.5 2.9 %collective-permute-done.23 = bf16[1,48,768]{2,1,0:T(8,128)(2,1)S(1)} collective-permute-done((bf16[1,48,768]{2,1,0:T(8,128)(2,1)S(1)}, bf16[1,48,768]{2,1,0:T(8,128)(2,1)S(1)}, u32[]{:S(2)}, u32[]{:S(2)}) %collective-permute-start.23) | collective-permute-done | bytes 73760 | tf_op jit(solution)/shard_map/ppermute | solution.py:331
  122.4 1.8 %collective-permute-start.25 = (bf16[4,48,768]{2,1,0:T(8,128)(2,1)S(1)}, bf16[4,48,768]{2,1,0:T(8,128)(2,1)S(1)}, u32[]{:S(2)}, u32[]{:S(2)}) collective-permute-start(bf16[4,48,768]{2,1,0:T(8,128)(2,1)S(1)} %pad_maximum_fusion.refs_0_), channel_id=1, source_target_pairs={{0,6},{1,7},{2,4},{3,5},{4,2},{5,3},{6,0},{7,1},{8,14},{9,15},{10,... | collective-permute-start | bytes 884744 | tf_op jit(solution)/shard_map/ppermute | solution.py:331
  124.2 1.6 %collective-permute-start.30 = (bf16[4,48,768]{2,1,0:T(8,128)(2,1)S(1)}, bf16[4,48,768]{2,1,0:T(8,128)(2,1)S(1)}, u32[]{:S(2)}, u32[]{:S(2)}) collective-permute-start(bf16[4,48,768]{2,1,0:T(8,128)(2,1)S(1)} %pad_maximum_fusion.1.refs_2_), channel_id=1, source_target_pairs={{0,56},{1,57},{2,58},{3,59},{4,60},{5,61},{6,62},{7,63},{8,16},{9,... | collective-permute-start | bytes 884744 | tf_op jit(solution)/shard_map/ppermute | solution.py:331
  126.4 2.8 %collective-permute-start.32 = (bf16[4,48,768]{2,1,0:T(8,128)(2,1)S(1)}, bf16[4,48,768]{2,1,0:T(8,128)(2,1)S(1)}, u32[]{:S(2)}, u32[]{:S(2)}) collective-permute-start(bf16[4,48,768]{2,1,0:T(8,128)(2,1)S(1)} %collective-permute-done.31.refs_3_), channel_id=1, source_target_pairs={{0,56},{1,57},{2,58},{3,59},{4,60},{5,61},{6,62},{7,63},{8,16},{9,... | collective-permute-start | bytes 884744 | tf_op jit(solution)/shard_map/ppermute | solution.py:331
  129.2 4.1 %collective-permute-done.25.refs_1_ = bf16[4,48,768]{2,1,0:T(8,128)(2,1)S(1)} collective-permute-done((bf16[4,48,768]{2,1,0:T(8,128)(2,1)S(1)}, bf16[4,48,768]{2,1,0:T(8,128)(2,1)S(1)}, u32[]{:S(2)}, u32[]{:S(2)}) %collective-permute-start.25) | collective-permute-done | bytes 294944 | tf_op jit(solution)/shard_map/ppermute | solution.py:331
  133.4 2.5 %shard_map.100.refs_4_ = f32[768,1536]{1,0:T(8,128)} custom-call(s32[2]{0:T(128)S(1)} %pad_add_fusion.2.mask_ref, bf16[4,48,768]{2,1,0:T(8,128)(2,1)S(1)} %pad_maximum_fusion.refs_0_, bf16[4,48,768]{2,1,0:T(8,128)(2,1)S(1)} %collective-permute-done.25.refs_1_, bf16[4,48,768]{2,1,0:T(8,128)(2,1)S(1)} %pad_maximum_fusion.1.refs_2_, ...), custom_call_target="tpu_custom_call" | custom-call | flops 1000000 | bytes 4000000 | tf_op jit(solution)/shard_map/pallas_call | solution.py:169
  136.9 3.1 %collective-permute-done.26.refs_1_ = bf16[4,48,768]{2,1,0:T(8,128)(2,1)S(1)} collective-permute-done((bf16[4,48,768]{2,1,0:T(8,128)(2,1)S(1)}, bf16[4,48,768]{2,1,0:T(8,128)(2,1)S(1)}, u32[]{:S(2)}, u32[]{:S(2)}) %collective-permute-start.26) | collective-permute-done | bytes 294944 | tf_op jit(solution)/shard_map/ppermute | solution.py:331
  140.1 2.5 %shard_map.101 = f32[768,1536]{1,0:T(8,128)} custom-call(s32[2]{0:T(128)S(1)} %pad_add_fusion.2.mask_ref, bf16[4,48,768]{2,1,0:T(8,128)(2,1)S(1)} %collective-permute-done.24.refs_0_, bf16[4,48,768]{2,1,0:T(8,128)(2,1)S(1)} %collective-permute-done.26.refs_1_, ...), custom_call_target="tpu_custom_call", output_to_operand_aliasing={{}: (5, {})} | custom-call | flops 1000000 | bytes 4000000 | tf_op jit(solution)/shard_map/pallas_call | solution.py:169
  (100 shorter events, 12.0 us)
Async XLA Ops:
  0.6 5.3 %collective-permute-start.1 = (bf16[512,768]{1,0:T(8,128)(2,1)}, bf16[512,768]{1,0:T(8,128)(2,1)S(1)}, u32[]{:S(2)}, u32[]{:S(2)}) collective-permute-start(bf16[512,768]{1,0:T(8,128)(2,1)} %bitcast.35), channel_id=1, source_target_pairs={{0,64},{64,0},{1,65},{65,1},{2,66},{66,2},{3,67},{67,3},{4,68},{68... | collective-permute-start | bytes 2359304 | tf_op jit(solution)/shard_map/ppermute | solution.py:190
  0.7 24.0 %collective-permute-start = (bf16[512,768]{1,0:T(8,128)(2,1)}, bf16[512,768]{1,0:T(8,128)(2,1)S(1)}, u32[]{:S(2)}, u32[]{:S(2)}) collective-permute-start(bf16[512,768]{1,0:T(8,128)(2,1)} %bitcast.36), channel_id=1, source_target_pairs={{0,128},{128,0},{1,129},{129,1},{2,130},{130,2},{3,131},{131,3},{4... | collective-permute-start | bytes 2359304 | tf_op jit(solution)/shard_map/ppermute | solution.py:190
  5.9 19.1 %copy-start.17 = (s32[1,8]{1,0:T(1,128)S(1)}, s32[1,8]{1,0:T(1,128)}, u32[]{:S(2)}) copy-start(s32[1,8]{1,0:T(1,128)} %param.8) | copy-start | bytes 100
  5.9 19.1 %copy-start.16 = (s32[1,8,128]{2,1,0:T(8,128)S(1)}, s32[1,8,128]{2,1,0:T(8,128)}, u32[]{:S(2)}) copy-start(s32[1,8,128]{2,1,0:T(8,128)} %param.10) | copy-start | bytes 12292
  24.8 2.4 %copy-start.14 = (bf16[512,768]{1,0:T(8,128)(2,1)}, bf16[512,768]{1,0:T(8,128)(2,1)S(1)}, u32[]{:S(2)}) copy-start(bf16[512,768]{1,0:T(8,128)(2,1)S(1)} %collective-permute-done.own_ref) | copy-start | bytes 2359300
  24.8 2.4 %collective-permute-start.2 = (bf16[512,768]{1,0:T(8,128)(2,1)S(1)}, bf16[512,768]{1,0:T(8,128)(2,1)S(1)}, u32[]{:S(2)}, u32[]{:S(2)}) collective-permute-start(bf16[512,768]{1,0:T(8,128)(2,1)S(1)} %collective-permute-done.own_ref), channel_id=1, source_target_pairs={{0,64},{64,0},{1,65},{65,1},{2,66},{66,2},{3,67},{67,3},{4,68},{68... | collective-permute-start | bytes 2359304 | tf_op jit(solution)/shard_map/ppermute | solution.py:190
  28.0 17.0 %copy-start = (bf16[1,512,1536]{2,1,0:T(8,128)(2,1)S(1)}, bf16[1,512,1536]{2,1,0:T(8,128)(2,1)}, u32[]{:S(2)}) copy-start(bf16[1,512,1536]{2,1,0:T(8,128)(2,1)} %param.11) | copy-start | bytes 4718596
  28.0 21.0 %copy-start.19 = (s32[1,8]{1,0:T(1,128)S(1)}, s32[1,8]{1,0:T(1,128)}, u32[]{:S(2)}) copy-start(s32[1,8]{1,0:T(1,128)} %param.9) | copy-start | bytes 100
  28.0 37.6 %copy-start.2 = (bf16[768,1536]{1,0:T(8,128)(2,1)S(1)}, bf16[768,1536]{1,0:T(8,128)(2,1)}, u32[]{:S(2)}) copy-start(bf16[768,1536]{1,0:T(8,128)(2,1)} %w_ref.5) | copy-start | bytes 7077892
  45.0 20.6 %copy-start.11 = (s32[2]{0:T(128)S(1)}, s32[2]{0:T(128)}, u32[]{:S(2)}) copy-start(s32[2]{0:T(128)} %pad_add_fusion.1.place_ref) | copy-start | bytes 28
  45.1 1.1 copy-start.1
  47.4 1.6 %copy-start.8 = (bf16[4,48,768]{2,1,0:T(8,128)(2,1)}, bf16[4,48,768]{2,1,0:T(8,128)(2,1)S(1)}, u32[]{:S(2)}) copy-start(bf16[4,48,768]{2,1,0:T(8,128)(2,1)S(1)} %get-tuple-element.29) | copy-start | bytes 884740
  47.4 1.6 %copy-start.10 = (bf16[4,48,768]{2,1,0:T(8,128)(2,1)}, bf16[4,48,768]{2,1,0:T(8,128)(2,1)S(1)}, u32[]{:S(2)}) copy-start(bf16[4,48,768]{2,1,0:T(8,128)(2,1)S(1)} %get-tuple-element.31) | copy-start | bytes 884740
  47.4 1.6 %copy-start.13 = (bf16[4,48,768]{2,1,0:T(8,128)(2,1)}, bf16[4,48,768]{2,1,0:T(8,128)(2,1)S(1)}, u32[]{:S(2)}) copy-start(bf16[4,48,768]{2,1,0:T(8,128)(2,1)S(1)} %get-tuple-element.30) | copy-start | bytes 884740
  47.4 11.9 %collective-permute-start.6 = (bf16[4,48,768]{2,1,0:T(8,128)(2,1)}, bf16[4,48,768]{2,1,0:T(8,128)(2,1)}, u32[]{:S(2)}, u32[]{:S(2)}) collective-permute-start(bf16[4,48,768]{2,1,0:T(8,128)(2,1)} %get-tuple-element.32), channel_id=1, source_target_pairs={{0,2},{1,3},{2,0},{3,1},{4,6},{5,7},{6,4},{7,5},{8,10},{9,11},{10,... | collective-permute-start | bytes 884744 | tf_op jit(solution)/shard_map/ppermute | solution.py:331
  52.4 11.4 %collective-permute-start.12 = (bf16[4,48,768]{2,1,0:T(8,128)(2,1)}, bf16[4,48,768]{2,1,0:T(8,128)(2,1)}, u32[]{:S(2)}, u32[]{:S(2)}) collective-permute-start(bf16[4,48,768]{2,1,0:T(8,128)(2,1)} %get-tuple-element.36), channel_id=1, source_target_pairs={{0,56},{1,57},{2,58},{3,59},{4,60},{5,61},{6,62},{7,63},{8,16},{9,... | collective-permute-start | bytes 884744 | tf_op jit(solution)/shard_map/ppermute | solution.py:331
  58.4 11.2 %collective-permute-start.5 = (bf16[4,48,768]{2,1,0:T(8,128)(2,1)}, bf16[4,48,768]{2,1,0:T(8,128)(2,1)}, u32[]{:S(2)}, u32[]{:S(2)}) collective-permute-start(bf16[4,48,768]{2,1,0:T(8,128)(2,1)} %copy-done.13), channel_id=1, source_target_pairs={{0,2},{1,3},{2,0},{3,1},{4,6},{5,7},{6,4},{7,5},{8,10},{9,11},{10,... | collective-permute-start | bytes 884744 | tf_op jit(solution)/shard_map/ppermute | solution.py:331
  59.3 17.3 %collective-permute-start.11 = (bf16[4,48,768]{2,1,0:T(8,128)(2,1)}, bf16[4,48,768]{2,1,0:T(8,128)(2,1)}, u32[]{:S(2)}, u32[]{:S(2)}) collective-permute-start(bf16[4,48,768]{2,1,0:T(8,128)(2,1)} %copy-done.12), channel_id=1, source_target_pairs={{0,56},{1,57},{2,58},{3,59},{4,60},{5,61},{6,62},{7,63},{8,16},{9,... | collective-permute-start | bytes 884744 | tf_op jit(solution)/shard_map/ppermute | solution.py:331
  61.2 40.0 %copy-start.4 = (bf16[512,768]{1,0:T(8,128)(2,1)S(1)}, bf16[512,768]{1,0:T(8,128)(2,1)}, u32[]{:S(2)}) copy-start(bf16[512,768]{1,0:T(8,128)(2,1)} %get-tuple-element.24.attn_ref) | copy-start | bytes 2359300
  61.2 8.4 %collective-permute-start.7 = (bf16[4,48,768]{2,1,0:T(8,128)(2,1)}, bf16[4,48,768]{2,1,0:T(8,128)(2,1)}, u32[]{:S(2)}, u32[]{:S(2)}) collective-permute-start(bf16[4,48,768]{2,1,0:T(8,128)(2,1)} %add_convert_fusion.1), channel_id=1, source_target_pairs={{0,6},{1,7},{2,4},{3,5},{4,2},{5,3},{6,0},{7,1},{8,14},{9,15},{10,... | collective-permute-start | bytes 884744 | tf_op jit(solution)/shard_map/ppermute | solution.py:331
  65.6 11.0 %collective-permute-start.13 = (bf16[4,48,768]{2,1,0:T(8,128)(2,1)}, bf16[4,48,768]{2,1,0:T(8,128)(2,1)}, u32[]{:S(2)}, u32[]{:S(2)}) collective-permute-start(bf16[4,48,768]{2,1,0:T(8,128)(2,1)} %add_convert_fusion), channel_id=1, source_target_pairs={{0,8},{1,9},{2,10},{3,11},{4,12},{5,13},{6,14},{7,15},{8,0},{9,1},... | collective-permute-start | bytes 884744 | tf_op jit(solution)/shard_map/ppermute | solution.py:331
  65.6 1.1 copy-start.3
  66.8 9.8 %copy-start.7 = (bf16[4,48,768]{2,1,0:T(8,128)(2,1)S(1)}, bf16[4,48,768]{2,1,0:T(8,128)(2,1)}, u32[]{:S(2)}) copy-start(bf16[4,48,768]{2,1,0:T(8,128)(2,1)} %copy-done.6) | copy-start | bytes 884740
  69.6 31.6 %collective-permute-start.3 = (bf16[512,768]{1,0:T(8,128)(2,1)}, bf16[512,768]{1,0:T(8,128)(2,1)}, u32[]{:S(2)}, u32[]{:S(2)}) collective-permute-start(bf16[512,768]{1,0:T(8,128)(2,1)} %shard_map.96), channel_id=1, source_target_pairs={{0,64},{64,0},{1,65},{65,1},{2,66},{66,2},{3,67},{67,3},{4,68},{68... | collective-permute-start | bytes 2359304 | tf_op jit(solution)/shard_map/ppermute | solution.py:190
  70.8 7.4 %collective-permute-start.10 = (bf16[1,48,768]{2,1,0:T(8,128)(2,1)S(1)}, bf16[1,48,768]{2,1,0:T(8,128)(2,1)S(1)}, u32[]{:S(2)}, u32[]{:S(2)}) collective-permute-start(bf16[1,48,768]{2,1,0:T(8,128)(2,1)S(1)} %get-tuple-element.38), channel_id=1, source_target_pairs={{0,16},{1,17},{2,18},{3,19},{4,20},{5,21},{6,22},{7,23},{8,56},{9,... | collective-permute-start | bytes 221192 | tf_op jit(solution)/shard_map/ppermute | solution.py:331
  73.5 7.5 %collective-permute-start.8 = (bf16[1,48,768]{2,1,0:T(8,128)(2,1)S(1)}, bf16[1,48,768]{2,1,0:T(8,128)(2,1)S(1)}, u32[]{:S(2)}, u32[]{:S(2)}) collective-permute-start(bf16[1,48,768]{2,1,0:T(8,128)(2,1)S(1)} %get-tuple-element.37), channel_id=1, source_target_pairs={{0,56},{1,57},{2,58},{3,59},{4,60},{5,61},{6,62},{7,63},{8,16},{9,... | collective-permute-start | bytes 221192 | tf_op jit(solution)/shard_map/ppermute | solution.py:331
  76.6 5.4 %collective-permute-start.9 = (bf16[1,48,768]{2,1,0:T(8,128)(2,1)S(1)}, bf16[1,48,768]{2,1,0:T(8,128)(2,1)S(1)}, u32[]{:S(2)}, u32[]{:S(2)}) collective-permute-start(bf16[1,48,768]{2,1,0:T(8,128)(2,1)S(1)} %get-tuple-element.39), channel_id=1, source_target_pairs={{0,8},{1,9},{2,10},{3,11},{4,12},{5,13},{6,14},{7,15},{8,0},{9,1},... | collective-permute-start | bytes 221192 | tf_op jit(solution)/shard_map/ppermute | solution.py:331
  77.8 5.2 %collective-permute-start.14 = (bf16[1,48,768]{2,1,0:T(8,128)(2,1)S(1)}, bf16[1,48,768]{2,1,0:T(8,128)(2,1)S(1)}, u32[]{:S(2)}, u32[]{:S(2)}) collective-permute-start(bf16[1,48,768]{2,1,0:T(8,128)(2,1)S(1)} %get-tuple-element.40), channel_id=1, source_target_pairs={{0,2},{1,3},{2,0},{3,1},{4,6},{5,7},{6,4},{7,5},{8,10},{9,11},{10,... | collective-permute-start | bytes 221192 | tf_op jit(solution)/shard_map/ppermute | solution.py:331
  78.3 5.6 %collective-permute-start.15 = (bf16[1,48,768]{2,1,0:T(8,128)(2,1)S(1)}, bf16[1,48,768]{2,1,0:T(8,128)(2,1)S(1)}, u32[]{:S(2)}, u32[]{:S(2)}) collective-permute-start(bf16[1,48,768]{2,1,0:T(8,128)(2,1)S(1)} %get-tuple-element.42), channel_id=1, source_target_pairs={{0,6},{1,7},{2,4},{3,5},{4,2},{5,3},{6,0},{7,1},{8,14},{9,15},{10,... | collective-permute-start | bytes 221192 | tf_op jit(solution)/shard_map/ppermute | solution.py:331
  80.9 5.9 %collective-permute-start.16 = (bf16[1,48,768]{2,1,0:T(8,128)(2,1)S(1)}, bf16[1,48,768]{2,1,0:T(8,128)(2,1)S(1)}, u32[]{:S(2)}, u32[]{:S(2)}) collective-permute-start(bf16[1,48,768]{2,1,0:T(8,128)(2,1)S(1)} %get-tuple-element.41), channel_id=1, source_target_pairs={{0,4},{1,5},{2,6},{3,7},{4,0},{5,1},{6,2},{7,3},{8,12},{9,13},{10,... | collective-permute-start | bytes 221192 | tf_op jit(solution)/shard_map/ppermute | solution.py:331
  87.8 6.1 %collective-permute-start.17 = (bf16[2,48,768]{2,1,0:T(8,128)(2,1)S(1)}, bf16[2,48,768]{2,1,0:T(8,128)(2,1)S(1)}, u32[]{:S(2)}, u32[]{:S(2)}) collective-permute-start(bf16[2,48,768]{2,1,0:T(8,128)(2,1)S(1)} %pad_maximum_fusion.2), channel_id=1, source_target_pairs={{0,1},{1,0},{2,3},{3,2},{4,5},{5,4},{6,7},{7,6},{8,9},{9,8},{10,11... | collective-permute-start | bytes 442376 | tf_op jit(solution)/shard_map/ppermute | solution.py:331
  89.3 5.6 %collective-permute-start.18 = (bf16[2,48,768]{2,1,0:T(8,128)(2,1)S(1)}, bf16[2,48,768]{2,1,0:T(8,128)(2,1)S(1)}, u32[]{:S(2)}, u32[]{:S(2)}) collective-permute-start(bf16[2,48,768]{2,1,0:T(8,128)(2,1)S(1)} %pad_maximum_fusion.2), channel_id=1, source_target_pairs={{0,129},{1,128},{2,131},{3,130},{4,133},{5,132},{6,135},{7,134},{8... | collective-permute-start | bytes 442376 | tf_op jit(solution)/shard_map/ppermute | solution.py:331
  89.9 6.6 %collective-permute-start.19 = (bf16[2,48,768]{2,1,0:T(8,128)(2,1)S(1)}, bf16[2,48,768]{2,1,0:T(8,128)(2,1)S(1)}, u32[]{:S(2)}, u32[]{:S(2)}) collective-permute-start(bf16[2,48,768]{2,1,0:T(8,128)(2,1)S(1)} %pad_maximum_fusion.2), channel_id=1, source_target_pairs={{0,128},{1,129},{2,130},{3,131},{4,132},{5,133},{6,134},{7,135},{8... | collective-permute-start | bytes 442376 | tf_op jit(solution)/shard_map/ppermute | solution.py:331
  96.6 12.9 %collective-permute-start.20 = (bf16[2,48,768]{2,1,0:T(8,128)(2,1)S(1)}, bf16[2,48,768]{2,1,0:T(8,128)(2,1)S(1)}, u32[]{:S(2)}, u32[]{:S(2)}) collective-permute-start(bf16[2,48,768]{2,1,0:T(8,128)(2,1)S(1)} %add_convert_fusion.3), channel_id=1, source_target_pairs={{0,32},{1,33},{2,34},{3,35},{4,36},{5,37},{6,38},{7,39},{8,40},{9,... | collective-permute-start | bytes 442376 | tf_op jit(solution)/shard_map/ppermute | solution.py:331
  101.2 1.0 copy-start.5
  107.4 28.6 %collective-permute-start.4 = (bf16[512,768]{1,0:T(8,128)(2,1)S(1)}, bf16[512,768]{1,0:T(8,128)(2,1)S(1)}, u32[]{:S(2)}, u32[]{:S(2)}) collective-permute-start(bf16[512,768]{1,0:T(8,128)(2,1)S(1)} %get-tuple-element.27), channel_id=1, source_target_pairs={{0,128},{128,0},{1,129},{129,1},{2,130},{130,2},{3,131},{131,3},{4... | collective-permute-start | bytes 2359304 | tf_op jit(solution)/shard_map/ppermute | solution.py:190
  109.6 5.3 %collective-permute-start.27 = (bf16[1,48,768]{2,1,0:T(8,128)(2,1)S(1)}, bf16[1,48,768]{2,1,0:T(8,128)(2,1)S(1)}, u32[]{:S(2)}, u32[]{:S(2)}) collective-permute-start(bf16[1,48,768]{2,1,0:T(8,128)(2,1)S(1)} %get-tuple-element.43), channel_id=1, source_target_pairs={{0,2},{1,3},{2,0},{3,1},{4,6},{5,7},{6,4},{7,5},{8,10},{9,11},{10,... | collective-permute-start | bytes 221192 | tf_op jit(solution)/shard_map/ppermute | solution.py:331
  109.7 6.2 %collective-permute-start.28 = (bf16[1,48,768]{2,1,0:T(8,128)(2,1)S(1)}, bf16[1,48,768]{2,1,0:T(8,128)(2,1)S(1)}, u32[]{:S(2)}, u32[]{:S(2)}) collective-permute-start(bf16[1,48,768]{2,1,0:T(8,128)(2,1)S(1)} %get-tuple-element.43), channel_id=1, source_target_pairs={{0,6},{1,7},{2,4},{3,5},{4,2},{5,3},{6,0},{7,1},{8,14},{9,15},{10,... | collective-permute-start | bytes 221192 | tf_op jit(solution)/shard_map/ppermute | solution.py:331
  111.9 6.0 %collective-permute-start.29 = (bf16[1,48,768]{2,1,0:T(8,128)(2,1)S(1)}, bf16[1,48,768]{2,1,0:T(8,128)(2,1)S(1)}, u32[]{:S(2)}, u32[]{:S(2)}) collective-permute-start(bf16[1,48,768]{2,1,0:T(8,128)(2,1)S(1)} %get-tuple-element.43), channel_id=1, source_target_pairs={{0,4},{1,5},{2,6},{3,7},{4,0},{5,1},{6,2},{7,3},{8,12},{9,13},{10,... | collective-permute-start | bytes 221192 | tf_op jit(solution)/shard_map/ppermute | solution.py:331
  113.7 5.8 %collective-permute-start.21 = (bf16[1,48,768]{2,1,0:T(8,128)(2,1)S(1)}, bf16[1,48,768]{2,1,0:T(8,128)(2,1)S(1)}, u32[]{:S(2)}, u32[]{:S(2)}) collective-permute-start(bf16[1,48,768]{2,1,0:T(8,128)(2,1)S(1)} %get-tuple-element.44), channel_id=1, source_target_pairs={{0,56},{1,57},{2,58},{3,59},{4,60},{5,61},{6,62},{7,63},{8,16},{9,... | collective-permute-start | bytes 221192 | tf_op jit(solution)/shard_map/ppermute | solution.py:331
  114.9 4.6 %collective-permute-start.22 = (bf16[1,48,768]{2,1,0:T(8,128)(2,1)S(1)}, bf16[1,48,768]{2,1,0:T(8,128)(2,1)S(1)}, u32[]{:S(2)}, u32[]{:S(2)}) collective-permute-start(bf16[1,48,768]{2,1,0:T(8,128)(2,1)S(1)} %get-tuple-element.44), channel_id=1, source_target_pairs={{0,8},{1,9},{2,10},{3,11},{4,12},{5,13},{6,14},{7,15},{8,0},{9,1},... | collective-permute-start | bytes 221192 | tf_op jit(solution)/shard_map/ppermute | solution.py:331
  115.9 6.5 %collective-permute-start.23 = (bf16[1,48,768]{2,1,0:T(8,128)(2,1)S(1)}, bf16[1,48,768]{2,1,0:T(8,128)(2,1)S(1)}, u32[]{:S(2)}, u32[]{:S(2)}) collective-permute-start(bf16[1,48,768]{2,1,0:T(8,128)(2,1)S(1)} %get-tuple-element.44), channel_id=1, source_target_pairs={{0,16},{1,17},{2,18},{3,19},{4,20},{5,21},{6,22},{7,23},{8,56},{9,... | collective-permute-start | bytes 221192 | tf_op jit(solution)/shard_map/ppermute | solution.py:331
  118.0 8.5 %collective-permute-start.31 = (bf16[4,48,768]{2,1,0:T(8,128)(2,1)S(1)}, bf16[4,48,768]{2,1,0:T(8,128)(2,1)S(1)}, u32[]{:S(2)}, u32[]{:S(2)}) collective-permute-start(bf16[4,48,768]{2,1,0:T(8,128)(2,1)S(1)} %pad_maximum_fusion.1.refs_2_), channel_id=1, source_target_pairs={{0,8},{1,9},{2,10},{3,11},{4,12},{5,13},{6,14},{7,15},{8,0},{9,1},... | collective-permute-start | bytes 884744 | tf_op jit(solution)/shard_map/ppermute | solution.py:331
  122.4 10.9 %collective-permute-start.25 = (bf16[4,48,768]{2,1,0:T(8,128)(2,1)S(1)}, bf16[4,48,768]{2,1,0:T(8,128)(2,1)S(1)}, u32[]{:S(2)}, u32[]{:S(2)}) collective-permute-start(bf16[4,48,768]{2,1,0:T(8,128)(2,1)S(1)} %pad_maximum_fusion.refs_0_), channel_id=1, source_target_pairs={{0,6},{1,7},{2,4},{3,5},{4,2},{5,3},{6,0},{7,1},{8,14},{9,15},{10,... | collective-permute-start | bytes 884744 | tf_op jit(solution)/shard_map/ppermute | solution.py:331
  124.2 12.7 %collective-permute-start.30 = (bf16[4,48,768]{2,1,0:T(8,128)(2,1)S(1)}, bf16[4,48,768]{2,1,0:T(8,128)(2,1)S(1)}, u32[]{:S(2)}, u32[]{:S(2)}) collective-permute-start(bf16[4,48,768]{2,1,0:T(8,128)(2,1)S(1)} %pad_maximum_fusion.1.refs_2_), channel_id=1, source_target_pairs={{0,56},{1,57},{2,58},{3,59},{4,60},{5,61},{6,62},{7,63},{8,16},{9,... | collective-permute-start | bytes 884744 | tf_op jit(solution)/shard_map/ppermute | solution.py:331
  125.8 11.1 %collective-permute-start.24 = (bf16[4,48,768]{2,1,0:T(8,128)(2,1)S(1)}, bf16[4,48,768]{2,1,0:T(8,128)(2,1)S(1)}, u32[]{:S(2)}, u32[]{:S(2)}) collective-permute-start(bf16[4,48,768]{2,1,0:T(8,128)(2,1)S(1)} %pad_maximum_fusion.refs_0_), channel_id=1, source_target_pairs={{0,2},{1,3},{2,0},{3,1},{4,6},{5,7},{6,4},{7,5},{8,10},{9,11},{10,... | collective-permute-start | bytes 884744 | tf_op jit(solution)/shard_map/ppermute | solution.py:331
  126.4 10.5 %collective-permute-start.32 = (bf16[4,48,768]{2,1,0:T(8,128)(2,1)S(1)}, bf16[4,48,768]{2,1,0:T(8,128)(2,1)S(1)}, u32[]{:S(2)}, u32[]{:S(2)}) collective-permute-start(bf16[4,48,768]{2,1,0:T(8,128)(2,1)S(1)} %collective-permute-done.31.refs_3_), channel_id=1, source_target_pairs={{0,56},{1,57},{2,58},{3,59},{4,60},{5,61},{6,62},{7,63},{8,16},{9,... | collective-permute-start | bytes 884744 | tf_op jit(solution)/shard_map/ppermute | solution.py:331
  133.3 6.7 %collective-permute-start.26 = (bf16[4,48,768]{2,1,0:T(8,128)(2,1)S(1)}, bf16[4,48,768]{2,1,0:T(8,128)(2,1)S(1)}, u32[]{:S(2)}, u32[]{:S(2)}) collective-permute-start(bf16[4,48,768]{2,1,0:T(8,128)(2,1)S(1)} %collective-permute-done.25.refs_1_), channel_id=1, source_target_pairs={{0,2},{1,3},{2,0},{3,1},{4,6},{5,7},{6,4},{7,5},{8,10},{9,11},{10,... | collective-permute-start | bytes 884744 | tf_op jit(solution)/shard_map/ppermute | solution.py:331
  (5 other events, 3.9 us)

commit v4 on v3

v4 whole, which is shorter than its diff:
```python
import functools

import jax
import jax.numpy as jnp
from jax import lax
from jax.experimental import pallas as pl
from jax.experimental.pallas import tpu as pltpu
from jax.sharding import Mesh
from jax.sharding import PartitionSpec as P

HD = 64
LAT = 128
IMAGES = 8
HEADER = 4
GROUP = 256
BIG = 128.0
EPS_NORM = 1e-05
EPS_HEAD = 1e-06
BF = jnp.bfloat16
F32 = jnp.float32
VMEM_LIMIT = 20 * 1024 * 1024
FULL_VMEM = 60 * 1024 * 1024


def norm_rows(head, own_ref, oth_ref, normed_ref, rows):
    share = own_ref.shape[1]
    step = 64

    def one(i, carry):
        at = pl.ds(pl.multiple_of(i * step, step), step)
        own = own_ref[at, :].astype(F32)
        oth = oth_ref[at, :].astype(F32)
        inv = 1.0 / (2 * share)
        mean = (jnp.sum(own, axis=1, keepdims=True) + jnp.sum(oth, axis=1, keepdims=True)) * inv
        own = own - mean
        oth = oth - mean
        var = (jnp.sum(own * own, axis=1, keepdims=True) + jnp.sum(oth * oth, axis=1, keepdims=True)) * inv
        scale = lax.rsqrt(var + EPS_NORM)
        own = (own * scale).astype(BF)
        oth = (oth * scale).astype(BF)

        @pl.when(head == 0)
        def _():
            normed_ref[at, :share] = own
            normed_ref[at, share:] = oth

        @pl.when(head != 0)
        def _():
            normed_ref[at, :share] = oth
            normed_ref[at, share:] = own

        return carry

    lax.fori_loop(0, rows // step, one, 0)


def head_norm(values, ones):
    mean = jnp.dot((values * values).astype(BF), ones, preferred_element_type=F32)
    return values * lax.rsqrt(mean + EPS_HEAD)


def ones_block():
    row = lax.broadcasted_iota(jnp.int32, (GROUP, GROUP), 0) // HD
    col = lax.broadcasted_iota(jnp.int32, (GROUP, GROUP), 1) // HD
    return jnp.where(row == col, 1.0 / HD, 0.0).astype(BF)


def features(place_ref, first, rows, inside, constant):
    pos = first + lax.broadcasted_iota(jnp.int32, (rows, 128), 0)
    lane = lax.broadcasted_iota(jnp.int32, (1, 128), 1) & (HD - 1)
    starts = jnp.zeros((1, 128), jnp.int32)
    ends = jnp.zeros((1, 128), jnp.int32)
    end = jnp.int32(0)
    for i in range(IMAGES):
        starts = jnp.where(lane == i, end, starts)
        end = end + place_ref[HEADER + i]
        ends = jnp.where(lane == i, end, ends)
    member = (pos >= starts) & (pos < ends)
    return jnp.where(lane == IMAGES, constant, jnp.where(member, inside, 0.0)).astype(BF)


def lower_half(rows):
    return lax.broadcasted_iota(jnp.int32, (rows, 128), 1) < HD


def attend_group(q, k, v, qfeat, kfeat, emit):
    q = (q.astype(F32) * 0.125).astype(BF)
    for pair in range(2):
        lanes = slice(pair * 128, pair * 128 + 128)
        qp, kp, vp = q[:, lanes], k[:, lanes], v[:, lanes]
        qlow, klow = lower_half(qp.shape[0]), lower_half(kp.shape[0])
        one = jnp.ones_like(vp)
        for odd in range(2):
            qa = jnp.where(qlow, qfeat, qp) if odd else jnp.where(qlow, qp, qfeat)
            ka = jnp.where(klow, kfeat, kp) if odd else jnp.where(klow, kp, kfeat)
            va = jnp.where(klow, one, vp) if odd else jnp.where(klow, vp, one)
            s = lax.dot_general(qa, ka, (((1,), (1,)), ((), ())), preferred_element_type=F32)
            w = jnp.exp(s).astype(BF)
            emit(2 * pair + odd, jnp.dot(w, va, preferred_element_type=F32))


def local_kernel(place_ref, own_ref, oth_ref, w_ref, q_ref, acc_ref, normed_ref, qf_ref, kf_ref, ones_ref):
    rows = own_ref.shape[0]

    @pl.when(pl.program_id(0) == 0)
    def _():
        norm_rows(place_ref[1], own_ref, oth_ref, normed_ref, rows)
        first = place_ref[0] * rows
        qf_ref[...] = features(place_ref, first, rows, BIG, -BIG)
        kf_ref[...] = features(place_ref, first, rows, 1.0, 1.0)
        ones_ref[...] = ones_block()

    normed = normed_ref[...]
    ones = ones_ref[...]
    q = head_norm(jnp.dot(normed, w_ref[0], preferred_element_type=F32), ones).astype(BF)
    k = head_norm(jnp.dot(normed, w_ref[1], preferred_element_type=F32), ones).astype(BF)
    v = jnp.dot(normed, w_ref[2], preferred_element_type=F32).astype(BF)
    q_ref[...] = q

    def emit(head, r):
        acc_ref[:, head * 128 : head * 128 + 128] = r

    attend_group(q, k, v, qf_ref[...], kf_ref[...], emit)


def foreign_kernel(place_ref, own_ref, oth_ref, wk_ref, wv_ref, q_ref, acc_in_ref, attn_ref, t0_ref, t1_ref, t2_ref, t3_ref, normed_ref, qf_ref, kf_ref, ones_ref, k_ref, v_ref, acc_ref, turned_ref):
    rows = own_ref.shape[0]
    half = rows // 2

    @pl.when(pl.program_id(0) == 0)
    def _():
        norm_rows(place_ref[1], own_ref, oth_ref, normed_ref, rows)
        qf_ref[...] = features(place_ref, place_ref[0] * rows, rows, BIG, -BIG)
        kf_ref[...] = features(place_ref, (1 - place_ref[0]) * rows, rows, 1.0, 1.0)
        ones_ref[...] = ones_block()

    normed = normed_ref[...]
    k_ref[...] = head_norm(jnp.dot(normed, wk_ref[0], preferred_element_type=F32), ones_ref[...]).astype(BF)
    v_ref[...] = jnp.dot(normed, wv_ref[0], preferred_element_type=F32).astype(BF)
    near = pl.ds(pl.multiple_of(place_ref[0] * half, half), half)
    far = pl.ds(pl.multiple_of((1 - place_ref[0]) * half, half), half)

    def emit_near(head, r):
        lanes = slice(head * 128, head * 128 + 128)
        acc_ref[:, lanes] = acc_in_ref[:, lanes] + r

    attend_group(q_ref[...], k_ref[near, :], v_ref[near, :], qf_ref[...], kf_ref[near, :], emit_near)

    def emit_far(head, r):
        lanes = slice(head * 128, head * 128 + 128)
        acc_ref[far, lanes] = acc_ref[far, lanes] + r

    attend_group(q_ref[far, :], k_ref[far, :], v_ref[far, :], qf_ref[far, :], kf_ref[far, :], emit_far)
    low = lower_half(rows)
    for pair in range(2):
        even = acc_ref[:, pair * 256 : pair * 256 + 128]
        odd = acc_ref[:, pair * 256 + 128 : pair * 256 + 256]
        total = pltpu.roll(jnp.where(low, odd, even), HD, 1)
        attn_ref[:, pair * 128 : pair * 128 + 128] = (jnp.where(low, even, odd) / total).astype(BF)
    group = pl.program_id(0)
    turned_ref[pl.ds(pl.multiple_of(group * GROUP, GROUP), GROUP), :] = attn_ref[...].T

    @pl.when(group == pl.num_programs(0) - 1)
    def _():
        for i, out in enumerate((t0_ref, t1_ref, t2_ref, t3_ref)):
            part = out.shape[0]
            out[...] = turned_ref[pl.ds(pl.multiple_of((i ^ place_ref[2]) * part, part), part), :]


def send_kernel(place_ref, attn_ref, w_ref, out_ref):
    out_ref[...] = jnp.dot(attn_ref[...], w_ref[...], preferred_element_type=F32).astype(BF)


def mixed_kernel(place_ref, attn_ref, w_ref, recv_ref, pick_ref, mixed_ref, send_ref, keep_ref):
    rows = attn_ref.shape[0]
    mixed = (jnp.dot(attn_ref[...], w_ref[...], preferred_element_type=F32) + recv_ref[...].astype(F32)).astype(BF)
    mixed_ref[...] = mixed
    row = lax.broadcasted_iota(jnp.int32, (rows, rows), 1)
    for half, out in ((0, send_ref), (1, keep_ref)):
        hot = jnp.where(pick_ref[half * rows : half * rows + rows, :] == row, 1.0, 0.0).astype(BF)
        out[...] = jnp.dot(hot, mixed, preferred_element_type=F32).astype(BF)


def call(kernel, place, grid, in_specs, out_specs, out_shape, scratch, flops, nbytes, args, alias=None, limit=VMEM_LIMIT):
    return pl.pallas_call(
        kernel,
        grid_spec=pltpu.PrefetchScalarGridSpec(
            num_scalar_prefetch=1, grid=grid, in_specs=in_specs, out_specs=out_specs, scratch_shapes=scratch
        ),
        out_shape=out_shape,
        input_output_aliases=alias or {},
        cost_estimate=pl.CostEstimate(flops=flops, bytes_accessed=nbytes, transcendentals=0),
        compiler_params=pltpu.CompilerParams(vmem_limit_bytes=limit),
    )(place, *args)


def whole(shape):
    return pl.BlockSpec(shape, lambda g, s: (0,) * len(shape))


def columns(rows, width):
    return pl.BlockSpec((rows, width), lambda g, s: (0, g))


def swap(value, axis):
    return lax.ppermute(value, axis, [(0, 1), (1, 0)])


def grad_kernel(place_ref, *refs):
    lefts, rights, outs, total_ref = refs[:4], refs[4:8], refs[8:12], refs[12]
    total = jnp.dot(lefts[0][...], rights[0][...], preferred_element_type=F32)
    for left, right in zip(lefts[1:], rights[1:]):
        total = total + jnp.dot(left[...], right[...], preferred_element_type=F32)
    total_ref[...] = total
    for i, out in enumerate(outs):
        piece = out.shape[0]
        out[...] = total_ref[pl.ds(pl.multiple_of((i ^ place_ref[3]) * piece, piece), piece), :].astype(BF)


def place_kernel(place_ref, part_ref, *refs, scale):
    out_ref = refs[-1]
    _, piece, _ = part_ref.shape
    for i in range(4):
        out_ref[i * piece : i * piece + piece, :] = part_ref[i ^ place_ref[3]].astype(F32) * scale


AXES = ("seq", "head", "z", "y", "xl")
ROUTES = (
    (("y", 0), ("y", 1), ("z", 0), ("z", 1)),
    (("z", 0), ("z", 1), ("y", 0), ("y", 1)),
)


def across(i, kind, n):
    if kind == 0:
        return i ^ 1
    return (i + 1) % n if i % 2 else (i - 1) % n


def bit_of(i, kind):
    return ((i + 1) >> 1) & 1 if kind == 0 else (i >> 1) & 1


def every_device(sizes):
    for i in range(sizes[0] * sizes[1] * sizes[2] * sizes[3] * sizes[4]):
        at, rest = {}, i
        for name, n in reversed(list(zip(AXES, sizes))):
            at[name] = rest % n
            rest //= n
        yield i, at


def index_of(at, sizes):
    i = 0
    for name, n in zip(AXES, sizes):
        i = i * n + at[name]
    return i


def pairs(sizes, partner):
    out = []
    for i, at in every_device(sizes):
        out.append((i, index_of(partner(at), sizes)))
    return out


def quad_tables(sizes, group):
    n = dict(zip(AXES, sizes))

    def partner(at, steps):
        for step in steps:
            axis, kind = ROUTES[at["head"]][2 * group + step]
            at = {**at, axis: across(at[axis], kind, n[axis])}
        return at

    return [pairs(sizes, lambda at, steps=steps: partner(at, steps)) for steps in ((1,), (0,), (0, 1))]


def x_tables(sizes):
    n = dict(zip(AXES, sizes))

    def partner(at, kinds):
        x = at["seq"] * n["xl"] + at["xl"]
        for kind in kinds:
            x = across(x, kind, n["seq"] * n["xl"])
        return {**at, "seq": x // n["xl"], "xl": x % n["xl"]}

    return [pairs(sizes, lambda at, kinds=kinds: partner(at, kinds)) for kinds in ((0,), (1,), (0, 1))]


def z_table(sizes):
    n = sizes[AXES.index("z")]
    return pairs(sizes, lambda at: {**at, "z": (at["z"] + n // 2) % n})


def mask_of(group, head):
    masks = []
    for core in (0, 1):
        mask = jnp.int32(0)
        for axis, kind in ROUTES[core][2 * group : 2 * group + 2]:
            mask = mask * 2 + bit_of(lax.axis_index(axis).astype(jnp.int32), kind)
        masks.append(mask)
    return jnp.where(head == 0, masks[0], masks[1])


def add(*terms):
    terms = [t.astype(F32) for t in terms]
    while len(terms) > 1:
        terms = [sum(terms[i + 1 : i + 2], terms[i]) for i in range(0, len(terms), 2)]
    return terms[0].astype(BF)


def move(value, table):
    return lax.ppermute(value, AXES, table)


def place_call(place, at, scale, part, before):
    _, piece, width = part.shape
    args, specs, alias = [part], [whole(part.shape)], None
    if before is not None:
        args, specs, alias = args + [before], specs + [pl.BlockSpec(memory_space=pl.ANY)], {2: 0}
    return call(
        functools.partial(place_kernel, scale=scale), place, (1,), specs,
        pl.BlockSpec((4 * piece, width), lambda g, s: (at ^ s[2], 0)),
        jax.ShapeDtypeStruct((16 * piece, width), F32), [], 10**6, 2 * 10**6, args, alias,
    )


def grad_call(place, lefts, rights):
    part, rows = lefts[0].shape
    width = rights[0].shape[1]
    piece = part // 4
    return call(
        grad_kernel, place, (width // GROUP,),
        [whole(lefts[0].shape)] * 4 + [columns(rows, GROUP)] * 4, [columns(piece, GROUP)] * 4,
        [jax.ShapeDtypeStruct((piece, width), BF)] * 4, [pltpu.VMEM((part, GROUP), F32)],
        12 * 10**8, 8 * 10**6, (*lefts, *rights),
    )


def body(tokens, lengths, owner_slot, latent_index, cotangent, qkv_weight, out_weight):
    own = tokens[0]
    rows, share = own.shape
    groups = share // GROUP
    seq = lax.axis_index("seq")
    head = lax.axis_index("head")
    sizes = lengths[0]
    ends = jnp.cumsum(sizes, dtype=jnp.int32)
    starts = ends - sizes
    place = jnp.concatenate([jnp.stack([seq, head, mask_of(0, head), mask_of(1, head)]).astype(jnp.int32), sizes])

    oth = swap(own, "head")
    foreign_own = swap(own, "seq")
    devices = tuple(lax.axis_size(a) for a in AXES)
    first, second = quad_tables(devices, 0), quad_tables(devices, 1)
    cots = [cotangent[0]] + [move(cotangent[0], table) for table in first]

    slots = owner_slot[0]
    picks = starts[:, None] + jnp.remainder(latent_index[0], sizes[:, None])
    order = slots[None, :] == jnp.arange(IMAGES, dtype=jnp.int32)[:, None]
    by_slot = jnp.sum(jnp.where(order[:, :, None], picks[None], 0), axis=1).reshape(2, rows)
    local = by_slot - seq * rows
    local = jnp.stack([jnp.where(seq == 0, local[1], local[0]), jnp.where(seq == 0, local[0], local[1])])
    local = local.reshape(2 * rows, 1)

    scratch = lambda r, qr, kr: [
        pltpu.VMEM((r, 2 * share), BF),
        pltpu.VMEM((qr, 128), BF),
        pltpu.VMEM((kr, 128), BF),
        pltpu.VMEM((GROUP, GROUP), BF),
    ]
    weight = lambda j: pl.BlockSpec((1, 2 * share, GROUP), lambda g, s: (j, 0, g))
    q, acc = call(
        local_kernel, place, (groups,),
        [whole((rows, share)), whole((rows, share)),
         pl.BlockSpec((3, 2 * share, GROUP), lambda g, s: (0, 0, g))],
        [columns(rows, GROUP), columns(rows, 2 * GROUP)],
        [jax.ShapeDtypeStruct((rows, share), BF), jax.ShapeDtypeStruct((rows, 2 * share), F32)],
        scratch(rows, rows, rows), 7 * 10**9, 12 * 10**6, (own, oth, qkv_weight), limit=FULL_VMEM,
    )
    foreign_own, q, local = lax.optimization_barrier((foreign_own, q, local))
    foreign_oth = swap(foreign_own, "head")
    quarter = whole((share // 4, rows))
    attn, *turned = call(
        foreign_kernel, place, (groups,),
        [whole((rows, share)), whole((rows, share)), weight(1), weight(2), columns(rows, GROUP), columns(rows, 2 * GROUP)],
        [columns(rows, GROUP)] + [quarter] * 4,
        [jax.ShapeDtypeStruct((rows, share), BF)] + [jax.ShapeDtypeStruct((share // 4, rows), BF)] * 4,
        scratch(rows, rows, rows)
        + [pltpu.VMEM((rows, GROUP), BF), pltpu.VMEM((rows, GROUP), BF), pltpu.VMEM((rows, 2 * GROUP), F32),
           pltpu.VMEM((share, rows), BF)],
        4 * 10**9, 14 * 10**6, (foreign_own, foreign_oth, qkv_weight, qkv_weight, q, acc), limit=FULL_VMEM,
    )
    lefts = [turned[0]] + [move(t, table) for t, table in zip(turned[1:], first)]

    partial = call(
        send_kernel, place, (groups,),
        [whole((rows, share)), pl.BlockSpec((share, GROUP), lambda g, s: (0, (1 - s[1]) * groups + g))],
        columns(rows, GROUP), jax.ShapeDtypeStruct((rows, share), BF), [], 6 * 10**8, 3 * 10**6, (attn, out_weight),
    )
    lefts[3], partial = lax.optimization_barrier((lefts[3], partial))
    recv = swap(partial, "head")

    pieces = grad_call(place, lefts, cots)
    grad = add(pieces[0], *[move(p, table) for p, table in zip(pieces[1:], second)])
    over_x = [move(grad, table) for table in x_tables(devices)]

    shape = jax.ShapeDtypeStruct((rows, share), BF)
    mixed, send, keep = call(
        mixed_kernel, place, (groups,),
        [whole((rows, share)), pl.BlockSpec((share, GROUP), lambda g, s: (0, s[1] * groups + g)),
         columns(rows, GROUP), whole((2 * rows, 1))],
        [columns(rows, GROUP)] * 3, [shape] * 3, [], 14 * 10**8, 6 * 10**6, (attn, out_weight, recv, local),
    )
    over_x[2], send = lax.optimization_barrier((over_x[2], send))
    grad = add(grad, *over_x)
    grad, send = lax.optimization_barrier((grad, send))
    latents = keep + swap(send, "seq")
    grad = add(grad, move(grad, z_table(devices)))
    held = jnp.stack([grad] + [move(grad, table) for table in second])
    held = [held] + [move(held, table) for table in first]
    scale = (2 * rows * lax.axis_size("z") * lax.axis_size("y") * lax.axis_size("xl")) ** (-0.5)
    grad_out = None
    for at, part in enumerate(held):
        grad_out = place_call(place, at, scale, part, grad_out)
    return mixed[None], latents[None], grad_out


def on_mesh(fine):
    dp = ("z", "y", "xl")
    in_specs = (
        P(dp, "seq", "head"),
        P(dp, None),
        P(dp, None),
        P(dp, None, None),
        P(dp, "seq", None),
        P(None, None, "head"),
        P("head", None),
    )
    out_specs = (P(dp, "seq", "head"), P(dp, "seq", "head"), P("head", None))
    return jax.shard_map(body, mesh=fine, in_specs=in_specs, out_specs=out_specs, check_vma=False)


def solution(mesh):
    return on_mesh(Mesh(mesh.devices.reshape(2, 2, 8, 4, 2), ("seq", "head", "z", "y", "xl")))
```

time: 143 us -> 140 us (0.979)
  waiting for transfers between devices: 21.5 us -> 32.2 us
  starting transfers between devices: 48.9 us -> 39.5 us
  other arithmetic: 11.8 us -> 6 us
  Pallas kernels: 50.4 us -> 55.2 us
  local copies, waits for them, and re-layouts: 9.09 us -> 6.25 us
    ppermute x28 -> x19, waiting for transfers between devices: 19.6 us -> 30.3 us  [move(): return lax.ppermute(value, AXES, table)]
    ppermute x28 -> x19, starting transfers between devices: 44.3 us -> 34.3 us  [move(): return lax.ppermute(value, AXES, table)]
    convert_element_type x8 -> x3, other arithmetic: 8.23 us -> 1.17 us  [add(): return terms[0].astype(BF)]
    pallas_call x8 -> x9, Pallas kernels: 50.4 us -> 55.2 us  [call(): pl.pallas_call(kernel, grid_spec=pltpu.PrefetchScalarGridSpec(num_scalar_...]
    unnamed x42 -> x21, local copies, waits for them, and re-layouts: 8.29 us -> 3.96 us
  transfers between devices with their start and end apart: 33 -> 24, of which waited for: 11 -> 12; matrix products, arithmetic and copies ran while one was open for 10% -> 5% of each run, Pallas kernels for 21% -> 38%
where the time goes in v4:
time: 140 us
  Pallas kernels  55.2 us (39%)
  starting transfers between devices  39.5 us (28%)
  waiting for transfers between devices  32.2 us (23%)
  local copies, waits for them, and re-layouts  6.25 us (4%)
  other arithmetic  6 us (4%)
    pallas_call x9, Pallas kernels, call(): pl.pallas_call(kernel, grid_spec=pltpu.PrefetchScalarGridSpec(num_scalar_...  55.2 us
    ppermute x19, starting transfers between devices, move(): return lax.ppermute(value, AXES, table)  34.3 us
    ppermute x19, waiting for transfers between devices, move(): return lax.ppermute(value, AXES, table)  30.3 us
    ppermute x5, starting transfers between devices, swap(): return lax.ppermute(value, axis, [(0, 1), (1, 0)])  5.23 us
    unnamed x21, local copies, waits for them, and re-layouts  3.96 us
  transfers between devices with their start and end apart: 24, of which 12 were waited for; matrix products, arithmetic and copies ran while one was open for 5% of the time, Pallas kernels for 38%

profile of v4, /device:TPU:2, one launch (start us, length us, event | category | flops | bytes accessed | tf_op | source)
XLA Modules:
  0.0 140.0 jit_solution(5735961038422276257)
XLA Ops:
  0.7 2.2 %collective-permute-start = (bf16[512,768]{1,0:T(8,128)(2,1)}, bf16[512,768]{1,0:T(8,128)(2,1)S(1)}, u32[]{:S(2)}, u32[]{:S(2)}) collective-permute-start(bf16[512,768]{1,0:T(8,128)(2,1)} %bitcast.45), channel_id=1, source_target_pairs={{0,128},{128,0},{1,129},{129,1},{2,130},{130,2},{3,131},{131,3},{4... | collective-permute-start | bytes 2359304 | tf_op jit(solution)/shard_map/ppermute | solution.py:206
  2.9 3.2 %collective-permute-start.9 = (bf16[512,1536]{1,0:T(8,128)(2,1)}, bf16[512,1536]{1,0:T(8,128)(2,1)}, u32[]{:S(2)}, u32[]{:S(2)}) collective-permute-start(bf16[512,1536]{1,0:T(8,128)(2,1)} %bitcast.31), channel_id=1, source_target_pairs={{0,4},{1,5},{2,6},{3,7},{4,0},{5,1},{6,2},{7,3},{8,12},{9,13},{10,... | collective-permute-start | bytes 4718600 | tf_op jit(solution)/shard_map/ppermute | solution.py:314
  6.1 0.7 collective-permute-start.8
  7.9 0.8 reduce-window.8
  9.3 0.9 fusion.1
  10.2 0.7 iota_compare_fusion
  11.1 1.3 concatenate.3.place_ref
  12.3 0.9 copy-done.9
  13.2 18.0 %shard_map.94 = (bf16[512,768]{1,0:T(8,128)(2,1)}, f32[512,1536]{1,0:T(8,128)}) custom-call(s32[12]{0:T(128)} %concatenate.3.place_ref, bf16[512,768]{1,0:T(8,128)(2,1)} %bitcast.46, bf16[512,768]{1,0:T(8,128)(2,1)} %copy-done.9, bf16[3,1536,768]{2,1,0:T(8,128)(2,1)} %wv_ref.1), custom_call_target="tpu_custom_call" | custom-call | flops 7000000000 | bytes 12000000 | tf_op jit(solution)/shard_map/pallas_call | solution.py:185
  31.2 2.7 %collective-permute-start.2 = (bf16[512,768]{1,0:T(8,128)(2,1)S(1)}, bf16[512,768]{1,0:T(8,128)(2,1)S(1)}, u32[]{:S(2)}, u32[]{:S(2)}) collective-permute-start(bf16[512,768]{1,0:T(8,128)(2,1)S(1)} %collective-permute-done.own_ref), channel_id=1, source_target_pairs={{0,64},{64,0},{1,65},{65,1},{2,66},{66,2},{3,67},{67,3},{4,68},{68... | collective-permute-start | bytes 2359304 | tf_op jit(solution)/shard_map/ppermute | solution.py:206
  33.9 1.9 %collective-permute-done.2.oth_ref = bf16[512,768]{1,0:T(8,128)(2,1)S(1)} collective-permute-done((bf16[512,768]{1,0:T(8,128)(2,1)S(1)}, bf16[512,768]{1,0:T(8,128)(2,1)S(1)}, u32[]{:S(2)}, u32[]{:S(2)}) %collective-permute-start.2) | collective-permute-done | bytes 786464 | tf_op jit(solution)/shard_map/ppermute | solution.py:206
  35.8 0.9 copy-done.8
  36.7 16.9 %shard_map.95 = (bf16[512,768]{1,0:T(8,128)(2,1)}, bf16[192,512]{1,0:T(8,128)(2,1)}, bf16[192,512]{1,0:T(8,128)(2,1)}, bf16[192,512]{1,0:T(8,128)(2,1)}, bf16[192,512]{1,0:T(8,128)(2,1)}) custom-call(s32[12]{0:T(128)} %concatenate.3.place_ref, bf16[512,768]{1,0:T(8,128)(2,1)} %copy-done.7, bf16[512,768]{1,0:T(8,128)(2,1)} %copy-done.8, ...), custom_call_target="tpu_custom_call" | custom-call | flops 4000000000 | bytes 14000000 | tf_op jit(solution)/shard_map/pallas_call | solution.py:185
  53.6 3.3 %collective-permute-start.3 = (bf16[192,512]{1,0:T(8,128)(2,1)}, bf16[192,512]{1,0:T(8,128)(2,1)S(1)}, u32[]{:S(2)}, u32[]{:S(2)}) collective-permute-start(bf16[192,512]{1,0:T(8,128)(2,1)} %get-tuple-element.31), channel_id=1, source_target_pairs={{0,4},{1,5},{2,6},{3,7},{4,0},{5,1},{6,2},{7,3},{8,12},{9,13},{10,... | collective-permute-start | bytes 589832 | tf_op jit(solution)/shard_map/ppermute | solution.py:314
  56.9 1.1 collective-permute-start.5
  58.0 3.1 %collective-permute-done.3.refs_3_ = bf16[192,512]{1,0:T(8,128)(2,1)S(1)} collective-permute-done((bf16[192,512]{1,0:T(8,128)(2,1)}, bf16[192,512]{1,0:T(8,128)(2,1)S(1)}, u32[]{:S(2)}, u32[]{:S(2)}) %collective-permute-start.3) | collective-permute-done | bytes 196640 | tf_op jit(solution)/shard_map/ppermute | solution.py:314
  61.1 1.7 %collective-permute-start.6 = (bf16[192,512]{1,0:T(8,128)(2,1)}, bf16[192,512]{1,0:T(8,128)(2,1)S(1)}, u32[]{:S(2)}, u32[]{:S(2)}) collective-permute-start(bf16[192,512]{1,0:T(8,128)(2,1)} %get-tuple-element.38), channel_id=1, source_target_pairs={{0,2},{1,3},{2,0},{3,1},{4,6},{5,7},{6,4},{7,5},{8,10},{9,11},{10,... | collective-permute-start | bytes 589832 | tf_op jit(solution)/shard_map/ppermute | solution.py:314
  62.8 1.1 copy-done.2
  63.9 2.8 %shard_map.96 = bf16[512,768]{1,0:T(8,128)(2,1)} custom-call(s32[12]{0:T(128)S(1)} %copy-done.6, bf16[512,768]{1,0:T(8,128)(2,1)S(1)} %copy-done.2, bf16[768,1536]{1,0:T(8,128)(2,1)S(1)} %copy-done), custom_call_target="tpu_custom_call" | custom-call | flops 600000000 | bytes 3000000 | tf_op jit(solution)/shard_map/pallas_call | solution.py:185
  67.0 5.8 %shard_map.98 = (bf16[48,1536]{1,0:T(8,128)(2,1)S(1)}, bf16[48,1536]{1,0:T(8,128)(2,1)S(1)}, bf16[48,1536]{1,0:T(8,128)(2,1)S(1)}, bf16[48,1536]{1,0:T(8,128)(2,1)S(1)}) custom-call(s32[12]{0:T(128)S(1)} %copy-done.6, bf16[192,512]{1,0:T(8,128)(2,1)S(1)} %copy-done.5, bf16[192,512]{1,0:T(8,128)(2,1)S(1)} %collective-permute-done.5.refs_1_, ...), custom_call_target="tpu_custom_call" | custom-call | flops 1200000000 | bytes 8000000 | tf_op jit(solution)/shard_map/pallas_call | solution.py:185
  72.8 3.7 %collective-permute-start.10 = (bf16[48,1536]{1,0:T(8,128)(2,1)S(1)}, bf16[48,1536]{1,0:T(8,128)(2,1)S(1)}, u32[]{:S(2)}, u32[]{:S(2)}) collective-permute-start(bf16[48,1536]{1,0:T(8,128)(2,1)S(1)} %get-tuple-element.41), channel_id=1, source_target_pairs={{0,56},{1,57},{2,58},{3,59},{4,60},{5,61},{6,62},{7,63},{8,16},{9,... | collective-permute-start | bytes 442376 | tf_op jit(solution)/shard_map/ppermute | solution.py:314
  76.5 2.5 %collective-permute-start.12 = (bf16[48,1536]{1,0:T(8,128)(2,1)S(1)}, bf16[48,1536]{1,0:T(8,128)(2,1)S(1)}, u32[]{:S(2)}, u32[]{:S(2)}) collective-permute-start(bf16[48,1536]{1,0:T(8,128)(2,1)S(1)} %get-tuple-element.43), channel_id=1, source_target_pairs={{0,16},{1,17},{2,18},{3,19},{4,20},{5,21},{6,22},{7,23},{8,56},{9,... | collective-permute-start | bytes 442376 | tf_op jit(solution)/shard_map/ppermute | solution.py:314
  78.9 0.7 collective-permute-done.10
  79.6 2.0 %collective-permute-done.11 = bf16[48,1536]{1,0:T(8,128)(2,1)S(1)} collective-permute-done((bf16[48,1536]{1,0:T(8,128)(2,1)S(1)}, bf16[48,1536]{1,0:T(8,128)(2,1)S(1)}, u32[]{:S(2)}, u32[]{:S(2)}) %collective-permute-start.11) | collective-permute-done | bytes 147488 | tf_op jit(solution)/shard_map/ppermute | solution.py:314
  81.6 2.1 %collective-permute-done.12 = bf16[48,1536]{1,0:T(8,128)(2,1)S(1)} collective-permute-done((bf16[48,1536]{1,0:T(8,128)(2,1)S(1)}, bf16[48,1536]{1,0:T(8,128)(2,1)S(1)}, u32[]{:S(2)}, u32[]{:S(2)}) %collective-permute-start.12) | collective-permute-done | bytes 147488 | tf_op jit(solution)/shard_map/ppermute | solution.py:314
  83.8 1.5 %collective-permute-start.15 = (bf16[48,1536]{1,0:T(8,128)(2,1)S(1)}, bf16[48,1536]{1,0:T(8,128)(2,1)S(1)}, u32[]{:S(2)}, u32[]{:S(2)}) collective-permute-start(bf16[48,1536]{1,0:T(8,128)(2,1)S(1)} %add_convert_fusion.2), channel_id=1, source_target_pairs={{0,128},{1,129},{2,130},{3,131},{4,132},{5,133},{6,134},{7,135},{8... | collective-permute-start | bytes 442376 | tf_op jit(solution)/shard_map/ppermute | solution.py:314
  85.3 1.5 %collective-permute-start.14 = (bf16[48,1536]{1,0:T(8,128)(2,1)S(1)}, bf16[48,1536]{1,0:T(8,128)(2,1)}, u32[]{:S(2)}, u32[]{:S(2)}) collective-permute-start(bf16[48,1536]{1,0:T(8,128)(2,1)S(1)} %add_convert_fusion.2), channel_id=1, source_target_pairs={{0,129},{1,128},{2,131},{3,130},{4,133},{5,132},{6,135},{7,134},{8... | collective-permute-start | bytes 442376 | tf_op jit(solution)/shard_map/ppermute | solution.py:314
  86.8 1.8 %collective-permute-start.13 = (bf16[48,1536]{1,0:T(8,128)(2,1)S(1)}, bf16[48,1536]{1,0:T(8,128)(2,1)}, u32[]{:S(2)}, u32[]{:S(2)}) collective-permute-start(bf16[48,1536]{1,0:T(8,128)(2,1)S(1)} %add_convert_fusion.2), channel_id=1, source_target_pairs={{0,1},{1,0},{2,3},{3,2},{4,5},{5,4},{6,7},{7,6},{8,9},{9,8},{10,11... | collective-permute-start | bytes 442376 | tf_op jit(solution)/shard_map/ppermute | solution.py:314
  88.6 1.0 copy.14.pick_ref
  89.6 1.0 copy-done.4
  90.7 5.1 %shard_map.97 = (bf16[512,768]{1,0:T(8,128)(2,1)}, bf16[512,768]{1,0:T(8,128)(2,1)S(1)}, bf16[512,768]{1,0:T(8,128)(2,1)S(1)}) custom-call(s32[12]{0:T(128)S(1)} %copy-done.6, bf16[512,768]{1,0:T(8,128)(2,1)S(1)} %copy-done.3, bf16[768,1536]{1,0:T(8,128)(2,1)S(1)} %copy-done, bf16[512,768]{1,0:T(8,128)(2,1)} %collective-permute-done.4.recv_ref, ...), custom_call_target="tpu_custom_call" | custom-call | flops 1400000000 | bytes 6000000 | tf_op jit(solution)/shard_map/pallas_call | solution.py:185
  95.8 1.1 add_convert_fusion.1
  96.9 3.6 %collective-permute-start.17 = (bf16[48,1536]{1,0:T(8,128)(2,1)S(1)}, bf16[48,1536]{1,0:T(8,128)(2,1)S(1)}, u32[]{:S(2)}, u32[]{:S(2)}) collective-permute-start(bf16[48,1536]{1,0:T(8,128)(2,1)S(1)} %add_convert_fusion.1), channel_id=1, source_target_pairs={{0,32},{1,33},{2,34},{3,35},{4,36},{5,37},{6,38},{7,39},{8,40},{9,... | collective-permute-start | bytes 442376 | tf_op jit(solution)/shard_map/ppermute | solution.py:314
  100.6 6.0 %collective-permute-done.17 = bf16[48,1536]{1,0:T(8,128)(2,1)S(1)} collective-permute-done((bf16[48,1536]{1,0:T(8,128)(2,1)S(1)}, bf16[48,1536]{1,0:T(8,128)(2,1)S(1)}, u32[]{:S(2)}, u32[]{:S(2)}) %collective-permute-start.17) | collective-permute-done | bytes 147488 | tf_op jit(solution)/shard_map/ppermute | solution.py:314
  106.7 0.8 collective-permute-start.20
  107.5 3.8 %collective-permute-start.19 = (bf16[48,1536]{1,0:T(8,128)(2,1)S(1)}, bf16[48,1536]{1,0:T(8,128)(2,1)S(1)}, u32[]{:S(2)}, u32[]{:S(2)}) collective-permute-start(bf16[48,1536]{1,0:T(8,128)(2,1)S(1)} %add_convert_fusion), channel_id=1, source_target_pairs={{0,8},{1,9},{2,10},{3,11},{4,12},{5,13},{6,14},{7,15},{8,0},{9,1},... | collective-permute-start | bytes 442376 | tf_op jit(solution)/shard_map/ppermute | solution.py:314
  111.4 2.6 %collective-permute-done.20 = bf16[48,1536]{1,0:T(8,128)(2,1)S(1)} collective-permute-done((bf16[48,1536]{1,0:T(8,128)(2,1)S(1)}, bf16[48,1536]{1,0:T(8,128)(2,1)S(1)}, u32[]{:S(2)}, u32[]{:S(2)}) %collective-permute-start.20) | collective-permute-done | bytes 147488 | tf_op jit(solution)/shard_map/ppermute | solution.py:314
  114.0 2.0 %collective-permute-done.19 = bf16[48,1536]{1,0:T(8,128)(2,1)S(1)} collective-permute-done((bf16[48,1536]{1,0:T(8,128)(2,1)S(1)}, bf16[48,1536]{1,0:T(8,128)(2,1)S(1)}, u32[]{:S(2)}, u32[]{:S(2)}) %collective-permute-start.19) | collective-permute-done | bytes 147488 | tf_op jit(solution)/shard_map/ppermute | solution.py:314
  116.0 3.3 %collective-permute-done.18 = bf16[48,1536]{1,0:T(8,128)(2,1)S(1)} collective-permute-done((bf16[48,1536]{1,0:T(8,128)(2,1)S(1)}, bf16[48,1536]{1,0:T(8,128)(2,1)S(1)}, u32[]{:S(2)}, u32[]{:S(2)}) %collective-permute-start.18) | collective-permute-done | bytes 147488 | tf_op jit(solution)/shard_map/ppermute | solution.py:314
  119.4 2.7 %collective-permute-start.23 = (bf16[4,48,1536]{2,1,0:T(8,128)(2,1)S(1)}, bf16[4,48,1536]{2,1,0:T(8,128)(2,1)S(1)}, u32[]{:S(2)}, u32[]{:S(2)}) collective-permute-start(bf16[4,48,1536]{2,1,0:T(8,128)(2,1)S(1)} %pad_maximum_fusion.part_ref), channel_id=1, source_target_pairs={{0,6},{1,7},{2,4},{3,5},{4,2},{5,3},{6,0},{7,1},{8,14},{9,15},{10,... | collective-permute-start | bytes 1769480 | tf_op jit(solution)/shard_map/ppermute | solution.py:314
  122.2 2.0 %collective-permute-start.21 = (bf16[4,48,1536]{2,1,0:T(8,128)(2,1)S(1)}, bf16[4,48,1536]{2,1,0:T(8,128)(2,1)S(1)}, u32[]{:S(2)}, u32[]{:S(2)}) collective-permute-start(bf16[4,48,1536]{2,1,0:T(8,128)(2,1)S(1)} %pad_maximum_fusion.part_ref), channel_id=1, source_target_pairs={{0,4},{1,5},{2,6},{3,7},{4,0},{5,1},{6,2},{7,3},{8,12},{9,13},{10,... | collective-permute-start | bytes 1769480 | tf_op jit(solution)/shard_map/ppermute | solution.py:314
  124.2 1.6 %shard_map.99.refs_0_ = f32[768,1536]{1,0:T(8,128)} custom-call(s32[12]{0:T(128)S(1)} %copy-done.6, bf16[4,48,1536]{2,1,0:T(8,128)(2,1)S(1)} %pad_maximum_fusion.part_ref), custom_call_target="tpu_custom_call" | custom-call | flops 1000000 | bytes 2000000 | tf_op jit(solution)/shard_map/pallas_call | solution.py:185
  125.8 1.0 add_bitcast_fusion
  126.8 3.8 %collective-permute-done.23.part_ref = bf16[4,48,1536]{2,1,0:T(8,128)(2,1)S(1)} collective-permute-done((bf16[4,48,1536]{2,1,0:T(8,128)(2,1)S(1)}, bf16[4,48,1536]{2,1,0:T(8,128)(2,1)S(1)}, u32[]{:S(2)}, u32[]{:S(2)}) %collective-permute-start.23) | collective-permute-done | bytes 589856 | tf_op jit(solution)/shard_map/ppermute | solution.py:314
  130.5 1.6 %shard_map.100.refs_0_ = f32[768,1536]{1,0:T(8,128)} custom-call(s32[12]{0:T(128)S(1)} %copy-done.6, bf16[4,48,1536]{2,1,0:T(8,128)(2,1)S(1)} %collective-permute-done.23.part_ref, f32[768,1536]{1,0:T(8,128)} %shard_map.99.refs_0_), custom_call_target="tpu_custom_call", output_to_operand_aliasing={{}: (2, {})} | custom-call | flops 1000000 | bytes 2000000 | tf_op jit(solution)/shard_map/pallas_call | solution.py:185
  132.2 1.6 %shard_map.101.refs_0_ = f32[768,1536]{1,0:T(8,128)} custom-call(s32[12]{0:T(128)S(1)} %copy-done.6, bf16[4,48,1536]{2,1,0:T(8,128)(2,1)S(1)} %collective-permute-done.22.part_ref, f32[768,1536]{1,0:T(8,128)} %shard_map.100.refs_0_), custom_call_target="tpu_custom_call", output_to_operand_aliasing={{}: (2, {})} | custom-call | flops 1000000 | bytes 2000000 | tf_op jit(solution)/shard_map/pallas_call | solution.py:185
  133.8 4.5 %collective-permute-done.21.part_ref = bf16[4,48,1536]{2,1,0:T(8,128)(2,1)S(1)} collective-permute-done((bf16[4,48,1536]{2,1,0:T(8,128)(2,1)S(1)}, bf16[4,48,1536]{2,1,0:T(8,128)(2,1)S(1)}, u32[]{:S(2)}, u32[]{:S(2)}) %collective-permute-start.21) | collective-permute-done | bytes 589856 | tf_op jit(solution)/shard_map/ppermute | solution.py:314
  138.3 1.6 %shard_map.102 = f32[768,1536]{1,0:T(8,128)} custom-call(s32[12]{0:T(128)S(1)} %copy-done.6, bf16[4,48,1536]{2,1,0:T(8,128)(2,1)S(1)} %collective-permute-done.21.part_ref, f32[768,1536]{1,0:T(8,128)} %shard_map.101.refs_0_), custom_call_target="tpu_custom_call", output_to_operand_aliasing={{}: (2, {})} | custom-call | flops 1000000 | bytes 2000000 | tf_op jit(solution)/shard_map/pallas_call | solution.py:185
  (46 shorter events, 2.8 us)
Async XLA Ops:
  0.6 11.7 %collective-permute-start.1 = (bf16[512,768]{1,0:T(8,128)(2,1)}, bf16[512,768]{1,0:T(8,128)(2,1)S(1)}, u32[]{:S(2)}, u32[]{:S(2)}) collective-permute-start(bf16[512,768]{1,0:T(8,128)(2,1)} %bitcast.44), channel_id=1, source_target_pairs={{0,64},{64,0},{1,65},{65,1},{2,66},{66,2},{3,67},{67,3},{4,68},{68... | collective-permute-start | bytes 2359304 | tf_op jit(solution)/shard_map/ppermute | solution.py:206
  0.7 30.5 %collective-permute-start = (bf16[512,768]{1,0:T(8,128)(2,1)}, bf16[512,768]{1,0:T(8,128)(2,1)S(1)}, u32[]{:S(2)}, u32[]{:S(2)}) collective-permute-start(bf16[512,768]{1,0:T(8,128)(2,1)} %bitcast.45), channel_id=1, source_target_pairs={{0,128},{128,0},{1,129},{129,1},{2,130},{130,2},{3,131},{131,3},{4... | collective-permute-start | bytes 2359304 | tf_op jit(solution)/shard_map/ppermute | solution.py:206
  2.9 63.8 %collective-permute-start.9 = (bf16[512,1536]{1,0:T(8,128)(2,1)}, bf16[512,1536]{1,0:T(8,128)(2,1)}, u32[]{:S(2)}, u32[]{:S(2)}) collective-permute-start(bf16[512,1536]{1,0:T(8,128)(2,1)} %bitcast.31), channel_id=1, source_target_pairs={{0,4},{1,5},{2,6},{3,7},{4,0},{5,1},{6,2},{7,3},{8,12},{9,13},{10,... | collective-permute-start | bytes 4718600 | tf_op jit(solution)/shard_map/ppermute | solution.py:314
  6.1 60.6 %collective-permute-start.8 = (bf16[512,1536]{1,0:T(8,128)(2,1)}, bf16[512,1536]{1,0:T(8,128)(2,1)}, u32[]{:S(2)}, u32[]{:S(2)}) collective-permute-start(bf16[512,1536]{1,0:T(8,128)(2,1)} %bitcast.32), channel_id=1, source_target_pairs={{0,2},{1,3},{2,0},{3,1},{4,6},{5,7},{6,4},{7,5},{8,10},{9,11},{10,... | collective-permute-start | bytes 4718600 | tf_op jit(solution)/shard_map/ppermute | solution.py:314
  6.8 59.9 %collective-permute-start.7 = (bf16[512,1536]{1,0:T(8,128)(2,1)}, bf16[512,1536]{1,0:T(8,128)(2,1)}, u32[]{:S(2)}, u32[]{:S(2)}) collective-permute-start(bf16[512,1536]{1,0:T(8,128)(2,1)} %bitcast.33), channel_id=1, source_target_pairs={{0,6},{1,7},{2,4},{3,5},{4,2},{5,3},{6,0},{7,1},{8,14},{9,15},{10,... | collective-permute-start | bytes 4718600 | tf_op jit(solution)/shard_map/ppermute | solution.py:314
  12.3 0.9 copy-start.9
  31.2 5.5 %copy-start.7 = (bf16[512,768]{1,0:T(8,128)(2,1)}, bf16[512,768]{1,0:T(8,128)(2,1)S(1)}, u32[]{:S(2)}) copy-start(bf16[512,768]{1,0:T(8,128)(2,1)S(1)} %collective-permute-done.own_ref) | copy-start | bytes 2359300
  31.2 4.6 %collective-permute-start.2 = (bf16[512,768]{1,0:T(8,128)(2,1)S(1)}, bf16[512,768]{1,0:T(8,128)(2,1)S(1)}, u32[]{:S(2)}, u32[]{:S(2)}) collective-permute-start(bf16[512,768]{1,0:T(8,128)(2,1)S(1)} %collective-permute-done.own_ref), channel_id=1, source_target_pairs={{0,64},{64,0},{1,65},{65,1},{2,66},{66,2},{3,67},{67,3},{4,68},{68... | collective-permute-start | bytes 2359304 | tf_op jit(solution)/shard_map/ppermute | solution.py:206
  35.8 0.9 copy-start.8
  36.7 26.1 %copy-start = (bf16[768,1536]{1,0:T(8,128)(2,1)S(1)}, bf16[768,1536]{1,0:T(8,128)(2,1)}, u32[]{:S(2)}) copy-start(bf16[768,1536]{1,0:T(8,128)(2,1)} %w_ref.5) | copy-start | bytes 7077892
  36.7 26.1 %copy-start.6 = (s32[12]{0:T(128)S(1)}, s32[12]{0:T(128)}, u32[]{:S(2)}) copy-start(s32[12]{0:T(128)} %concatenate.3.place_ref) | copy-start | bytes 148
  53.6 13.4 %copy-start.1 = (bf16[1,512,1536]{2,1,0:T(8,128)(2,1)S(1)}, bf16[1,512,1536]{2,1,0:T(8,128)(2,1)}, u32[]{:S(2)}) copy-start(bf16[1,512,1536]{2,1,0:T(8,128)(2,1)} %param.11) | copy-start | bytes 4718596
  53.6 7.5 %collective-permute-start.3 = (bf16[192,512]{1,0:T(8,128)(2,1)}, bf16[192,512]{1,0:T(8,128)(2,1)S(1)}, u32[]{:S(2)}, u32[]{:S(2)}) collective-permute-start(bf16[192,512]{1,0:T(8,128)(2,1)} %get-tuple-element.31), channel_id=1, source_target_pairs={{0,4},{1,5},{2,6},{3,7},{4,0},{5,1},{6,2},{7,3},{8,12},{9,13},{10,... | collective-permute-start | bytes 589832 | tf_op jit(solution)/shard_map/ppermute | solution.py:314
  56.9 9.8 %collective-permute-start.5 = (bf16[192,512]{1,0:T(8,128)(2,1)}, bf16[192,512]{1,0:T(8,128)(2,1)S(1)}, u32[]{:S(2)}, u32[]{:S(2)}) collective-permute-start(bf16[192,512]{1,0:T(8,128)(2,1)} %get-tuple-element.37), channel_id=1, source_target_pairs={{0,6},{1,7},{2,4},{3,5},{4,2},{5,3},{6,0},{7,1},{8,14},{9,15},{10,... | collective-permute-start | bytes 589832 | tf_op jit(solution)/shard_map/ppermute | solution.py:314
  61.1 5.9 %collective-permute-start.6 = (bf16[192,512]{1,0:T(8,128)(2,1)}, bf16[192,512]{1,0:T(8,128)(2,1)S(1)}, u32[]{:S(2)}, u32[]{:S(2)}) collective-permute-start(bf16[192,512]{1,0:T(8,128)(2,1)} %get-tuple-element.38), channel_id=1, source_target_pairs={{0,2},{1,3},{2,0},{3,1},{4,6},{5,7},{6,4},{7,5},{8,10},{9,11},{10,... | collective-permute-start | bytes 589832 | tf_op jit(solution)/shard_map/ppermute | solution.py:314
  62.8 1.1 copy-start.2
  63.9 3.1 %copy-start.5 = (bf16[192,512]{1,0:T(8,128)(2,1)S(1)}, bf16[192,512]{1,0:T(8,128)(2,1)}, u32[]{:S(2)}) copy-start(bf16[192,512]{1,0:T(8,128)(2,1)} %get-tuple-element.36.refs_0_) | copy-start | bytes 589828
  66.7 22.9 %collective-permute-start.4 = (bf16[512,768]{1,0:T(8,128)(2,1)}, bf16[512,768]{1,0:T(8,128)(2,1)}, u32[]{:S(2)}, u32[]{:S(2)}) collective-permute-start(bf16[512,768]{1,0:T(8,128)(2,1)} %shard_map.96), channel_id=1, source_target_pairs={{0,64},{64,0},{1,65},{65,1},{2,66},{66,2},{3,67},{67,3},{4,68},{68... | collective-permute-start | bytes 2359304 | tf_op jit(solution)/shard_map/ppermute | solution.py:206
  67.0 22.7 %copy-start.3 = (bf16[512,768]{1,0:T(8,128)(2,1)S(1)}, bf16[512,768]{1,0:T(8,128)(2,1)}, u32[]{:S(2)}) copy-start(bf16[512,768]{1,0:T(8,128)(2,1)} %get-tuple-element.30.attn_ref) | copy-start | bytes 2359300
  72.8 6.8 %collective-permute-start.10 = (bf16[48,1536]{1,0:T(8,128)(2,1)S(1)}, bf16[48,1536]{1,0:T(8,128)(2,1)S(1)}, u32[]{:S(2)}, u32[]{:S(2)}) collective-permute-start(bf16[48,1536]{1,0:T(8,128)(2,1)S(1)} %get-tuple-element.41), channel_id=1, source_target_pairs={{0,56},{1,57},{2,58},{3,59},{4,60},{5,61},{6,62},{7,63},{8,16},{9,... | collective-permute-start | bytes 442376 | tf_op jit(solution)/shard_map/ppermute | solution.py:314
  76.5 5.1 %collective-permute-start.11 = (bf16[48,1536]{1,0:T(8,128)(2,1)S(1)}, bf16[48,1536]{1,0:T(8,128)(2,1)S(1)}, u32[]{:S(2)}, u32[]{:S(2)}) collective-permute-start(bf16[48,1536]{1,0:T(8,128)(2,1)S(1)} %get-tuple-element.42), channel_id=1, source_target_pairs={{0,8},{1,9},{2,10},{3,11},{4,12},{5,13},{6,14},{7,15},{8,0},{9,1},... | collective-permute-start | bytes 442376 | tf_op jit(solution)/shard_map/ppermute | solution.py:314
  76.5 7.3 %collective-permute-start.12 = (bf16[48,1536]{1,0:T(8,128)(2,1)S(1)}, bf16[48,1536]{1,0:T(8,128)(2,1)S(1)}, u32[]{:S(2)}, u32[]{:S(2)}) collective-permute-start(bf16[48,1536]{1,0:T(8,128)(2,1)S(1)} %get-tuple-element.43), channel_id=1, source_target_pairs={{0,16},{1,17},{2,18},{3,19},{4,20},{5,21},{6,22},{7,23},{8,56},{9,... | collective-permute-start | bytes 442376 | tf_op jit(solution)/shard_map/ppermute | solution.py:314
  83.8 12.0 %collective-permute-start.15 = (bf16[48,1536]{1,0:T(8,128)(2,1)S(1)}, bf16[48,1536]{1,0:T(8,128)(2,1)S(1)}, u32[]{:S(2)}, u32[]{:S(2)}) collective-permute-start(bf16[48,1536]{1,0:T(8,128)(2,1)S(1)} %add_convert_fusion.2), channel_id=1, source_target_pairs={{0,128},{1,129},{2,130},{3,131},{4,132},{5,133},{6,134},{7,135},{8... | collective-permute-start | bytes 442376 | tf_op jit(solution)/shard_map/ppermute | solution.py:314
  85.3 10.5 %collective-permute-start.14 = (bf16[48,1536]{1,0:T(8,128)(2,1)S(1)}, bf16[48,1536]{1,0:T(8,128)(2,1)}, u32[]{:S(2)}, u32[]{:S(2)}) collective-permute-start(bf16[48,1536]{1,0:T(8,128)(2,1)S(1)} %add_convert_fusion.2), channel_id=1, source_target_pairs={{0,129},{1,128},{2,131},{3,130},{4,133},{5,132},{6,135},{7,134},{8... | collective-permute-start | bytes 442376 | tf_op jit(solution)/shard_map/ppermute | solution.py:314
  86.8 9.0 %collective-permute-start.13 = (bf16[48,1536]{1,0:T(8,128)(2,1)S(1)}, bf16[48,1536]{1,0:T(8,128)(2,1)}, u32[]{:S(2)}, u32[]{:S(2)}) collective-permute-start(bf16[48,1536]{1,0:T(8,128)(2,1)S(1)} %add_convert_fusion.2), channel_id=1, source_target_pairs={{0,1},{1,0},{2,3},{3,2},{4,5},{5,4},{6,7},{7,6},{8,9},{9,8},{10,11... | collective-permute-start | bytes 442376 | tf_op jit(solution)/shard_map/ppermute | solution.py:314
  89.6 1.0 copy-start.4
  96.9 9.7 %collective-permute-start.17 = (bf16[48,1536]{1,0:T(8,128)(2,1)S(1)}, bf16[48,1536]{1,0:T(8,128)(2,1)S(1)}, u32[]{:S(2)}, u32[]{:S(2)}) collective-permute-start(bf16[48,1536]{1,0:T(8,128)(2,1)S(1)} %add_convert_fusion.1), channel_id=1, source_target_pairs={{0,32},{1,33},{2,34},{3,35},{4,36},{5,37},{6,38},{7,39},{8,40},{9,... | collective-permute-start | bytes 442376 | tf_op jit(solution)/shard_map/ppermute | solution.py:314
  100.5 25.3 %collective-permute-start.16 = (bf16[512,768]{1,0:T(8,128)(2,1)S(1)}, bf16[512,768]{1,0:T(8,128)(2,1)S(1)}, u32[]{:S(2)}, u32[]{:S(2)}) collective-permute-start(bf16[512,768]{1,0:T(8,128)(2,1)S(1)} %get-tuple-element.47), channel_id=1, source_target_pairs={{0,128},{128,0},{1,129},{129,1},{2,130},{130,2},{3,131},{131,3},{4... | collective-permute-start | bytes 2359304 | tf_op jit(solution)/shard_map/ppermute | solution.py:206
  106.7 7.3 %collective-permute-start.20 = (bf16[48,1536]{1,0:T(8,128)(2,1)S(1)}, bf16[48,1536]{1,0:T(8,128)(2,1)S(1)}, u32[]{:S(2)}, u32[]{:S(2)}) collective-permute-start(bf16[48,1536]{1,0:T(8,128)(2,1)S(1)} %add_convert_fusion), channel_id=1, source_target_pairs={{0,16},{1,17},{2,18},{3,19},{4,20},{5,21},{6,22},{7,23},{8,56},{9,... | collective-permute-start | bytes 442376 | tf_op jit(solution)/shard_map/ppermute | solution.py:314
  107.5 8.5 %collective-permute-start.19 = (bf16[48,1536]{1,0:T(8,128)(2,1)S(1)}, bf16[48,1536]{1,0:T(8,128)(2,1)S(1)}, u32[]{:S(2)}, u32[]{:S(2)}) collective-permute-start(bf16[48,1536]{1,0:T(8,128)(2,1)S(1)} %add_convert_fusion), channel_id=1, source_target_pairs={{0,8},{1,9},{2,10},{3,11},{4,12},{5,13},{6,14},{7,15},{8,0},{9,1},... | collective-permute-start | bytes 442376 | tf_op jit(solution)/shard_map/ppermute | solution.py:314
  111.3 8.0 %collective-permute-start.18 = (bf16[48,1536]{1,0:T(8,128)(2,1)S(1)}, bf16[48,1536]{1,0:T(8,128)(2,1)S(1)}, u32[]{:S(2)}, u32[]{:S(2)}) collective-permute-start(bf16[48,1536]{1,0:T(8,128)(2,1)S(1)} %add_convert_fusion), channel_id=1, source_target_pairs={{0,56},{1,57},{2,58},{3,59},{4,60},{5,61},{6,62},{7,63},{8,16},{9,... | collective-permute-start | bytes 442376 | tf_op jit(solution)/shard_map/ppermute | solution.py:314
  119.4 11.2 %collective-permute-start.23 = (bf16[4,48,1536]{2,1,0:T(8,128)(2,1)S(1)}, bf16[4,48,1536]{2,1,0:T(8,128)(2,1)S(1)}, u32[]{:S(2)}, u32[]{:S(2)}) collective-permute-start(bf16[4,48,1536]{2,1,0:T(8,128)(2,1)S(1)} %pad_maximum_fusion.part_ref), channel_id=1, source_target_pairs={{0,6},{1,7},{2,4},{3,5},{4,2},{5,3},{6,0},{7,1},{8,14},{9,15},{10,... | collective-permute-start | bytes 1769480 | tf_op jit(solution)/shard_map/ppermute | solution.py:314
  122.1 10.1 %collective-permute-start.22 = (bf16[4,48,1536]{2,1,0:T(8,128)(2,1)S(1)}, bf16[4,48,1536]{2,1,0:T(8,128)(2,1)S(1)}, u32[]{:S(2)}, u32[]{:S(2)}) collective-permute-start(bf16[4,48,1536]{2,1,0:T(8,128)(2,1)S(1)} %pad_maximum_fusion.part_ref), channel_id=1, source_target_pairs={{0,2},{1,3},{2,0},{3,1},{4,6},{5,7},{6,4},{7,5},{8,10},{9,11},{10,... | collective-permute-start | bytes 1769480 | tf_op jit(solution)/shard_map/ppermute | solution.py:314
  122.2 16.1 %collective-permute-start.21 = (bf16[4,48,1536]{2,1,0:T(8,128)(2,1)S(1)}, bf16[4,48,1536]{2,1,0:T(8,128)(2,1)S(1)}, u32[]{:S(2)}, u32[]{:S(2)}) collective-permute-start(bf16[4,48,1536]{2,1,0:T(8,128)(2,1)S(1)} %pad_maximum_fusion.part_ref), channel_id=1, source_target_pairs={{0,4},{1,5},{2,6},{3,7},{4,0},{5,1},{6,2},{7,3},{8,12},{9,13},{10,... | collective-permute-start | bytes 1769480 | tf_op jit(solution)/shard_map/ppermute | solution.py:314

commit v5 on v4

--- a/solution.py
+++ b/solution.py
@@ -19,39 +19,26 @@
 BF = jnp.bfloat16
 F32 = jnp.float32
 VMEM_LIMIT = 20 * 1024 * 1024
-FULL_VMEM = 60 * 1024 * 1024
-
-
-def norm_rows(head, own_ref, oth_ref, normed_ref, rows):
-    share = own_ref.shape[1]
-    step = 64
-
-    def one(i, carry):
-        at = pl.ds(pl.multiple_of(i * step, step), step)
-        own = own_ref[at, :].astype(F32)
-        oth = oth_ref[at, :].astype(F32)
-        inv = 1.0 / (2 * share)
-        mean = (jnp.sum(own, axis=1, keepdims=True) + jnp.sum(oth, axis=1, keepdims=True)) * inv
-        own = own - mean
-        oth = oth - mean
-        var = (jnp.sum(own * own, axis=1, keepdims=True) + jnp.sum(oth * oth, axis=1, keepdims=True)) * inv
-        scale = lax.rsqrt(var + EPS_NORM)
-        own = (own * scale).astype(BF)
-        oth = (oth * scale).astype(BF)
-
-        @pl.when(head == 0)
-        def _():
-            normed_ref[at, :share] = own
-            normed_ref[at, share:] = oth
-
-        @pl.when(head != 0)
-        def _():
-            normed_ref[at, :share] = oth
-            normed_ref[at, share:] = own
-
-        return carry
-
-    lax.fori_loop(0, rows // step, one, 0)
+BIG_VMEM = 60 * 1024 * 1024
+
+
+def norm_rows(head, own_ref, oth_ref, normed_ref):
+    rows, share = own_ref.shape
+    step = 128
+    one = jnp.ones((share, 128), BF)
+    row_sum = lambda a, b: jnp.dot(a, one, preferred_element_type=F32) + jnp.dot(b, one, preferred_element_type=F32)
+    wide = lambda value: jnp.concatenate([value] * (share // 128), axis=1)
+    own_at = pl.ds(pl.multiple_of(head * share, share), share)
+    oth_at = pl.ds(pl.multiple_of((1 - head) * share, share), share)
+    for i in range(0, rows, step):
+        at = slice(i, i + step)
+        mean = wide(row_sum(own_ref[at, :], oth_ref[at, :]) * (0.5 / share))
+        own = own_ref[at, :].astype(F32) - mean
+        oth = oth_ref[at, :].astype(F32) - mean
+        var = row_sum((own * own).astype(BF), (oth * oth).astype(BF)) * (0.5 / share)
+        scale = wide(lax.rsqrt(var + EPS_NORM))
+        normed_ref[at, own_at] = (own * scale).astype(BF)
+        normed_ref[at, oth_at] = (oth * scale).astype(BF)
 
 
 def head_norm(values, ones):
@@ -60,8 +47,8 @@
 
 
 def ones_block():
-    row = lax.broadcasted_iota(jnp.int32, (GROUP, GROUP), 0) // HD
-    col = lax.broadcasted_iota(jnp.int32, (GROUP, GROUP), 1) // HD
+    row = lax.broadcasted_iota(jnp.int32, (GROUP, GROUP), 0) >> 6
+    col = lax.broadcasted_iota(jnp.int32, (GROUP, GROUP), 1) >> 6
     return jnp.where(row == col, 1.0 / HD, 0.0).astype(BF)
 
 
@@ -84,10 +71,9 @@
 
 
 def attend_group(q, k, v, qfeat, kfeat, emit):
-    q = (q.astype(F32) * 0.125).astype(BF)
     for pair in range(2):
         lanes = slice(pair * 128, pair * 128 + 128)
-        qp, kp, vp = q[:, lanes], k[:, lanes], v[:, lanes]
+        qp, kp, vp = (q(lanes).astype(F32) * 0.125).astype(BF), k(lanes), v(lanes)
         qlow, klow = lower_half(qp.shape[0]), lower_half(kp.shape[0])
         one = jnp.ones_like(vp)
         for odd in range(2):
@@ -99,72 +85,98 @@
             emit(2 * pair + odd, jnp.dot(w, va, preferred_element_type=F32))
 
 
-def local_kernel(place_ref, own_ref, oth_ref, w_ref, q_ref, acc_ref, normed_ref, qf_ref, kf_ref, ones_ref):
+def local_kernel(place_ref, own_ref, oth_ref, w_ref, q_ref, acc_ref, normed_ref, qf_ref, kf_ref, wbuf_ref, qbuf_ref, abuf_ref, k_ref, v_ref, sems):
     rows = own_ref.shape[0]
-
-    @pl.when(pl.program_id(0) == 0)
-    def _():
-        norm_rows(place_ref[1], own_ref, oth_ref, normed_ref, rows)
-        first = place_ref[0] * rows
-        qf_ref[...] = features(place_ref, first, rows, BIG, -BIG)
-        kf_ref[...] = features(place_ref, first, rows, 1.0, 1.0)
-        ones_ref[...] = ones_block()
-
-    normed = normed_ref[...]
-    ones = ones_ref[...]
-    q = head_norm(jnp.dot(normed, w_ref[0], preferred_element_type=F32), ones).astype(BF)
-    k = head_norm(jnp.dot(normed, w_ref[1], preferred_element_type=F32), ones).astype(BF)
-    v = jnp.dot(normed, w_ref[2], preferred_element_type=F32).astype(BF)
-    q_ref[...] = q
-
-    def emit(head, r):
-        acc_ref[:, head * 128 : head * 128 + 128] = r
-
-    attend_group(q, k, v, qf_ref[...], kf_ref[...], emit)
-
-
-def foreign_kernel(place_ref, own_ref, oth_ref, wk_ref, wv_ref, q_ref, acc_in_ref, attn_ref, t0_ref, t1_ref, t2_ref, t3_ref, normed_ref, qf_ref, kf_ref, ones_ref, k_ref, v_ref, acc_ref, turned_ref):
+    groups = wbuf_ref.shape[0]
+    loads = [
+        pltpu.make_async_copy(w_ref.at[:, :, g * GROUP : g * GROUP + GROUP], wbuf_ref.at[g], sems.at[g])
+        for g in range(groups)
+    ]
+    for load in loads:
+        load.start()
+    norm_rows(place_ref[1], own_ref, oth_ref, normed_ref)
+    first = place_ref[0] * rows
+    qf_ref[...] = features(place_ref, first, rows, BIG, -BIG)
+    kf_ref[...] = features(place_ref, first, rows, 1.0, 1.0)
+    ones = ones_block()
+    stores = []
+    for g in range(groups):
+        loads[g].wait()
+        normed = normed_ref[...]
+        qbuf_ref[g] = head_norm(jnp.dot(normed, wbuf_ref[g, 0], preferred_element_type=F32), ones).astype(BF)
+        k_ref[...] = head_norm(jnp.dot(normed, wbuf_ref[g, 1], preferred_element_type=F32), ones).astype(BF)
+        v_ref[...] = jnp.dot(normed, wbuf_ref[g, 2], preferred_element_type=F32).astype(BF)
+        stores.append(pltpu.make_async_copy(qbuf_ref.at[g], q_ref.at[g], sems.at[groups + g]))
+        stores[-1].start()
+
+        def emit(head, r):
+            abuf_ref[g, :, head * 128 : head * 128 + 128] = r.astype(BF)
+
+        attend_group(
+            lambda lanes: qbuf_ref[g, :, lanes], lambda lanes: k_ref[:, lanes], lambda lanes: v_ref[:, lanes],
+            qf_ref[...], kf_ref[...], emit,
+        )
+        stores.append(pltpu.make_async_copy(abuf_ref.at[g], acc_ref.at[g], sems.at[2 * groups + g]))
+        stores[-1].start()
+    for store in stores:
+        store.wait()
+
+
+def foreign_kernel(place_ref, own_ref, oth_ref, w_ref, q_ref, acc_ref, attn_ref, t0_ref, t1_ref, t2_ref, t3_ref, normed_ref, qf_ref, kf_ref, wbuf_ref, qbuf_ref, abuf_ref, k_ref, v_ref, sum_ref, turned_ref, sems):
     rows = own_ref.shape[0]
     half = rows // 2
-
-    @pl.when(pl.program_id(0) == 0)
-    def _():
-        norm_rows(place_ref[1], own_ref, oth_ref, normed_ref, rows)
-        qf_ref[...] = features(place_ref, place_ref[0] * rows, rows, BIG, -BIG)
-        kf_ref[...] = features(place_ref, (1 - place_ref[0]) * rows, rows, 1.0, 1.0)
-        ones_ref[...] = ones_block()
-
-    normed = normed_ref[...]
-    k_ref[...] = head_norm(jnp.dot(normed, wk_ref[0], preferred_element_type=F32), ones_ref[...]).astype(BF)
-    v_ref[...] = jnp.dot(normed, wv_ref[0], preferred_element_type=F32).astype(BF)
+    groups = wbuf_ref.shape[0]
+    loads = []
+    for g in range(groups):
+        lanes = slice(g * GROUP, g * GROUP + GROUP)
+        loads.append([
+            pltpu.make_async_copy(w_ref.at[1:3, :, lanes], wbuf_ref.at[g], sems.at[g]),
+            pltpu.make_async_copy(q_ref.at[g], qbuf_ref.at[g], sems.at[groups + g]),
+            pltpu.make_async_copy(acc_ref.at[g], abuf_ref.at[g], sems.at[2 * groups + g]),
+        ])
+        for load in loads[-1]:
+            load.start()
+    norm_rows(place_ref[1], own_ref, oth_ref, normed_ref)
+    qf_ref[...] = features(place_ref, place_ref[0] * rows, rows, BIG, -BIG)
+    kf_ref[...] = features(place_ref, (1 - place_ref[0]) * rows, rows, 1.0, 1.0)
+    ones = ones_block()
     near = pl.ds(pl.multiple_of(place_ref[0] * half, half), half)
     far = pl.ds(pl.multiple_of((1 - place_ref[0]) * half, half), half)
-
-    def emit_near(head, r):
-        lanes = slice(head * 128, head * 128 + 128)
-        acc_ref[:, lanes] = acc_in_ref[:, lanes] + r
-
-    attend_group(q_ref[...], k_ref[near, :], v_ref[near, :], qf_ref[...], kf_ref[near, :], emit_near)
-
-    def emit_far(head, r):
-        lanes = slice(head * 128, head * 128 + 128)
-        acc_ref[far, lanes] = acc_ref[far, lanes] + r
-
-    attend_group(q_ref[far, :], k_ref[far, :], v_ref[far, :], qf_ref[far, :], kf_ref[far, :], emit_far)
     low = lower_half(rows)
-    for pair in range(2):
-        even = acc_ref[:, pair * 256 : pair * 256 + 128]
-        odd = acc_ref[:, pair * 256 + 128 : pair * 256 + 256]
-        total = pltpu.roll(jnp.where(low, odd, even), HD, 1)
-        attn_ref[:, pair * 128 : pair * 128 + 128] = (jnp.where(low, even, odd) / total).astype(BF)
-    group = pl.program_id(0)
-    turned_ref[pl.ds(pl.multiple_of(group * GROUP, GROUP), GROUP), :] = attn_ref[...].T
-
-    @pl.when(group == pl.num_programs(0) - 1)
-    def _():
-        for i, out in enumerate((t0_ref, t1_ref, t2_ref, t3_ref)):
-            part = out.shape[0]
-            out[...] = turned_ref[pl.ds(pl.multiple_of((i ^ place_ref[2]) * part, part), part), :]
+    for g in range(groups):
+        for load in loads[g]:
+            load.wait()
+        normed = normed_ref[...]
+        k_ref[...] = head_norm(jnp.dot(normed, wbuf_ref[g, 0], preferred_element_type=F32), ones).astype(BF)
+        v_ref[...] = jnp.dot(normed, wbuf_ref[g, 1], preferred_element_type=F32).astype(BF)
+
+        def emit_near(head, r):
+            lanes = slice(head * 128, head * 128 + 128)
+            sum_ref[:, lanes] = abuf_ref[g, :, lanes].astype(F32) + r
+
+        def emit_far(head, r):
+            lanes = slice(head * 128, head * 128 + 128)
+            sum_ref[far, lanes] = sum_ref[far, lanes] + r
+
+        attend_group(
+            lambda lanes: qbuf_ref[g, :, lanes], lambda lanes: k_ref[near, lanes], lambda lanes: v_ref[near, lanes],
+            qf_ref[...], kf_ref[near, :], emit_near,
+        )
+        attend_group(
+            lambda lanes: qbuf_ref[g, far, lanes], lambda lanes: k_ref[far, lanes], lambda lanes: v_ref[far, lanes],
+            qf_ref[far, :], kf_ref[far, :], emit_far,
+        )
+        for pair in range(2):
+            even = sum_ref[:, pair * 256 : pair * 256 + 128]
+            odd = sum_ref[:, pair * 256 + 128 : pair * 256 + 256]
+            total = pltpu.roll(jnp.where(low, odd, even), HD, 1)
+            first = g * GROUP + pair * 128
+            attn = (jnp.where(low, even, odd) / total).astype(BF)
+            attn_ref[:, first : first + 128] = attn
+            turned_ref[first : first + 128, :] = attn.T
+    for i, out in enumerate((t0_ref, t1_ref, t2_ref, t3_ref)):
+        part = out.shape[0]
+        out[...] = turned_ref[pl.ds(pl.multiple_of((i ^ place_ref[2]) * part, part), part), :]
 
 
 def send_kernel(place_ref, attn_ref, w_ref, out_ref):
@@ -345,8 +357,6 @@
     seq = lax.axis_index("seq")
     head = lax.axis_index("head")
     sizes = lengths[0]
-    ends = jnp.cumsum(sizes, dtype=jnp.int32)
-    starts = ends - sizes
     place = jnp.concatenate([jnp.stack([seq, head, mask_of(0, head), mask_of(1, head)]).astype(jnp.int32), sizes])
 
     oth = swap(own, "head")
@@ -355,6 +365,36 @@
     first, second = quad_tables(devices, 0), quad_tables(devices, 1)
     cots = [cotangent[0]] + [move(cotangent[0], table) for table in first]
 
+    anywhere = pl.BlockSpec(memory_space=pl.ANY)
+    scratch = lambda projections: [
+        pltpu.VMEM((rows, 2 * share), BF),
+        pltpu.VMEM((rows, 128), BF),
+        pltpu.VMEM((rows, 128), BF),
+        pltpu.VMEM((groups, projections, 2 * share, GROUP), BF),
+        pltpu.VMEM((groups, rows, GROUP), BF),
+        pltpu.VMEM((groups, rows, 2 * GROUP), BF),
+        pltpu.VMEM((rows, GROUP), BF),
+        pltpu.VMEM((rows, GROUP), BF),
+    ]
+    q, acc = call(
+        local_kernel, place, (1,), [whole((rows, share)), whole((rows, share)), anywhere], [anywhere] * 2,
+        [jax.ShapeDtypeStruct((groups, rows, GROUP), BF), jax.ShapeDtypeStruct((groups, rows, 2 * GROUP), BF)],
+        scratch(3) + [pltpu.SemaphoreType.DMA((3 * groups,))], 10**8, 10**6, (own, oth, qkv_weight), limit=BIG_VMEM,
+    )
+    foreign_own, q, cots[1], cots[2] = lax.optimization_barrier((foreign_own, q, cots[1], cots[2]))
+    foreign_oth = swap(foreign_own, "head")
+    quarter = whole((share // 4, rows))
+    attn, *turned = call(
+        foreign_kernel, place, (1,), [whole((rows, share)), whole((rows, share))] + [anywhere] * 3,
+        [whole((rows, share))] + [quarter] * 4,
+        [jax.ShapeDtypeStruct((rows, share), BF)] + [jax.ShapeDtypeStruct((share // 4, rows), BF)] * 4,
+        scratch(2)
+        + [pltpu.VMEM((rows, 2 * GROUP), F32), pltpu.VMEM((share, rows), BF), pltpu.SemaphoreType.DMA((3 * groups,))],
+        10**9, 10**6, (foreign_own, foreign_oth, qkv_weight, q, acc), limit=BIG_VMEM,
+    )
+    attn, latent_index, sizes, owner_slot = lax.optimization_barrier((attn, latent_index, sizes, owner_slot))
+    ends = jnp.cumsum(sizes, dtype=jnp.int32)
+    starts = ends - sizes
     slots = owner_slot[0]
     picks = starts[:, None] + jnp.remainder(latent_index[0], sizes[:, None])
     order = slots[None, :] == jnp.arange(IMAGES, dtype=jnp.int32)[:, None]
@@ -363,40 +403,12 @@
     local = jnp.stack([jnp.where(seq == 0, local[1], local[0]), jnp.where(seq == 0, local[0], local[1])])
     local = local.reshape(2 * rows, 1)
 
-    scratch = lambda r, qr, kr: [
-        pltpu.VMEM((r, 2 * share), BF),
-        pltpu.VMEM((qr, 128), BF),
-        pltpu.VMEM((kr, 128), BF),
-        pltpu.VMEM((GROUP, GROUP), BF),
-    ]
-    weight = lambda j: pl.BlockSpec((1, 2 * share, GROUP), lambda g, s: (j, 0, g))
-    q, acc = call(
-        local_kernel, place, (groups,),
-        [whole((rows, share)), whole((rows, share)),
-         pl.BlockSpec((3, 2 * share, GROUP), lambda g, s: (0, 0, g))],
-        [columns(rows, GROUP), columns(rows, 2 * GROUP)],
-        [jax.ShapeDtypeStruct((rows, share), BF), jax.ShapeDtypeStruct((rows, 2 * share), F32)],
-        scratch(rows, rows, rows), 7 * 10**9, 12 * 10**6, (own, oth, qkv_weight), limit=FULL_VMEM,
-    )
-    foreign_own, q, local = lax.optimization_barrier((foreign_own, q, local))
-    foreign_oth = swap(foreign_own, "head")
-    quarter = whole((share // 4, rows))
-    attn, *turned = call(
-        foreign_kernel, place, (groups,),
-        [whole((rows, share)), whole((rows, share)), weight(1), weight(2), columns(rows, GROUP), columns(rows, 2 * GROUP)],
-        [columns(rows, GROUP)] + [quarter] * 4,
-        [jax.ShapeDtypeStruct((rows, share), BF)] + [jax.ShapeDtypeStruct((share // 4, rows), BF)] * 4,
-        scratch(rows, rows, rows)
-        + [pltpu.VMEM((rows, GROUP), BF), pltpu.VMEM((rows, GROUP), BF), pltpu.VMEM((rows, 2 * GROUP), F32),
-           pltpu.VMEM((share, rows), BF)],
-        4 * 10**9, 14 * 10**6, (foreign_own, foreign_oth, qkv_weight, qkv_weight, q, acc), limit=FULL_VMEM,
-    )
     lefts = [turned[0]] + [move(t, table) for t, table in zip(turned[1:], first)]
 
     partial = call(
         send_kernel, place, (groups,),
         [whole((rows, share)), pl.BlockSpec((share, GROUP), lambda g, s: (0, (1 - s[1]) * groups + g))],
-        columns(rows, GROUP), jax.ShapeDtypeStruct((rows, share), BF), [], 6 * 10**8, 3 * 10**6, (attn, out_weight),
+        columns(rows, GROUP), jax.ShapeDtypeStruct((rows, share), BF), [], 6 * 10**8, 3 * 10**6, (attn, out_weight), limit=BIG_VMEM,
     )
     lefts[3], partial = lax.optimization_barrier((lefts[3], partial))
     recv = swap(partial, "head")

time: 140 us -> 132 us (0.943)
  waiting for transfers between devices: 32.2 us -> 27.1 us
  other arithmetic: 6 us -> 2.73 us
    ppermute x19, waiting for transfers between devices: 30.3 us -> 26.6 us  [move(): return lax.ppermute(value, AXES, table)]
    ppermute x5, waiting for transfers between devices: 1.92 us -> 0.51 us  [swap(): return lax.ppermute(value, axis, [(0, 1), (1, 0)])]
    unnamed x21 -> x26, local copies, waits for them, and re-layouts: 3.96 us -> 4.92 us
  transfers between devices with their start and end apart: 24 -> 24, of which waited for: 12 -> 11; matrix products, arithmetic and copies ran while one was open for 5% -> 3% of each run, Pallas kernels for 38% -> 36%
where the time goes in v5:
time: 132 us; the launch traced here: 131 us
  Pallas kernels  54.3 us (41%)
  starting transfers between devices  40.1 us (30%)
  waiting for transfers between devices  27.1 us (21%)
  local copies, waits for them, and re-layouts  6.2 us (5%)
  other arithmetic  2.73 us (2%)
    pallas_call x9, Pallas kernels, call(): pl.pallas_call(kernel, grid_spec=pltpu.PrefetchScalarGridSpec(num_scalar_...  54.3 us
    ppermute x19, starting transfers between devices, move(): return lax.ppermute(value, AXES, table)  34.6 us
    ppermute x19, waiting for transfers between devices, move(): return lax.ppermute(value, AXES, table)  26.6 us
    ppermute x5, starting transfers between devices, swap(): return lax.ppermute(value, axis, [(0, 1), (1, 0)])  5.54 us
    unnamed x26, local copies, waits for them, and re-layouts  4.92 us
  transfers between devices with their start and end apart: 24, of which 11 were waited for; matrix products, arithmetic and copies ran while one was open for 3% of the time, Pallas kernels for 36%

profile of v5, /device:TPU:2, one launch (start us, length us, event | category | flops | bytes accessed | tf_op | source)
XLA Modules:
  0.0 131.3 jit_solution(3523561279156710174)
XLA Ops:
  0.6 1.7 %collective-permute-start.3 = (bf16[512,1536]{1,0:T(8,128)(2,1)}, bf16[512,1536]{1,0:T(8,128)(2,1)S(1)}, u32[]{:S(2)}, u32[]{:S(2)}) collective-permute-start(bf16[512,1536]{1,0:T(8,128)(2,1)} %bitcast.27), channel_id=1, source_target_pairs={{0,2},{1,3},{2,0},{3,1},{4,6},{5,7},{6,4},{7,5},{8,10},{9,11},{10,... | collective-permute-start | bytes 4718600 | tf_op jit(solution)/shard_map/ppermute | solution.py:326
  2.3 2.2 %collective-permute-start.2 = (bf16[512,1536]{1,0:T(8,128)(2,1)}, bf16[512,1536]{1,0:T(8,128)(2,1)}, u32[]{:S(2)}, u32[]{:S(2)}) collective-permute-start(bf16[512,1536]{1,0:T(8,128)(2,1)} %bitcast.28), channel_id=1, source_target_pairs={{0,6},{1,7},{2,4},{3,5},{4,2},{5,3},{6,0},{7,1},{8,14},{9,15},{10,... | collective-permute-start | bytes 4718600 | tf_op jit(solution)/shard_map/ppermute | solution.py:326
  4.5 2.4 %collective-permute-start.1 = (bf16[512,768]{1,0:T(8,128)(2,1)}, bf16[512,768]{1,0:T(8,128)(2,1)}, u32[]{:S(2)}, u32[]{:S(2)}) collective-permute-start(bf16[512,768]{1,0:T(8,128)(2,1)} %bitcast.32), channel_id=1, source_target_pairs={{0,64},{64,0},{1,65},{65,1},{2,66},{66,2},{3,67},{67,3},{4,68},{68... | collective-permute-start | bytes 2359304 | tf_op jit(solution)/shard_map/ppermute | solution.py:218
  6.9 2.1 %collective-permute-start = (bf16[512,768]{1,0:T(8,128)(2,1)}, bf16[512,768]{1,0:T(8,128)(2,1)}, u32[]{:S(2)}, u32[]{:S(2)}) collective-permute-start(bf16[512,768]{1,0:T(8,128)(2,1)} %bitcast.33), channel_id=1, source_target_pairs={{0,128},{128,0},{1,129},{129,1},{2,130},{130,2},{3,131},{131,3},{4... | collective-permute-start | bytes 2359304 | tf_op jit(solution)/shard_map/ppermute | solution.py:218
  9.0 1.3 concatenate.3.place_ref
  10.3 17.4 %shard_map.94 = (bf16[3,512,256]{2,1,0:T(8,128)(2,1)}, bf16[3,512,512]{2,1,0:T(8,128)(2,1)}) custom-call(s32[12]{0:T(128)} %concatenate.3.place_ref, bf16[512,768]{1,0:T(8,128)(2,1)} %bitcast.34, bf16[512,768]{1,0:T(8,128)(2,1)} %collective-permute-done.1.oth_ref, bf16[3,1536,768]{2,1,0:T(8,128)(2,1)} %w_ref.5), custom_call_target="tpu_custom_call" | custom-call | flops 100000000 | bytes 1000000 | tf_op jit(solution)/shard_map/pallas_call | solution.py:197
  27.6 0.5 collective-permute-done.own_ref
  28.1 0.1 collective-permute-start.4
  28.2 3.5 %collective-permute-start.9 = (bf16[512,1536]{1,0:T(8,128)(2,1)S(1)}, bf16[512,1536]{1,0:T(8,128)(2,1)}, u32[]{:S(2)}, u32[]{:S(2)}) collective-permute-start(bf16[512,1536]{1,0:T(8,128)(2,1)S(1)} %bitcast.29), channel_id=1, source_target_pairs={{0,4},{1,5},{2,6},{3,7},{4,0},{5,1},{6,2},{7,3},{8,12},{9,13},{10,... | collective-permute-start | bytes 4718600 | tf_op jit(solution)/shard_map/ppermute | solution.py:326
  31.7 14.9 %shard_map.95 = (bf16[512,768]{1,0:T(8,128)(2,1)}, bf16[192,512]{1,0:T(8,128)(2,1)}, bf16[192,512]{1,0:T(8,128)(2,1)}, bf16[192,512]{1,0:T(8,128)(2,1)}, bf16[192,512]{1,0:T(8,128)(2,1)}) custom-call(s32[12]{0:T(128)} %concatenate.3.place_ref, bf16[512,768]{1,0:T(8,128)(2,1)} %collective-permute-done.own_ref, ...), custom_call_target="tpu_custom_call" | custom-call | flops 1000000000 | bytes 1000000 | tf_op jit(solution)/shard_map/pallas_call | solution.py:197
  46.7 0.2 reduce-window.9
  46.9 2.3 %collective-permute-start.5 = (bf16[192,512]{1,0:T(8,128)(2,1)}, bf16[192,512]{1,0:T(8,128)(2,1)S(1)}, u32[]{:S(2)}, u32[]{:S(2)}) collective-permute-start(bf16[192,512]{1,0:T(8,128)(2,1)} %get-tuple-element.37), channel_id=1, source_target_pairs={{0,4},{1,5},{2,6},{3,7},{4,0},{5,1},{6,2},{7,3},{8,12},{9,13},{10,... | collective-permute-start | bytes 589832 | tf_op jit(solution)/shard_map/ppermute | solution.py:326
  49.2 1.1 collective-permute-start.7
  50.4 4.5 %shard_map.96 = bf16[512,768]{1,0:T(8,128)(2,1)} custom-call(s32[12]{0:T(128)} %concatenate.3.place_ref, bf16[512,768]{1,0:T(8,128)(2,1)} %get-tuple-element.36.attn_ref, bf16[768,1536]{1,0:T(8,128)(2,1)} %w_ref.7), custom_call_target="tpu_custom_call" | custom-call | flops 600000000 | bytes 3000000 | tf_op jit(solution)/shard_map/pallas_call | solution.py:197
  54.9 0.2 fusion.1
  55.3 1.1 collective-permute-done.7.refs_1_
  56.4 1.4 %copy-done.2 = bf16[1,512,1536]{2,1,0:T(8,128)(2,1)S(1)} copy-done((bf16[1,512,1536]{2,1,0:T(8,128)(2,1)S(1)}, bf16[1,512,1536]{2,1,0:T(8,128)(2,1)}, u32[]{:S(2)}) %copy-start.2) | copy-done | bytes 1572888
  57.8 1.4 %copy-done.4 = bf16[512,1536]{1,0:T(8,128)(2,1)S(1)} copy-done((bf16[512,1536]{1,0:T(8,128)(2,1)S(1)}, bf16[512,1536]{1,0:T(8,128)(2,1)}, u32[]{:S(2)}) %copy-start.4) | copy-done | bytes 1572888
  59.2 5.8 %shard_map.98 = (bf16[48,1536]{1,0:T(8,128)(2,1)S(1)}, bf16[48,1536]{1,0:T(8,128)(2,1)S(1)}, bf16[48,1536]{1,0:T(8,128)(2,1)S(1)}, bf16[48,1536]{1,0:T(8,128)(2,1)S(1)}) custom-call(s32[12]{0:T(128)S(1)} %copy-done.8, bf16[192,512]{1,0:T(8,128)(2,1)S(1)} %copy-done.7, bf16[192,512]{1,0:T(8,128)(2,1)S(1)} %collective-permute-done.7.refs_1_, ...), custom_call_target="tpu_custom_call" | custom-call | flops 1200000000 | bytes 8000000 | tf_op jit(solution)/shard_map/pallas_call | solution.py:197
  65.0 3.4 %collective-permute-start.10 = (bf16[48,1536]{1,0:T(8,128)(2,1)S(1)}, bf16[48,1536]{1,0:T(8,128)(2,1)S(1)}, u32[]{:S(2)}, u32[]{:S(2)}) collective-permute-start(bf16[48,1536]{1,0:T(8,128)(2,1)S(1)} %get-tuple-element.51), channel_id=1, source_target_pairs={{0,56},{1,57},{2,58},{3,59},{4,60},{5,61},{6,62},{7,63},{8,16},{9,... | collective-permute-start | bytes 442376 | tf_op jit(solution)/shard_map/ppermute | solution.py:326
  68.5 2.5 %collective-permute-start.12 = (bf16[48,1536]{1,0:T(8,128)(2,1)S(1)}, bf16[48,1536]{1,0:T(8,128)(2,1)S(1)}, u32[]{:S(2)}, u32[]{:S(2)}) collective-permute-start(bf16[48,1536]{1,0:T(8,128)(2,1)S(1)} %get-tuple-element.53), channel_id=1, source_target_pairs={{0,16},{1,17},{2,18},{3,19},{4,20},{5,21},{6,22},{7,23},{8,56},{9,... | collective-permute-start | bytes 442376 | tf_op jit(solution)/shard_map/ppermute | solution.py:326
  70.9 0.8 collective-permute-done.10
  71.7 1.9 %collective-permute-done.11 = bf16[48,1536]{1,0:T(8,128)(2,1)S(1)} collective-permute-done((bf16[48,1536]{1,0:T(8,128)(2,1)S(1)}, bf16[48,1536]{1,0:T(8,128)(2,1)S(1)}, u32[]{:S(2)}, u32[]{:S(2)}) %collective-permute-start.11) | collective-permute-done | bytes 147488 | tf_op jit(solution)/shard_map/ppermute | solution.py:326
  73.6 2.1 %collective-permute-done.12 = bf16[48,1536]{1,0:T(8,128)(2,1)S(1)} collective-permute-done((bf16[48,1536]{1,0:T(8,128)(2,1)S(1)}, bf16[48,1536]{1,0:T(8,128)(2,1)S(1)}, u32[]{:S(2)}, u32[]{:S(2)}) %collective-permute-start.12) | collective-permute-done | bytes 147488 | tf_op jit(solution)/shard_map/ppermute | solution.py:326
  75.8 2.2 %collective-permute-start.15 = (bf16[48,1536]{1,0:T(8,128)(2,1)S(1)}, bf16[48,1536]{1,0:T(8,128)(2,1)S(1)}, u32[]{:S(2)}, u32[]{:S(2)}) collective-permute-start(bf16[48,1536]{1,0:T(8,128)(2,1)S(1)} %add_convert_fusion.2), channel_id=1, source_target_pairs={{0,128},{1,129},{2,130},{3,131},{4,132},{5,133},{6,134},{7,135},{8... | collective-permute-start | bytes 442376 | tf_op jit(solution)/shard_map/ppermute | solution.py:326
  78.0 2.6 %collective-permute-start.13 = (bf16[48,1536]{1,0:T(8,128)(2,1)S(1)}, bf16[48,1536]{1,0:T(8,128)(2,1)}, u32[]{:S(2)}, u32[]{:S(2)}) collective-permute-start(bf16[48,1536]{1,0:T(8,128)(2,1)S(1)} %add_convert_fusion.2), channel_id=1, source_target_pairs={{0,1},{1,0},{2,3},{3,2},{4,5},{5,4},{6,7},{7,6},{8,9},{9,8},{10,11... | collective-permute-start | bytes 442376 | tf_op jit(solution)/shard_map/ppermute | solution.py:326
  80.6 1.0 copy.16
  81.6 1.0 copy-done.6
  82.7 5.2 %shard_map.97 = (bf16[512,768]{1,0:T(8,128)(2,1)}, bf16[512,768]{1,0:T(8,128)(2,1)S(1)}, bf16[512,768]{1,0:T(8,128)(2,1)S(1)}) custom-call(s32[12]{0:T(128)S(1)} %copy-done.8, bf16[512,768]{1,0:T(8,128)(2,1)S(1)} %copy-done.5, bf16[768,1536]{1,0:T(8,128)(2,1)S(1)} %copy-done, bf16[512,768]{1,0:T(8,128)(2,1)} %collective-permute-done.6.recv_ref, ...), custom_call_target="tpu_custom_call" | custom-call | flops 1400000000 | bytes 6000000 | tf_op jit(solution)/shard_map/pallas_call | solution.py:197
  87.8 1.1 add_convert_fusion.1
  88.9 3.6 %collective-permute-start.17 = (bf16[48,1536]{1,0:T(8,128)(2,1)S(1)}, bf16[48,1536]{1,0:T(8,128)(2,1)S(1)}, u32[]{:S(2)}, u32[]{:S(2)}) collective-permute-start(bf16[48,1536]{1,0:T(8,128)(2,1)S(1)} %add_convert_fusion.1), channel_id=1, source_target_pairs={{0,32},{1,33},{2,34},{3,35},{4,36},{5,37},{6,38},{7,39},{8,40},{9,... | collective-permute-start | bytes 442376 | tf_op jit(solution)/shard_map/ppermute | solution.py:326
  92.5 0.9 collective-permute-start.16
  93.4 5.0 %collective-permute-done.17 = bf16[48,1536]{1,0:T(8,128)(2,1)S(1)} collective-permute-done((bf16[48,1536]{1,0:T(8,128)(2,1)S(1)}, bf16[48,1536]{1,0:T(8,128)(2,1)S(1)}, u32[]{:S(2)}, u32[]{:S(2)}) %collective-permute-start.17) | collective-permute-done | bytes 147488 | tf_op jit(solution)/shard_map/ppermute | solution.py:326
  98.5 2.9 %collective-permute-start.20 = (bf16[48,1536]{1,0:T(8,128)(2,1)S(1)}, bf16[48,1536]{1,0:T(8,128)(2,1)S(1)}, u32[]{:S(2)}, u32[]{:S(2)}) collective-permute-start(bf16[48,1536]{1,0:T(8,128)(2,1)S(1)} %add_convert_fusion), channel_id=1, source_target_pairs={{0,16},{1,17},{2,18},{3,19},{4,20},{5,21},{6,22},{7,23},{8,56},{9,... | collective-permute-start | bytes 442376 | tf_op jit(solution)/shard_map/ppermute | solution.py:326
  101.4 1.4 %collective-permute-start.19 = (bf16[48,1536]{1,0:T(8,128)(2,1)S(1)}, bf16[48,1536]{1,0:T(8,128)(2,1)S(1)}, u32[]{:S(2)}, u32[]{:S(2)}) collective-permute-start(bf16[48,1536]{1,0:T(8,128)(2,1)S(1)} %add_convert_fusion), channel_id=1, source_target_pairs={{0,8},{1,9},{2,10},{3,11},{4,12},{5,13},{6,14},{7,15},{8,0},{9,1},... | collective-permute-start | bytes 442376 | tf_op jit(solution)/shard_map/ppermute | solution.py:326
  102.8 0.5 collective-permute-start.18
  103.2 2.6 %collective-permute-done.20 = bf16[48,1536]{1,0:T(8,128)(2,1)S(1)} collective-permute-done((bf16[48,1536]{1,0:T(8,128)(2,1)S(1)}, bf16[48,1536]{1,0:T(8,128)(2,1)S(1)}, u32[]{:S(2)}, u32[]{:S(2)}) %collective-permute-start.20) | collective-permute-done | bytes 147488 | tf_op jit(solution)/shard_map/ppermute | solution.py:326
  105.8 1.7 %collective-permute-done.19 = bf16[48,1536]{1,0:T(8,128)(2,1)S(1)} collective-permute-done((bf16[48,1536]{1,0:T(8,128)(2,1)S(1)}, bf16[48,1536]{1,0:T(8,128)(2,1)S(1)}, u32[]{:S(2)}, u32[]{:S(2)}) %collective-permute-start.19) | collective-permute-done | bytes 147488 | tf_op jit(solution)/shard_map/ppermute | solution.py:326
  107.5 3.1 %collective-permute-done.18 = bf16[48,1536]{1,0:T(8,128)(2,1)S(1)} collective-permute-done((bf16[48,1536]{1,0:T(8,128)(2,1)S(1)}, bf16[48,1536]{1,0:T(8,128)(2,1)S(1)}, u32[]{:S(2)}, u32[]{:S(2)}) %collective-permute-start.18) | collective-permute-done | bytes 147488 | tf_op jit(solution)/shard_map/ppermute | solution.py:326
  110.8 2.7 %collective-permute-start.22 = (bf16[4,48,1536]{2,1,0:T(8,128)(2,1)S(1)}, bf16[4,48,1536]{2,1,0:T(8,128)(2,1)S(1)}, u32[]{:S(2)}, u32[]{:S(2)}) collective-permute-start(bf16[4,48,1536]{2,1,0:T(8,128)(2,1)S(1)} %pad_maximum_fusion.part_ref), channel_id=1, source_target_pairs={{0,2},{1,3},{2,0},{3,1},{4,6},{5,7},{6,4},{7,5},{8,10},{9,11},{10,... | collective-permute-start | bytes 1769480 | tf_op jit(solution)/shard_map/ppermute | solution.py:326
  113.5 1.9 %collective-permute-start.21 = (bf16[4,48,1536]{2,1,0:T(8,128)(2,1)S(1)}, bf16[4,48,1536]{2,1,0:T(8,128)(2,1)S(1)}, u32[]{:S(2)}, u32[]{:S(2)}) collective-permute-start(bf16[4,48,1536]{2,1,0:T(8,128)(2,1)S(1)} %pad_maximum_fusion.part_ref), channel_id=1, source_target_pairs={{0,4},{1,5},{2,6},{3,7},{4,0},{5,1},{6,2},{7,3},{8,12},{9,13},{10,... | collective-permute-start | bytes 1769480 | tf_op jit(solution)/shard_map/ppermute | solution.py:326
  115.5 1.6 %shard_map.99.refs_0_ = f32[768,1536]{1,0:T(8,128)} custom-call(s32[12]{0:T(128)S(1)} %copy-done.8, bf16[4,48,1536]{2,1,0:T(8,128)(2,1)S(1)} %pad_maximum_fusion.part_ref), custom_call_target="tpu_custom_call" | custom-call | flops 1000000 | bytes 2000000 | tf_op jit(solution)/shard_map/pallas_call | solution.py:197
  117.1 1.0 add_bitcast_fusion
  118.0 3.8 %collective-permute-done.23.part_ref = bf16[4,48,1536]{2,1,0:T(8,128)(2,1)S(1)} collective-permute-done((bf16[4,48,1536]{2,1,0:T(8,128)(2,1)S(1)}, bf16[4,48,1536]{2,1,0:T(8,128)(2,1)S(1)}, u32[]{:S(2)}, u32[]{:S(2)}) %collective-permute-start.23) | collective-permute-done | bytes 589856 | tf_op jit(solution)/shard_map/ppermute | solution.py:326
  121.8 1.6 %shard_map.100.refs_0_ = f32[768,1536]{1,0:T(8,128)} custom-call(s32[12]{0:T(128)S(1)} %copy-done.8, bf16[4,48,1536]{2,1,0:T(8,128)(2,1)S(1)} %collective-permute-done.23.part_ref, f32[768,1536]{1,0:T(8,128)} %shard_map.99.refs_0_), custom_call_target="tpu_custom_call", output_to_operand_aliasing={{}: (2, {})} | custom-call | flops 1000000 | bytes 2000000 | tf_op jit(solution)/shard_map/pallas_call | solution.py:197
  123.5 1.6 %shard_map.101.refs_0_ = f32[768,1536]{1,0:T(8,128)} custom-call(s32[12]{0:T(128)S(1)} %copy-done.8, bf16[4,48,1536]{2,1,0:T(8,128)(2,1)S(1)} %collective-permute-done.22.part_ref, f32[768,1536]{1,0:T(8,128)} %shard_map.100.refs_0_), custom_call_target="tpu_custom_call", output_to_operand_aliasing={{}: (2, {})} | custom-call | flops 1000000 | bytes 2000000 | tf_op jit(solution)/shard_map/pallas_call | solution.py:197
  125.1 4.5 %collective-permute-done.21.part_ref = bf16[4,48,1536]{2,1,0:T(8,128)(2,1)S(1)} collective-permute-done((bf16[4,48,1536]{2,1,0:T(8,128)(2,1)S(1)}, bf16[4,48,1536]{2,1,0:T(8,128)(2,1)S(1)}, u32[]{:S(2)}, u32[]{:S(2)}) %collective-permute-start.21) | collective-permute-done | bytes 589856 | tf_op jit(solution)/shard_map/ppermute | solution.py:326
  129.6 1.6 %shard_map.102 = f32[768,1536]{1,0:T(8,128)} custom-call(s32[12]{0:T(128)S(1)} %copy-done.8, bf16[4,48,1536]{2,1,0:T(8,128)(2,1)S(1)} %collective-permute-done.21.part_ref, f32[768,1536]{1,0:T(8,128)} %shard_map.101.refs_0_), custom_call_target="tpu_custom_call", output_to_operand_aliasing={{}: (2, {})} | custom-call | flops 1000000 | bytes 2000000 | tf_op jit(solution)/shard_map/pallas_call | solution.py:197
  (50 shorter events, 0.6 us)
Async XLA Ops:
  0.6 27.5 %collective-permute-start.3 = (bf16[512,1536]{1,0:T(8,128)(2,1)}, bf16[512,1536]{1,0:T(8,128)(2,1)S(1)}, u32[]{:S(2)}, u32[]{:S(2)}) collective-permute-start(bf16[512,1536]{1,0:T(8,128)(2,1)} %bitcast.27), channel_id=1, source_target_pairs={{0,2},{1,3},{2,0},{3,1},{4,6},{5,7},{6,4},{7,5},{8,10},{9,11},{10,... | collective-permute-start | bytes 4718600 | tf_op jit(solution)/shard_map/ppermute | solution.py:326
  2.3 25.8 %collective-permute-start.2 = (bf16[512,1536]{1,0:T(8,128)(2,1)}, bf16[512,1536]{1,0:T(8,128)(2,1)}, u32[]{:S(2)}, u32[]{:S(2)}) collective-permute-start(bf16[512,1536]{1,0:T(8,128)(2,1)} %bitcast.28), channel_id=1, source_target_pairs={{0,6},{1,7},{2,4},{3,5},{4,2},{5,3},{6,0},{7,1},{8,14},{9,15},{10,... | collective-permute-start | bytes 4718600 | tf_op jit(solution)/shard_map/ppermute | solution.py:326
  4.5 5.8 %collective-permute-start.1 = (bf16[512,768]{1,0:T(8,128)(2,1)}, bf16[512,768]{1,0:T(8,128)(2,1)}, u32[]{:S(2)}, u32[]{:S(2)}) collective-permute-start(bf16[512,768]{1,0:T(8,128)(2,1)} %bitcast.32), channel_id=1, source_target_pairs={{0,64},{64,0},{1,65},{65,1},{2,66},{66,2},{3,67},{67,3},{4,68},{68... | collective-permute-start | bytes 2359304 | tf_op jit(solution)/shard_map/ppermute | solution.py:218
  6.9 21.3 %collective-permute-start = (bf16[512,768]{1,0:T(8,128)(2,1)}, bf16[512,768]{1,0:T(8,128)(2,1)}, u32[]{:S(2)}, u32[]{:S(2)}) collective-permute-start(bf16[512,768]{1,0:T(8,128)(2,1)} %bitcast.33), channel_id=1, source_target_pairs={{0,128},{128,0},{1,129},{129,1},{2,130},{130,2},{3,131},{131,3},{4... | collective-permute-start | bytes 2359304 | tf_op jit(solution)/shard_map/ppermute | solution.py:218
  10.3 18.0 %copy-start.1 = (bf16[1,512,1536]{2,1,0:T(8,128)(2,1)S(1)}, bf16[1,512,1536]{2,1,0:T(8,128)(2,1)}, u32[]{:S(2)}) copy-start(bf16[1,512,1536]{2,1,0:T(8,128)(2,1)} %param.11) | copy-start | bytes 4718596
  28.1 18.5 %copy-start.3 = (bf16[512,1536]{1,0:T(8,128)(2,1)}, bf16[512,1536]{1,0:T(8,128)(2,1)S(1)}, u32[]{:S(2)}) copy-start(bf16[512,1536]{1,0:T(8,128)(2,1)S(1)} %collective-permute-done.3.refs_6_) | copy-start | bytes 4718596
  28.1 3.6 %collective-permute-start.4 = (bf16[512,768]{1,0:T(8,128)(2,1)}, bf16[512,768]{1,0:T(8,128)(2,1)}, u32[]{:S(2)}, u32[]{:S(2)}) collective-permute-start(bf16[512,768]{1,0:T(8,128)(2,1)} %collective-permute-done.own_ref), channel_id=1, source_target_pairs={{0,64},{64,0},{1,65},{65,1},{2,66},{66,2},{3,67},{67,3},{4,68},{68... | collective-permute-start | bytes 2359304 | tf_op jit(solution)/shard_map/ppermute | solution.py:218
  28.2 27.0 %collective-permute-start.9 = (bf16[512,1536]{1,0:T(8,128)(2,1)S(1)}, bf16[512,1536]{1,0:T(8,128)(2,1)}, u32[]{:S(2)}, u32[]{:S(2)}) collective-permute-start(bf16[512,1536]{1,0:T(8,128)(2,1)S(1)} %bitcast.29), channel_id=1, source_target_pairs={{0,4},{1,5},{2,6},{3,7},{4,0},{5,1},{6,2},{7,3},{8,12},{9,13},{10,... | collective-permute-start | bytes 4718600 | tf_op jit(solution)/shard_map/ppermute | solution.py:326
  31.7 15.0 %copy-start.10 = (s32[1,8]{1,0:T(1,128)S(1)}, s32[1,8]{1,0:T(1,128)}, u32[]{:S(2)}) copy-start(s32[1,8]{1,0:T(1,128)} %param.8) | copy-start | bytes 100
  46.7 8.2 %copy-start.11 = (s32[1,8]{1,0:T(1,128)S(1)}, s32[1,8]{1,0:T(1,128)}, u32[]{:S(2)}) copy-start(s32[1,8]{1,0:T(1,128)} %param.9) | copy-start | bytes 100
  46.7 8.3 %copy-start.9 = (s32[1,8,128]{2,1,0:T(8,128)S(1)}, s32[1,8,128]{2,1,0:T(8,128)}, u32[]{:S(2)}) copy-start(s32[1,8,128]{2,1,0:T(8,128)} %param.10) | copy-start | bytes 12292
  46.7 9.7 %copy-start.7 = (bf16[192,512]{1,0:T(8,128)(2,1)S(1)}, bf16[192,512]{1,0:T(8,128)(2,1)}, u32[]{:S(2)}) copy-start(bf16[192,512]{1,0:T(8,128)(2,1)} %get-tuple-element.44.refs_0_) | copy-start | bytes 589828
  46.7 9.7 %copy-start.8 = (s32[12]{0:T(128)S(1)}, s32[12]{0:T(128)}, u32[]{:S(2)}) copy-start(s32[12]{0:T(128)} %concatenate.3.place_ref) | copy-start | bytes 148
  46.9 8.3 %collective-permute-start.5 = (bf16[192,512]{1,0:T(8,128)(2,1)}, bf16[192,512]{1,0:T(8,128)(2,1)S(1)}, u32[]{:S(2)}, u32[]{:S(2)}) collective-permute-start(bf16[192,512]{1,0:T(8,128)(2,1)} %get-tuple-element.37), channel_id=1, source_target_pairs={{0,4},{1,5},{2,6},{3,7},{4,0},{5,1},{6,2},{7,3},{8,12},{9,13},{10,... | collective-permute-start | bytes 589832 | tf_op jit(solution)/shard_map/ppermute | solution.py:326
  49.2 7.1 %collective-permute-start.7 = (bf16[192,512]{1,0:T(8,128)(2,1)}, bf16[192,512]{1,0:T(8,128)(2,1)S(1)}, u32[]{:S(2)}, u32[]{:S(2)}) collective-permute-start(bf16[192,512]{1,0:T(8,128)(2,1)} %get-tuple-element.45), channel_id=1, source_target_pairs={{0,6},{1,7},{2,4},{3,5},{4,2},{5,3},{6,0},{7,1},{8,14},{9,15},{10,... | collective-permute-start | bytes 589832 | tf_op jit(solution)/shard_map/ppermute | solution.py:326
  50.3 6.1 %collective-permute-start.8 = (bf16[192,512]{1,0:T(8,128)(2,1)}, bf16[192,512]{1,0:T(8,128)(2,1)S(1)}, u32[]{:S(2)}, u32[]{:S(2)}) collective-permute-start(bf16[192,512]{1,0:T(8,128)(2,1)} %get-tuple-element.46), channel_id=1, source_target_pairs={{0,2},{1,3},{2,0},{3,1},{4,6},{5,7},{6,4},{7,5},{8,10},{9,11},{10,... | collective-permute-start | bytes 589832 | tf_op jit(solution)/shard_map/ppermute | solution.py:326
  56.4 1.4 %copy-start.2 = (bf16[1,512,1536]{2,1,0:T(8,128)(2,1)S(1)}, bf16[1,512,1536]{2,1,0:T(8,128)(2,1)}, u32[]{:S(2)}) copy-start(bf16[1,512,1536]{2,1,0:T(8,128)(2,1)} %param.11) | copy-start | bytes 4718596
  57.8 1.4 %copy-start.4 = (bf16[512,1536]{1,0:T(8,128)(2,1)S(1)}, bf16[512,1536]{1,0:T(8,128)(2,1)}, u32[]{:S(2)}) copy-start(bf16[512,1536]{1,0:T(8,128)(2,1)} %copy-done.3) | copy-start | bytes 4718596
  59.2 22.4 %copy-start = (bf16[768,1536]{1,0:T(8,128)(2,1)S(1)}, bf16[768,1536]{1,0:T(8,128)(2,1)}, u32[]{:S(2)}) copy-start(bf16[768,1536]{1,0:T(8,128)(2,1)} %w_ref.7) | copy-start | bytes 7077892
  59.2 22.4 %copy-start.5 = (bf16[512,768]{1,0:T(8,128)(2,1)S(1)}, bf16[512,768]{1,0:T(8,128)(2,1)}, u32[]{:S(2)}) copy-start(bf16[512,768]{1,0:T(8,128)(2,1)} %get-tuple-element.36.attn_ref) | copy-start | bytes 2359300
  65.0 6.7 %collective-permute-start.10 = (bf16[48,1536]{1,0:T(8,128)(2,1)S(1)}, bf16[48,1536]{1,0:T(8,128)(2,1)S(1)}, u32[]{:S(2)}, u32[]{:S(2)}) collective-permute-start(bf16[48,1536]{1,0:T(8,128)(2,1)S(1)} %get-tuple-element.51), channel_id=1, source_target_pairs={{0,56},{1,57},{2,58},{3,59},{4,60},{5,61},{6,62},{7,63},{8,16},{9,... | collective-permute-start | bytes 442376 | tf_op jit(solution)/shard_map/ppermute | solution.py:326
  68.5 5.1 %collective-permute-start.11 = (bf16[48,1536]{1,0:T(8,128)(2,1)S(1)}, bf16[48,1536]{1,0:T(8,128)(2,1)S(1)}, u32[]{:S(2)}, u32[]{:S(2)}) collective-permute-start(bf16[48,1536]{1,0:T(8,128)(2,1)S(1)} %get-tuple-element.52), channel_id=1, source_target_pairs={{0,8},{1,9},{2,10},{3,11},{4,12},{5,13},{6,14},{7,15},{8,0},{9,1},... | collective-permute-start | bytes 442376 | tf_op jit(solution)/shard_map/ppermute | solution.py:326
  68.5 7.3 %collective-permute-start.12 = (bf16[48,1536]{1,0:T(8,128)(2,1)S(1)}, bf16[48,1536]{1,0:T(8,128)(2,1)S(1)}, u32[]{:S(2)}, u32[]{:S(2)}) collective-permute-start(bf16[48,1536]{1,0:T(8,128)(2,1)S(1)} %get-tuple-element.53), channel_id=1, source_target_pairs={{0,16},{1,17},{2,18},{3,19},{4,20},{5,21},{6,22},{7,23},{8,56},{9,... | collective-permute-start | bytes 442376 | tf_op jit(solution)/shard_map/ppermute | solution.py:326
  70.9 10.7 %collective-permute-start.6 = (bf16[512,768]{1,0:T(8,128)(2,1)}, bf16[512,768]{1,0:T(8,128)(2,1)}, u32[]{:S(2)}, u32[]{:S(2)}) collective-permute-start(bf16[512,768]{1,0:T(8,128)(2,1)} %shard_map.96), channel_id=1, source_target_pairs={{0,64},{64,0},{1,65},{65,1},{2,66},{66,2},{3,67},{67,3},{4,68},{68... | collective-permute-start | bytes 2359304 | tf_op jit(solution)/shard_map/ppermute | solution.py:218
  75.8 12.0 %collective-permute-start.15 = (bf16[48,1536]{1,0:T(8,128)(2,1)S(1)}, bf16[48,1536]{1,0:T(8,128)(2,1)S(1)}, u32[]{:S(2)}, u32[]{:S(2)}) collective-permute-start(bf16[48,1536]{1,0:T(8,128)(2,1)S(1)} %add_convert_fusion.2), channel_id=1, source_target_pairs={{0,128},{1,129},{2,130},{3,131},{4,132},{5,133},{6,134},{7,135},{8... | collective-permute-start | bytes 442376 | tf_op jit(solution)/shard_map/ppermute | solution.py:326
  78.0 9.8 %collective-permute-start.14 = (bf16[48,1536]{1,0:T(8,128)(2,1)S(1)}, bf16[48,1536]{1,0:T(8,128)(2,1)}, u32[]{:S(2)}, u32[]{:S(2)}) collective-permute-start(bf16[48,1536]{1,0:T(8,128)(2,1)S(1)} %add_convert_fusion.2), channel_id=1, source_target_pairs={{0,129},{1,128},{2,131},{3,130},{4,133},{5,132},{6,135},{7,134},{8... | collective-permute-start | bytes 442376 | tf_op jit(solution)/shard_map/ppermute | solution.py:326
  78.0 9.8 %collective-permute-start.13 = (bf16[48,1536]{1,0:T(8,128)(2,1)S(1)}, bf16[48,1536]{1,0:T(8,128)(2,1)}, u32[]{:S(2)}, u32[]{:S(2)}) collective-permute-start(bf16[48,1536]{1,0:T(8,128)(2,1)S(1)} %add_convert_fusion.2), channel_id=1, source_target_pairs={{0,1},{1,0},{2,3},{3,2},{4,5},{5,4},{6,7},{7,6},{8,9},{9,8},{10,11... | collective-permute-start | bytes 442376 | tf_op jit(solution)/shard_map/ppermute | solution.py:326
  81.6 1.0 copy-start.6
  88.9 9.5 %collective-permute-start.17 = (bf16[48,1536]{1,0:T(8,128)(2,1)S(1)}, bf16[48,1536]{1,0:T(8,128)(2,1)S(1)}, u32[]{:S(2)}, u32[]{:S(2)}) collective-permute-start(bf16[48,1536]{1,0:T(8,128)(2,1)S(1)} %add_convert_fusion.1), channel_id=1, source_target_pairs={{0,32},{1,33},{2,34},{3,35},{4,36},{5,37},{6,38},{7,39},{8,40},{9,... | collective-permute-start | bytes 442376 | tf_op jit(solution)/shard_map/ppermute | solution.py:326
  92.5 24.6 %collective-permute-start.16 = (bf16[512,768]{1,0:T(8,128)(2,1)S(1)}, bf16[512,768]{1,0:T(8,128)(2,1)S(1)}, u32[]{:S(2)}, u32[]{:S(2)}) collective-permute-start(bf16[512,768]{1,0:T(8,128)(2,1)S(1)} %get-tuple-element.57), channel_id=1, source_target_pairs={{0,128},{128,0},{1,129},{129,1},{2,130},{130,2},{3,131},{131,3},{4... | collective-permute-start | bytes 2359304 | tf_op jit(solution)/shard_map/ppermute | solution.py:218
  98.5 7.3 %collective-permute-start.20 = (bf16[48,1536]{1,0:T(8,128)(2,1)S(1)}, bf16[48,1536]{1,0:T(8,128)(2,1)S(1)}, u32[]{:S(2)}, u32[]{:S(2)}) collective-permute-start(bf16[48,1536]{1,0:T(8,128)(2,1)S(1)} %add_convert_fusion), channel_id=1, source_target_pairs={{0,16},{1,17},{2,18},{3,19},{4,20},{5,21},{6,22},{7,23},{8,56},{9,... | collective-permute-start | bytes 442376 | tf_op jit(solution)/shard_map/ppermute | solution.py:326
  101.4 6.1 %collective-permute-start.19 = (bf16[48,1536]{1,0:T(8,128)(2,1)S(1)}, bf16[48,1536]{1,0:T(8,128)(2,1)S(1)}, u32[]{:S(2)}, u32[]{:S(2)}) collective-permute-start(bf16[48,1536]{1,0:T(8,128)(2,1)S(1)} %add_convert_fusion), channel_id=1, source_target_pairs={{0,8},{1,9},{2,10},{3,11},{4,12},{5,13},{6,14},{7,15},{8,0},{9,1},... | collective-permute-start | bytes 442376 | tf_op jit(solution)/shard_map/ppermute | solution.py:326
  102.8 7.8 %collective-permute-start.18 = (bf16[48,1536]{1,0:T(8,128)(2,1)S(1)}, bf16[48,1536]{1,0:T(8,128)(2,1)S(1)}, u32[]{:S(2)}, u32[]{:S(2)}) collective-permute-start(bf16[48,1536]{1,0:T(8,128)(2,1)S(1)} %add_convert_fusion), channel_id=1, source_target_pairs={{0,56},{1,57},{2,58},{3,59},{4,60},{5,61},{6,62},{7,63},{8,16},{9,... | collective-permute-start | bytes 442376 | tf_op jit(solution)/shard_map/ppermute | solution.py:326
  110.7 11.2 %collective-permute-start.23 = (bf16[4,48,1536]{2,1,0:T(8,128)(2,1)S(1)}, bf16[4,48,1536]{2,1,0:T(8,128)(2,1)S(1)}, u32[]{:S(2)}, u32[]{:S(2)}) collective-permute-start(bf16[4,48,1536]{2,1,0:T(8,128)(2,1)S(1)} %pad_maximum_fusion.part_ref), channel_id=1, source_target_pairs={{0,6},{1,7},{2,4},{3,5},{4,2},{5,3},{6,0},{7,1},{8,14},{9,15},{10,... | collective-permute-start | bytes 1769480 | tf_op jit(solution)/shard_map/ppermute | solution.py:326
  110.8 12.7 %collective-permute-start.22 = (bf16[4,48,1536]{2,1,0:T(8,128)(2,1)S(1)}, bf16[4,48,1536]{2,1,0:T(8,128)(2,1)S(1)}, u32[]{:S(2)}, u32[]{:S(2)}) collective-permute-start(bf16[4,48,1536]{2,1,0:T(8,128)(2,1)S(1)} %pad_maximum_fusion.part_ref), channel_id=1, source_target_pairs={{0,2},{1,3},{2,0},{3,1},{4,6},{5,7},{6,4},{7,5},{8,10},{9,11},{10,... | collective-permute-start | bytes 1769480 | tf_op jit(solution)/shard_map/ppermute | solution.py:326
  113.5 16.1 %collective-permute-start.21 = (bf16[4,48,1536]{2,1,0:T(8,128)(2,1)S(1)}, bf16[4,48,1536]{2,1,0:T(8,128)(2,1)S(1)}, u32[]{:S(2)}, u32[]{:S(2)}) collective-permute-start(bf16[4,48,1536]{2,1,0:T(8,128)(2,1)S(1)} %pad_maximum_fusion.part_ref), channel_id=1, source_target_pairs={{0,4},{1,5},{2,6},{3,7},{4,0},{5,1},{6,2},{7,3},{8,12},{9,13},{10,... | collective-permute-start | bytes 1769480 | tf_op jit(solution)/shard_map/ppermute | solution.py:326
